TPU v7x, 512 devices: a whole 4x4x16 slice. The times are simulated.
512 devices in a mesh: ctx: 64 (over z, x), tp: 8 (over y, core).
Axes of the slice: x: 4, y: 4, z: 16, core: 2. Of those that a mesh axis runs over, the one named last changes fastest.
Arguments:
- queries: bfloat16 [8192, 8192], P('ctx', 'tp'), may hold values from -1.75 to 1.75
- key_rows: bfloat16 [8192, 8192], P('ctx', 'tp'), may hold values from -1.8 to 1.8
- value_rows: bfloat16 [8192, 8192], P('ctx', 'tp'), may hold values from -6 to 6
- log_decay: float32 [8192, 64], P('ctx', 'tp'), may hold values from -1 to 0
- norm_gain: float32 [8192], P('tp'), may hold values from 0.5 to 1.5
- grad_output: bfloat16 [8192, 8192], P('ctx', 'tp'), may hold values from -6 to 6
Outputs:
- normed: bfloat16 [8192, 8192], P('ctx', 'tp')
- grad_queries: bfloat16 [8192, 8192], P('ctx', 'tp')
- grad_keys: bfloat16 [8192, 8192], P('ctx', 'tp')
- grad_values: bfloat16 [8192, 8192], P('ctx', 'tp')
All inputs are finite; a program needn't handle non-finite values.
Results may differ from a plain program's by a relative error of at most 0.002.
Values sent between devices are 32-bit elements; how exact they have to be, the bound alone decides.
No kernel may reach another device: no remote copies, remote signals or barrier semaphores. Data moves between devices by JAX's collectives and lax.ppermute only.
A program may use at most 192 MiB of HBM per device.

v0:
```python
import jax
import jax.numpy as jnp
from jax import lax
from jax.sharding import PartitionSpec as P

epsilon = 1e-06
highest = lax.Precision.HIGHEST


def carried_in(value, axis, join, neutral, backward):
    count, mine = (lax.axis_size(axis), lax.axis_index(axis))
    pieces = jax.tree.map(lambda part: lax.all_gather(part, axis), value)
    if backward:
        pieces = jax.tree.map(lambda part: part[::-1], pieces)
        mine = count - 1 - mine
    running = jax.tree.map(
        lambda part, zero: jnp.full_like(part, 0) + jnp.asarray(zero, part.dtype), value, neutral
    )

    def lap(position, running):
        longer = join(running, jax.tree.map(lambda part: part[position], pieces))
        return jax.tree.map(lambda new, old: jnp.where(position < mine, new, old), longer, running)

    return lax.fori_loop(0, count - 1, lap, running)


def combine_states(earlier, later):
    return (later[1][:, None, None] * earlier[0] + later[0], earlier[1] * later[1])


def shards(queries, key_rows, value_rows, log_decay, norm_gain, grad_output):
    tok_rows, feat_width = queries.shape
    head_count = log_decay.shape[1]
    head_size = feat_width // head_count
    block_rows = min(128, tok_rows)
    block_count = tok_rows // block_rows
    block_shape = (block_count, block_rows, head_count, head_size)
    query_blocks = queries.reshape(block_shape)
    key_blocks = key_rows.reshape(block_shape)
    query_wide = query_blocks.astype(jnp.float32)
    key_wide = key_blocks.astype(jnp.float32)
    value_wide = value_rows.reshape(block_shape).astype(jnp.float32)
    cumulative = jnp.cumsum(log_decay.reshape(block_count, block_rows, head_count), axis=1)
    totals = cumulative[:, -1, :]
    places = jnp.arange(block_rows)
    lower_mask = places[:, None] >= places[None, :]
    differences = jnp.transpose(cumulative[:, :, None, :] - cumulative[:, None, :, :], (0, 3, 1, 2))
    weights = jnp.where(lower_mask, jnp.exp(jnp.where(lower_mask, differences, 0.0)), 0.0)
    rising = jnp.exp(cumulative)[..., None]
    trailing = jnp.exp(totals[:, None, :] - cumulative)[..., None]
    scores = (
        jnp.einsum("cthd,cshd->chts", query_blocks, key_blocks, preferred_element_type=jnp.float32)
        * weights
    )
    inside = jnp.einsum("chts,cshe->cthe", scores, value_wide, precision=highest)
    block_states = jnp.einsum("cshd,cshe->chde", key_wide * trailing, value_wide, precision=highest)
    empty_state = jnp.zeros((head_count, head_size, head_size), jnp.float32)
    running = empty_state
    member = 0
    before = [running]
    running = jnp.exp(totals[member])[:, None, None] * running + block_states[member]
    gains = jnp.exp(jnp.sum(totals, axis=0))
    identity = (empty_state, jnp.ones((head_count,), jnp.float32))
    incoming, _ = carried_in((running, gains), "ctx", combine_states, identity, False)
    leading = jnp.exp(jnp.cumsum(totals, axis=0) - totals)
    entry_states = jnp.stack(before) + leading[:, :, None, None] * incoming[None]
    outside = jnp.einsum("cthd,chde->cthe", query_wide, entry_states, precision=highest) * rising
    mixed = (inside + outside).reshape(tok_rows, feat_width)
    scaled_grad = grad_output.astype(jnp.float32) * norm_gain
    squares, products = lax.psum(
        (jnp.sum(mixed * mixed, axis=1), jnp.sum(scaled_grad * mixed, axis=1)), "tp"
    )
    full_width = feat_width * lax.axis_size("tp")
    row_scale = lax.rsqrt(squares / full_width + epsilon)[:, None]
    normed = (mixed * row_scale * norm_gain).astype(jnp.bfloat16)
    grad_mixed = row_scale * scaled_grad - row_scale * row_scale * row_scale * mixed * (
        products[:, None] / full_width
    )
    grad_blocks = grad_mixed.reshape(block_shape)
    back_states = jnp.einsum("cthd,cthe->chde", query_wide * rising, grad_blocks, precision=highest)
    after = [empty_state] * block_count
    carried = empty_state
    for member in reversed(range(block_count)):
        after[member] = carried
        carried = jnp.exp(totals[member])[:, None, None] * carried + back_states[member]
    later_states, _ = carried_in((carried, gains), "ctx", combine_states, identity, True)
    remaining = jnp.exp(jnp.sum(totals, axis=0)[None, :] - jnp.cumsum(totals, axis=0))
    exit_states = jnp.stack(after) + remaining[:, :, None, None] * later_states[None]
    grad_scores = (
        jnp.einsum("cthe,cshe->chts", grad_blocks, value_wide, precision=highest) * weights
    )
    grad_q = jnp.einsum("chts,cshd->cthd", grad_scores, key_wide, precision=highest)
    grad_q = (
        grad_q
        + jnp.einsum("cthe,chde->cthd", grad_blocks, entry_states, precision=highest) * rising
    )
    grad_k = jnp.einsum("chts,cthd->cshd", grad_scores, query_wide, precision=highest)
    grad_k = (
        grad_k
        + jnp.einsum("cshe,chde->cshd", value_wide, exit_states, precision=highest) * trailing
    )
    grad_v = jnp.einsum("chts,cthe->cshe", scores, grad_blocks, precision=highest)
    grad_v = (
        grad_v + jnp.einsum("cshd,chde->cshe", key_wide, exit_states, precision=highest) * trailing
    )
    return (
        normed,
        grad_q.reshape(tok_rows, feat_width).astype(jnp.bfloat16),
        grad_k.reshape(tok_rows, feat_width).astype(jnp.bfloat16),
        grad_v.reshape(tok_rows, feat_width).astype(jnp.bfloat16),
    )


def solution(mesh):
    in_specs = (
        P("ctx", "tp"),
        P("ctx", "tp"),
        P("ctx", "tp"),
        P("ctx", "tp"),
        P("tp"),
        P("ctx", "tp"),
    )
    out_specs = (P("ctx", "tp"), P("ctx", "tp"), P("ctx", "tp"), P("ctx", "tp"))
    return jax.shard_map(shards, mesh=mesh, in_specs=in_specs, out_specs=out_specs, check_vma=False)
```

profile of v0, /device:TPU:1, one launch (start us, length us, event | category | flops | bytes accessed | tf_op | source)
XLA Modules:
  0.0 806.8 jit_solution(8398468890401210177)
XLA Ops:
  9.6 1.2 convolution_add_fusion.1
  12.1 72.1 %all-gather = f32[64,1,8]{2,1,0:T(1,128)S(1)} all-gather(f32[1,1,8]{2,1,0:T(1,128)S(1)} %get-tuple-element.269), channel_id=2, replica_groups=mesh['ctx'=64,'tp'=8] {'ctx'}, dimensions={0}, use_global_device_ids=true | all-gather | bytes 2080 | tf_op jit(solution)/shard_map/all_gather | solution.py:12
  84.1 1.3 fusion.3
  85.4 224.9 %all-gather.6.cloned.1.call-done = f32[512,128,128]{2,1,0:T(8,128)} async-done(((f32[8,128,128]{2,1,0:T(8,128)}), f32[512,128,128]{2,1,0:T(8,128)}) %all-gather.6.cloned.1.call-update) | async-done | bytes 33554448 | tf_op jit(solution)/shard_map/all_gather | solution.py:12
  310.3 76.4 %while.28 = (s32[]{:T(128)}, f32[8,128,128]{2,1,0:T(8,128)S(1)}, s32[]{:T(128)}, f32[64,8]{1,0:T(8,128)S(1)}, f32[64,8,128,128]{3,2,1,0:T(8,128)}, /*index=5*/s32[]{:T(128)}, s32[]{:T(128)}) while((s32[]{:T(128)}, f32[8,128,128]{2,1,0:T(8,128)S(1)}, s32[]{:T(128)}, f32[64,8]{1,0:T(8,128)S(1)}, f32[64,8,128,128]{3,2,1,0:T(8,128)}, ...), condition=%wide.region_2.3_spmd.clone, body=%wide.region_1.2_spmd.clone.sunk | while | flops 524292 | bytes 1573065 | solution.py:24
  389.5 12.8 %all-reduce = (f32[128]{0:T(128)S(1)}, f32[128]{0:T(128)S(1)}) all-reduce(f32[128]{0:T(128)S(1)} %get-tuple-element.274, f32[128]{0:T(128)S(1)} %multiply_reduce_fusion), channel_id=1, replica_groups=mesh['ctx'=64,'tp'=8] {'tp'}, use_global_device_ids=true, to_apply=%region_4.5 | all-reduce | flops 256 | bytes 2048 | tf_op jit(solution)/shard_map/psum | solution.py:70
  402.4 1.9 multiply_subtract_fusion
  404.4 2.0 convolution_add_fusion
  409.4 286.9 %all-gather.8.cloned.1.call-done = f32[512,128,128]{2,1,0:T(8,128)} async-done(((f32[8,128,128]{2,1,0:T(8,128)}), f32[512,128,128]{2,1,0:T(8,128)}) %all-gather.8.cloned.1.call-update) | async-done | bytes 33554448 | tf_op jit(solution)/shard_map/all_gather | solution.py:12
  696.3 23.0 %rev.7 = f32[64,8,128,128]{3,2,1,0:T(8,128)} reverse(f32[64,8,128,128]{3,2,1,0:T(8,128)} %bitcast.168), dimensions={0} | reverse | bytes 67108864 | tf_op jit(solution)/shard_map/rev | solution.py:14
  719.3 76.5 %while.29 = (s32[]{:T(128)}, f32[8,128,128]{2,1,0:T(8,128)S(1)}, s32[]{:T(128)}, f32[64,8]{1,0:T(8,128)S(1)}, f32[64,8,128,128]{3,2,1,0:T(8,128)}, /*index=5*/s32[]{:T(128)}, s32[]{:T(128)}) while((s32[]{:T(128)}, f32[8,128,128]{2,1,0:T(8,128)S(1)}, s32[]{:T(128)}, f32[64,8]{1,0:T(8,128)S(1)}, f32[64,8,128,128]{3,2,1,0:T(8,128)}, ...), condition=%wide.region_8.9_spmd.clone, body=%wide.region_7.8_spmd.clone.sunk | while | flops 524292 | bytes 1573065 | solution.py:24
  720.5 1.2 fusion.64
  723.0 1.2 fusion.64
  724.2 1.2 fusion.64
  725.4 1.2 fusion.64
  726.6 1.2 fusion.64
  727.8 1.2 fusion.64
  729.0 1.2 fusion.64
  730.2 1.2 fusion.64
  731.5 1.2 fusion.64
  732.7 1.2 fusion.64
  733.9 1.2 fusion.64
  735.1 1.2 fusion.64
  736.3 1.2 fusion.64
  (276 shorter events, 147.2 us)
Async XLA Ops:
  7.2 2.5 copy-start
  7.2 303.2 %all-gather.6.cloned.1.call-start = ((), (), s32[]{:S(2)}) async-start(), calls=%async_computation | async-start | bytes 34078720 | tf_op jit(solution)/shard_map/all_gather | solution.py:12
  10.9 685.4 %all-gather.8.cloned.1.call-start = ((), (), s32[]{:S(2)}) async-start(), calls=%async_computation.1 | async-start | bytes 34078720 | tf_op jit(solution)/shard_map/all_gather | solution.py:12
  696.3 99.5 %copy-start.1 = (bf16[128,1024]{1,0:T(8,128)(2,1)S(1)}, bf16[128,1024]{1,0:T(8,128)(2,1)}, u32[]{:S(2)}) copy-start(bf16[128,1024]{1,0:T(8,128)(2,1)} %param.11) | copy-start | bytes 786436
Sparse Core Ops, SparseCore 0:
  11.0 299.3 all-gather.5
  406.6 289.6 all-gather.7
where the time goes:
time: 813 us; the launch traced here: 807 us
  waiting for transfers between devices  512 us (63%)
  other arithmetic  151 us (19%)
  blocking collectives  84.9 us (10%)
  local copies, waits for them, and re-layouts  30.4 us (4%)
  between operations  14.2 us (2%)
  matrix products  10.3 us (1%)
    all_gather x2, waiting for transfers between devices, carried_in(): pieces = jax.tree.map(lambda part: lax.all_gather(part, axis), value)  512 us
    select_n x126, other arithmetic, lap(): jnp.where(position < mine, new, old)  148 us
    all_gather x1, blocking collectives, carried_in(): pieces = jax.tree.map(lambda part: lax.all_gather(part, axis), value)  72.1 us
    rev x2, local copies, waits for them, and re-layouts, carried_in(): pieces = jax.tree.map(lambda part: part[::-1], pieces)  23 us
  transfers between devices with their start and end apart: 2, of which 2 were waited for; matrix products, arithmetic and copies ran while one was open for 1% of the time, Pallas kernels for 0%

commit v1 on v0

v1 whole, which is shorter than its diff:
```python
import functools

import jax
import jax.numpy as jnp
from jax import lax
from jax.experimental import pallas as pl
from jax.experimental.pallas import tpu as pltpu
from jax.sharding import Mesh
from jax.sharding import PartitionSpec as P

epsilon = 1e-06
highest = lax.Precision.HIGHEST
f32 = jnp.float32
bf16 = jnp.bfloat16

NN = (((1,), (0,)), ((), ()))
NT = (((1,), (1,)), ((), ()))
TN = (((0,), (0,)), ((), ()))


def halves(wide):
    high = wide.astype(bf16)
    return high, (wide - high.astype(f32)).astype(bf16)


def product(left, right, dims):
    lefts = halves(left) if left.dtype == f32 else (left,)
    rights = halves(right) if right.dtype == f32 else (right,)
    total = None
    for i, a in enumerate(lefts):
        for j, b in enumerate(rights):
            if i + j < 2:
                term = lax.dot_general(a, b, dims, preferred_element_type=f32)
                total = term if total is None else total + term
    return total


def decays(log_decay):
    rows = log_decay.shape[0]
    above = lax.broadcasted_iota(jnp.int32, (rows, rows), 0)
    along = lax.broadcasted_iota(jnp.int32, (rows, rows), 1)
    upper = (above <= along).astype(f32)
    lower = (above >= along).astype(f32)
    tall = lax.dot_general(lower, log_decay, NN, precision=highest, preferred_element_type=f32)
    wide = lax.dot_general(log_decay, upper, TN, precision=highest, preferred_element_type=f32)
    return tall, wide, above >= along


def weights_of(tall, wide, mask, head):
    differences = tall[:, head : head + 1] - wide[head : head + 1, :]
    return jnp.where(mask, jnp.exp(jnp.where(mask, differences, 0.0)), 0.0)


def cols(head, size):
    return slice(head * size, (head + 1) * size)


def states_kernel(heads, members, key_ref, value_ref, decay_ref, out_ref):
    size = key_ref.shape[1] // heads
    per = members // heads
    rows = size // per
    tall, _, _ = decays(decay_ref[...])
    total = tall[-1:, :]
    trailing = jnp.exp(total - tall)
    for head in range(heads):
        key = key_ref[:, cols(head, size)].astype(f32) * trailing[:, head : head + 1]
        state = product(key, value_ref[:, cols(head, size)], TN)
        mark = jnp.broadcast_to(total[:, head : head + 1], (8, size))
        for part in range(per):
            out_ref[head * per + part, :rows, :] = state[part * rows : (part + 1) * rows, :]
            out_ref[head * per + part, rows:, :] = mark


def times(gain, state):
    return (gain[None] * state.reshape(-1, 8, state.shape[-1])).reshape(state.shape)


def group_kernel(members, copies, backward, rows, piece_ref, decay_ref, out_ref):
    total = None
    order = reversed(range(members)) if backward else range(members)
    whole = jnp.zeros(decay_ref.shape[1:], f32)
    for member in order:
        mark = decay_ref[member]
        state = piece_ref[member, :rows, :]
        total = state if total is None else times(jnp.exp(mark), total) + state
        whole = whole + mark
    for copy in range(copies):
        out_ref[copy, :rows, :] = total
        out_ref[copy, rows:, :] = whole


def spread_kernel(members, groups, backward, rows, mine_ref, piece_ref, decay_ref, total_ref, out_ref):
    mine = mine_ref[0]
    running = jnp.zeros((rows, piece_ref.shape[-1]), f32)
    for group in reversed(range(groups)) if backward else range(groups):
        longer = times(jnp.exp(total_ref[group, rows:, :]), running) + total_ref[group, :rows, :]
        running = jnp.where(group > mine if backward else group < mine, longer, running)
    for member in reversed(range(members)) if backward else range(members):
        out_ref[member] = running
        running = times(jnp.exp(decay_ref[member]), running) + piece_ref[member, :rows, :]


def inside_kernel(heads, query_ref, key_ref, value_ref, decay_ref, out_ref):
    size = key_ref.shape[1] // heads
    tall, wide, mask = decays(decay_ref[...])
    for head in range(heads):
        here = cols(head, size)
        scores = product(query_ref[:, here], key_ref[:, here], NT) * weights_of(tall, wide, mask, head)
        out_ref[:, here] = product(scores, value_ref[:, here], NN)


def mixed_kernel(
    heads, query_ref, decay_ref, inside_ref, state_ref, gain_ref, grad_ref, out_ref, sums_ref
):
    size = query_ref.shape[1] // heads
    rows = query_ref.shape[0]
    tall, _, _ = decays(decay_ref[...])
    rising = jnp.exp(tall)
    squares = jnp.zeros((rows, size), f32)
    products = jnp.zeros((rows, size), f32)
    for head in range(heads):
        here = cols(head, size)
        outside = product(query_ref[:, here], state_ref[head], NN)
        mixed = inside_ref[:, here] + outside * rising[:, head : head + 1]
        out_ref[:, here] = mixed
        squares = squares + mixed * mixed
        products = products + grad_ref[:, here].astype(f32) * gain_ref[:, here] * mixed
    ones = jnp.ones((8, size), f32)
    square = lax.dot_general(ones, squares, NT, precision=highest, preferred_element_type=f32)
    product_ = lax.dot_general(ones, products, NT, precision=highest, preferred_element_type=f32)
    sums_ref[0:1, :] = square[0:1, :]
    sums_ref[1:2, :] = product_[0:1, :]


def norm_kernel(
    heads, members, full_width, query_ref, decay_ref, mixed_ref, gain_ref, grad_ref, sums_ref, normed_ref, slope_ref, out_ref
):
    size = query_ref.shape[1] // heads
    per = members // heads
    cut = size // per
    tall, _, _ = decays(decay_ref[...])
    rising = jnp.exp(tall)
    ones = jnp.ones((sums_ref.shape[0], size), f32)
    square = lax.dot_general(sums_ref[:, 0, :], ones, TN, precision=highest, preferred_element_type=f32)
    product_ = lax.dot_general(sums_ref[:, 1, :], ones, TN, precision=highest, preferred_element_type=f32)
    scale = lax.rsqrt(square / full_width + epsilon)
    pull = scale * scale * scale * (product_ / full_width)
    for head in range(heads):
        here = cols(head, size)
        mixed = mixed_ref[:, here]
        gain = gain_ref[:, here]
        normed_ref[:, here] = (mixed * scale * gain).astype(bf16)
        slope = scale * (grad_ref[:, here].astype(f32) * gain) - pull * mixed
        slope_ref[:, here] = slope
        state = product(query_ref[:, here], slope * rising[:, head : head + 1], TN)
        for part in range(per):
            out_ref[head * per + part] = state[part * cut : (part + 1) * cut, :]


def near_kernel(
    heads, query_ref, key_ref, value_ref, decay_ref, state_ref, slope_ref, grad_q_ref, near_k_ref, near_v_ref
):
    size = key_ref.shape[1] // heads
    tall, wide, mask = decays(decay_ref[...])
    rising = jnp.exp(tall)
    for head in range(heads):
        here = cols(head, size)
        query, key, value = query_ref[:, here], key_ref[:, here], value_ref[:, here]
        slope = slope_ref[:, here]
        weights = weights_of(tall, wide, mask, head)
        scores = product(query, key, NT) * weights
        grad_scores = product(slope, value, NT) * weights
        outer = product(slope, state_ref[head], NT) * rising[:, head : head + 1]
        grad_q_ref[:, here] = (product(grad_scores, key, NN) + outer).astype(bf16)
        near_k_ref[:, here] = product(grad_scores, query, TN)
        near_v_ref[:, here] = product(scores, slope, TN)


def far_kernel(heads, key_ref, value_ref, decay_ref, state_ref, near_k_ref, near_v_ref, grad_k_ref, grad_v_ref):
    size = key_ref.shape[1] // heads
    tall, _, _ = decays(decay_ref[...])
    trailing = jnp.exp(tall[-1:, :] - tall)
    for head in range(heads):
        here = cols(head, size)
        late = trailing[:, head : head + 1]
        state = state_ref[head]
        grad_k = near_k_ref[:, here] + product(value_ref[:, here], state, NT) * late
        grad_v = near_v_ref[:, here] + product(key_ref[:, here], state, NN) * late
        grad_k_ref[:, here] = grad_k.astype(bf16)
        grad_v_ref[:, here] = grad_v.astype(bf16)


def call(kernel, outs, *args, scalars=0, flops=0):
    vmem = pl.BlockSpec(memory_space=pltpu.VMEM)
    smem = pl.BlockSpec(memory_space=pltpu.SMEM)
    moved = sum(a.size * a.dtype.itemsize for a in (*args, *outs))
    return pl.pallas_call(
        kernel,
        out_shape=outs,
        in_specs=[smem] * scalars + [vmem] * (len(args) - scalars),
        out_specs=[vmem] * len(outs),
        cost_estimate=pl.CostEstimate(flops=flops, bytes_accessed=moved, transcendentals=0),
        compiler_params=pltpu.CompilerParams(vmem_limit_bytes=32 * 1024 * 1024),
    )(*args)


def shards(groups, tp, queries, key_rows, value_rows, log_decay, norm_gain, grad_output):
    near, far = ("zl", "x"), "zh"
    members = lax.axis_size(near)
    tok_rows, feat_width = queries.shape
    heads = log_decay.shape[1]
    size = feat_width // heads
    rows = heads * size // members
    wide = jax.ShapeDtypeStruct((tok_rows, feat_width), f32)
    narrow = jax.ShapeDtypeStruct((tok_rows, feat_width), bf16)
    gain = norm_gain.reshape(1, feat_width)
    mine = lax.axis_index(far).astype(jnp.int32).reshape(1)
    bind = functools.partial
    shape = jax.ShapeDtypeStruct
    unit = 2 * heads * tok_rows * size * size

    def exchange(parts, axis):
        return lax.all_to_all(parts, axis, 0, 0)

    def carried(pieces, marks, backward):
        (total,) = call(
            bind(group_kernel, members, groups, backward, rows),
            [shape((groups, rows + 8, size), f32)],
            pieces,
            marks,
        )
        totals = exchange(total, far)
        (entering,) = call(
            bind(spread_kernel, members, groups, backward, rows),
            [shape((members, rows, size), f32)],
            mine,
            pieces,
            marks,
            totals,
            scalars=1,
        )
        return exchange(entering, near).reshape(heads, size, size)

    (states,) = call(
        bind(states_kernel, heads, members),
        [shape((members, rows + 8, size), f32)],
        key_rows,
        value_rows,
        log_decay,
        flops=2 * unit,
    )
    pieces = exchange(states, near)
    marks = pieces[:, rows:, :]
    (inside,) = call(
        bind(inside_kernel, heads), [wide], queries, key_rows, value_rows, log_decay, flops=3 * unit
    )
    entry = carried(pieces, marks, False)
    mixed, sums = call(
        bind(mixed_kernel, heads),
        [wide, shape((2, tok_rows), f32)],
        queries,
        log_decay,
        inside,
        entry,
        gain,
        grad_output,
        flops=2 * unit,
    )
    gathered = lax.all_gather(sums, tp)
    normed, slope, back = call(
        bind(norm_kernel, heads, members, feat_width * lax.axis_size(tp)),
        [narrow, wide, shape((members, rows, size), f32)],
        queries,
        log_decay,
        mixed,
        gain,
        grad_output,
        gathered,
        flops=2 * unit,
    )
    back_pieces = exchange(back, near)
    grad_q, near_k, near_v = call(
        bind(near_kernel, heads),
        [narrow, wide, wide],
        queries,
        key_rows,
        value_rows,
        log_decay,
        entry,
        slope,
        flops=13 * unit,
    )
    leaving = carried(back_pieces, marks, True)
    grad_k, grad_v = call(
        bind(far_kernel, heads),
        [narrow, narrow],
        key_rows,
        value_rows,
        log_decay,
        leaving,
        near_k,
        near_v,
        flops=4 * unit,
    )
    return normed, grad_q, grad_k, grad_v


def solution(mesh):
    groups = 4
    folded = Mesh(mesh.devices.reshape(groups, 4, 4, -1), ("zh", "zl", "x", "tp"))
    both = P(("zh", "zl", "x"), "tp")
    return jax.shard_map(
        functools.partial(shards, groups, "tp"),
        mesh=folded,
        in_specs=(both, both, both, both, P("tp"), both),
        out_specs=(both, both, both, both),
        check_vma=False,
    )
```

time: 813 us -> 149 us (0.18)
  the two profiles are of different devices: /device:TPU:1 before, /device:TPU:32 now
where the time goes in v1:
time: 149 us; the launch traced here: 148 us
  blocking collectives  75.9 us (51%)
  waiting for transfers between devices  32.5 us (22%)
  starting transfers between devices  23.6 us (16%)
  Pallas kernels  10.8 us (7%)
  local copies, waits for them, and re-layouts  4.55 us (3%)
    all_to_all x3, blocking collectives, exchange(): return lax.all_to_all(parts, axis, 0, 0)  65.1 us
    all_to_all x3, waiting for transfers between devices, exchange(): return lax.all_to_all(parts, axis, 0, 0)  32.5 us
    all_to_all x3, starting transfers between devices, exchange(): return lax.all_to_all(parts, axis, 0, 0)  23.6 us
    all_gather x1, blocking collectives, shards(): gathered = lax.all_gather(sums, tp)  10.8 us
    pallas_call x10, Pallas kernels, call(): pl.pallas_call(kernel, out_shape=outs, in_specs=[smem] * scalars + [vmem]...  10.8 us
    unnamed x19, local copies, waits for them, and re-layouts  4.55 us
  transfers between devices with their start and end apart: 3, of which 3 were waited for; matrix products, arithmetic and copies ran while one was open for 0% of the time, Pallas kernels for 3%

profile of v1, /device:TPU:32, one launch (start us, length us, event | category | flops | bytes accessed | tf_op | source)
XLA Modules:
  0.0 148.1 jit_solution(6345747414654104280)
XLA Ops:
  0.6 0.8 copy.19.decay_ref
  1.4 0.9 copy-done.1
  2.4 0.9 copy-done.3
  3.3 0.8 shard_map.94
  4.1 24.9 %all_to_all.30.piece_ref = f32[16,72,128]{2,1,0:T(8,128)S(1)} all-to-all(f32[16,72,128]{2,1,0:T(8,128)S(1)} %shard_map.94), channel_id=1, replica_groups=mesh['zh'=4,'zl'=4,'x'=4,'tp'=8] {'zl','x'}, dimensions={0} | all-to-all | bytes 1179648 | tf_op jit(solution)/shard_map/all_to_all | solution.py:223
  29.0 0.7 shard_map.95
  29.7 12.4 %all-to-all-start.1 = ((f32[4,72,128]{2,1,0:T(8,128)}), f32[4,72,128]{2,1,0:T(8,128)S(1)}, u32[]{:S(2)}, u32[]{:S(2)}) async-start(f32[4,72,128]{2,1,0:T(8,128)} %shard_map.95), calls=%async_computation.1 | async-start | bytes 294912 | tf_op jit(solution)/shard_map/all_to_all | solution.py:223
  42.1 14.1 %all-to-all-done.1.total_ref = f32[4,72,128]{2,1,0:T(8,128)S(1)} async-done(((f32[4,72,128]{2,1,0:T(8,128)}), f32[4,72,128]{2,1,0:T(8,128)S(1)}, u32[]{:S(2)}, u32[]{:S(2)}) %all-to-all-start.1) | async-done | bytes 147488 | tf_op jit(solution)/shard_map/all_to_all | solution.py:223
  56.2 0.9 shard_map.96
  57.0 6.8 %all-to-all-start.2 = ((f32[16,64,128]{2,1,0:T(8,128)}), f32[16,64,128]{2,1,0:T(8,128)S(1)}, u32[]{:S(2)}, u32[]{:S(2)}) async-start(f32[16,64,128]{2,1,0:T(8,128)} %shard_map.96), calls=%async_computation.2 | async-start | bytes 1048576 | tf_op jit(solution)/shard_map/all_to_all | solution.py:223
  63.9 0.7 shard_map.93.inside_ref
  64.7 10.6 %all-to-all-done.2 = f32[16,64,128]{2,1,0:T(8,128)S(1)} async-done(((f32[16,64,128]{2,1,0:T(8,128)}), f32[16,64,128]{2,1,0:T(8,128)S(1)}, u32[]{:S(2)}, u32[]{:S(2)}) %all-to-all-start.2) | async-done | bytes 524320 | tf_op jit(solution)/shard_map/all_to_all | solution.py:223
  75.3 0.8 shard_map.97
  76.1 10.8 %all-gather.1.sums_ref = f32[8,2,128]{2,1,0:T(2,128)S(1)} all-gather(f32[1,2,128]{2,1,0:T(2,128)S(1)} %bitcast.10), channel_id=2, replica_groups=mesh['zh'=4,'zl'=4,'x'=4,'tp'=8] {'tp'}, dimensions={0}, use_global_device_ids=true | all-gather | bytes 9216 | tf_op jit(solution)/shard_map/all_gather | solution.py:269
  86.9 1.1 shard_map.98
  88.0 20.2 %all_to_all.31.piece_ref = f32[16,64,128]{2,1,0:T(8,128)S(1)} all-to-all(f32[16,64,128]{2,1,0:T(8,128)S(1)} %get-tuple-element.19), channel_id=1, replica_groups=mesh['zh'=4,'zl'=4,'x'=4,'tp'=8] {'zl','x'}, dimensions={0} | all-to-all | bytes 1048576 | tf_op jit(solution)/shard_map/all_to_all | solution.py:223
  108.3 20.0 %all_to_all.32.total_ref = f32[4,72,128]{2,1,0:T(8,128)S(1)} all-to-all(f32[4,72,128]{2,1,0:T(8,128)S(1)} %shard_map.100), channel_id=1, replica_groups=mesh['zh'=4,'zl'=4,'x'=4,'tp'=8] {'zh'}, dimensions={0} | all-to-all | bytes 294912 | tf_op jit(solution)/shard_map/all_to_all | solution.py:223
  128.3 0.9 shard_map.101
  129.1 4.4 %all-to-all-start.5 = ((f32[16,64,128]{2,1,0:T(8,128)}), f32[16,64,128]{2,1,0:T(8,128)S(1)}, u32[]{:S(2)}, u32[]{:S(2)}) async-start(f32[16,64,128]{2,1,0:T(8,128)} %shard_map.101), calls=%async_computation.5 | async-start | bytes 1048576 | tf_op jit(solution)/shard_map/all_to_all | solution.py:223
  133.6 3.3 %shard_map.99 = (bf16[128,1024]{1,0:T(8,128)(2,1)}, f32[128,1024]{1,0:T(8,128)S(1)}, f32[128,1024]{1,0:T(8,128)S(1)}) custom-call(bf16[128,1024]{1,0:T(8,128)(2,1)S(1)} %copy-done, bf16[128,1024]{1,0:T(8,128)(2,1)S(1)} %copy-done.2, bf16[128,1024]{1,0:T(8,128)(2,1)S(1)} %copy-done.4, f32[128,8]{1,0:T(8,128)S(1)} %copy.19.decay_ref, ...), custom_call_target="tpu_custom_call" | custom-call | flops 436207616 | bytes 3149824 | tf_op jit(solution)/shard_map/pallas_call | solution.py:197
  136.9 0.8 copy-done.6
  137.7 7.9 %all-to-all-done.5 = f32[16,64,128]{2,1,0:T(8,128)S(1)} async-done(((f32[16,64,128]{2,1,0:T(8,128)}), f32[16,64,128]{2,1,0:T(8,128)S(1)}, u32[]{:S(2)}, u32[]{:S(2)}) %all-to-all-start.5) | async-done | bytes 524320 | tf_op jit(solution)/shard_map/all_to_all | solution.py:223
  145.5 1.0 copy-done.7
  146.6 1.5 %shard_map.102 = (bf16[128,1024]{1,0:T(8,128)(2,1)}, bf16[128,1024]{1,0:T(8,128)(2,1)}) custom-call(bf16[128,1024]{1,0:T(8,128)(2,1)S(1)} %copy-done.2, bf16[128,1024]{1,0:T(8,128)(2,1)S(1)} %copy-done.4, f32[128,8]{1,0:T(8,128)S(1)} %copy.19.decay_ref, f32[8,128,128]{2,1,0:T(8,128)S(1)} %bitcast.7, f32[128,1024]{1,0:T(8,128)S(1)} %get-tuple-element.20.near_k_ref, ...), custom_call_target="tpu_custom_call" | custom-call | flops 134217728 | bytes 2625536 | tf_op jit(solution)/shard_map/pallas_call | solution.py:197
  (16 shorter events, 0.1 us)
Async XLA Ops:
  1.4 0.9 copy-start.1
  2.4 0.9 copy-start.3
  29.7 26.4 %all-to-all-start.1 = ((f32[4,72,128]{2,1,0:T(8,128)}), f32[4,72,128]{2,1,0:T(8,128)S(1)}, u32[]{:S(2)}, u32[]{:S(2)}) async-start(f32[4,72,128]{2,1,0:T(8,128)} %shard_map.95), calls=%async_computation.1 | async-start | bytes 294912 | tf_op jit(solution)/shard_map/all_to_all | solution.py:223
  57.0 6.8 %copy-start = (bf16[128,1024]{1,0:T(8,128)(2,1)S(1)}, bf16[128,1024]{1,0:T(8,128)(2,1)}, u32[]{:S(2)}) copy-start(bf16[128,1024]{1,0:T(8,128)(2,1)} %query_ref.7) | copy-start | bytes 786436
  57.0 6.8 %copy-start.2 = (bf16[128,1024]{1,0:T(8,128)(2,1)S(1)}, bf16[128,1024]{1,0:T(8,128)(2,1)}, u32[]{:S(2)}) copy-start(bf16[128,1024]{1,0:T(8,128)(2,1)} %key_ref.7) | copy-start | bytes 786436
  57.0 6.8 %copy-start.4 = (bf16[128,1024]{1,0:T(8,128)(2,1)S(1)}, bf16[128,1024]{1,0:T(8,128)(2,1)}, u32[]{:S(2)}) copy-start(bf16[128,1024]{1,0:T(8,128)(2,1)} %value_ref.7) | copy-start | bytes 786436
  57.0 18.2 %all-to-all-start.2 = ((f32[16,64,128]{2,1,0:T(8,128)}), f32[16,64,128]{2,1,0:T(8,128)S(1)}, u32[]{:S(2)}, u32[]{:S(2)}) async-start(f32[16,64,128]{2,1,0:T(8,128)} %shard_map.96), calls=%async_computation.2 | async-start | bytes 1048576 | tf_op jit(solution)/shard_map/all_to_all | solution.py:223
  63.9 11.4 %copy-start.5 = (bf16[128,1024]{1,0:T(8,128)(2,1)S(1)}, bf16[128,1024]{1,0:T(8,128)(2,1)}, u32[]{:S(2)}) copy-start(bf16[128,1024]{1,0:T(8,128)(2,1)} %grad_ref.3) | copy-start | bytes 786436
  63.9 11.4 %copy-start.8 = (f32[1024]{0:T(1024)S(1)}, f32[1024]{0:T(1024)}, u32[]{:S(2)}) copy-start(f32[1024]{0:T(1024)} %param.10) | copy-start | bytes 12292
  129.1 16.4 %all-to-all-start.5 = ((f32[16,64,128]{2,1,0:T(8,128)}), f32[16,64,128]{2,1,0:T(8,128)S(1)}, u32[]{:S(2)}, u32[]{:S(2)}) async-start(f32[16,64,128]{2,1,0:T(8,128)} %shard_map.101), calls=%async_computation.5 | async-start | bytes 1048576 | tf_op jit(solution)/shard_map/all_to_all | solution.py:223
  136.9 0.8 copy-start.6
  145.5 1.0 copy-start.7

commit v2 on v1

--- a/solution.py
+++ b/solution.py
@@ -36,13 +36,13 @@
 
 
 def decays(log_decay):
-    rows = log_decay.shape[0]
+    rows = log_decay.shape[1]
     above = lax.broadcasted_iota(jnp.int32, (rows, rows), 0)
     along = lax.broadcasted_iota(jnp.int32, (rows, rows), 1)
     upper = (above <= along).astype(f32)
     lower = (above >= along).astype(f32)
-    tall = lax.dot_general(lower, log_decay, NN, precision=highest, preferred_element_type=f32)
-    wide = lax.dot_general(log_decay, upper, TN, precision=highest, preferred_element_type=f32)
+    tall = lax.dot_general(lower, log_decay, NT, precision=highest, preferred_element_type=f32)
+    wide = lax.dot_general(log_decay, upper, NN, precision=highest, preferred_element_type=f32)
     return tall, wide, above >= along
 
 
@@ -55,13 +55,24 @@
     return slice(head * size, (head + 1) * size)
 
 
-def states_kernel(heads, members, key_ref, value_ref, decay_ref, out_ref):
+def states_kernel(heads, members, key_far, value_far, decay_far, out_ref, key_ref, value_ref, decay_ref, sems):
     size = key_ref.shape[1] // heads
     per = members // heads
     rows = size // per
+    copies = [
+        pltpu.make_async_copy(source, target, sems.at[i])
+        for i, (source, target) in enumerate(
+            ((decay_far, decay_ref), (key_far, key_ref), (value_far, value_ref))
+        )
+    ]
+    for copy in copies:
+        copy.start()
+    copies[0].wait()
     tall, _, _ = decays(decay_ref[...])
     total = tall[-1:, :]
     trailing = jnp.exp(total - tall)
+    copies[1].wait()
+    copies[2].wait()
     for head in range(heads):
         key = key_ref[:, cols(head, size)].astype(f32) * trailing[:, head : head + 1]
         state = product(key, value_ref[:, cols(head, size)], TN)
@@ -190,17 +201,20 @@
         grad_v_ref[:, here] = grad_v.astype(bf16)
 
 
-def call(kernel, outs, *args, scalars=0, flops=0):
+def call(kernel, outs, *args, scalars=0, flops=0, copied=()):
     vmem = pl.BlockSpec(memory_space=pltpu.VMEM)
+    hbm = pl.BlockSpec(memory_space=pltpu.HBM)
     smem = pl.BlockSpec(memory_space=pltpu.SMEM)
     moved = sum(a.size * a.dtype.itemsize for a in (*args, *outs))
     return pl.pallas_call(
         kernel,
         out_shape=outs,
-        in_specs=[smem] * scalars + [vmem] * (len(args) - scalars),
+        in_specs=[smem] * scalars + [hbm if copied else vmem] * (len(args) - scalars),
         out_specs=[vmem] * len(outs),
+        scratch_shapes=[pltpu.VMEM(a.shape, a.dtype) for a in copied]
+        + ([pltpu.SemaphoreType.DMA((len(copied),))] if copied else []),
         cost_estimate=pl.CostEstimate(flops=flops, bytes_accessed=moved, transcendentals=0),
-        compiler_params=pltpu.CompilerParams(vmem_limit_bytes=32 * 1024 * 1024),
+        compiler_params=pltpu.CompilerParams(vmem_limit_bytes=12 * 1024 * 1024),
     )(*args)
 
 
@@ -214,6 +228,7 @@
     wide = jax.ShapeDtypeStruct((tok_rows, feat_width), f32)
     narrow = jax.ShapeDtypeStruct((tok_rows, feat_width), bf16)
     gain = norm_gain.reshape(1, feat_width)
+    log_decay = log_decay.T
     mine = lax.axis_index(far).astype(jnp.int32).reshape(1)
     bind = functools.partial
     shape = jax.ShapeDtypeStruct
@@ -248,6 +263,7 @@
         value_rows,
         log_decay,
         flops=2 * unit,
+        copied=(key_rows, value_rows, log_decay),
     )
     pieces = exchange(states, near)
     marks = pieces[:, rows:, :]

time: 149 us -> 149 us (level)
    unnamed x19 -> x22, local copies, waits for them, and re-layouts: 4.55 us -> 4.44 us
where the time goes in v2:
time: 149 us; the launch traced here: 148 us
  blocking collectives  75.9 us (51%)
  waiting for transfers between devices  32.6 us (22%)
  starting transfers between devices  23.6 us (16%)
  Pallas kernels  10.8 us (7%)
  local copies, waits for them, and re-layouts  4.45 us (3%)
    all_to_all x3, blocking collectives, exchange(): return lax.all_to_all(parts, axis, 0, 0)  65.1 us
    all_to_all x3, waiting for transfers between devices, exchange(): return lax.all_to_all(parts, axis, 0, 0)  32.6 us
    all_to_all x3, starting transfers between devices, exchange(): return lax.all_to_all(parts, axis, 0, 0)  23.6 us
    all_gather x1, blocking collectives, shards(): gathered = lax.all_gather(sums, tp)  10.8 us
    pallas_call x10, Pallas kernels, call(): pl.pallas_call(kernel, out_shape=outs, in_specs=[smem] * scalars + [hbm i...  10.8 us
    unnamed x22, local copies, waits for them, and re-layouts  4.44 us
  transfers between devices with their start and end apart: 3, of which 3 were waited for; matrix products, arithmetic and copies ran while one was open for 0% of the time, Pallas kernels for 3%

profile of v2, /device:TPU:32, one launch (start us, length us, event | category | flops | bytes accessed | tf_op | source)
XLA Modules:
  0.0 148.1 jit_solution(6498761036305255248)
XLA Ops:
  0.6 0.9 copy-done.1
  1.6 0.9 copy-done.3
  2.5 0.7 copy-done.8
  3.2 1.0 shard_map.94
  4.2 24.9 %all_to_all.30.piece_ref = f32[16,72,128]{2,1,0:T(8,128)S(1)} all-to-all(f32[16,72,128]{2,1,0:T(8,128)S(1)} %shard_map.94), channel_id=1, replica_groups=mesh['zh'=4,'zl'=4,'x'=4,'tp'=8] {'zl','x'}, dimensions={0} | all-to-all | bytes 1179648 | tf_op jit(solution)/shard_map/all_to_all | solution.py:238
  29.1 0.7 shard_map.95
  29.8 12.4 %all-to-all-start.1 = ((f32[4,72,128]{2,1,0:T(8,128)}), f32[4,72,128]{2,1,0:T(8,128)S(1)}, u32[]{:S(2)}, u32[]{:S(2)}) async-start(f32[4,72,128]{2,1,0:T(8,128)} %shard_map.95), calls=%async_computation.1 | async-start | bytes 294912 | tf_op jit(solution)/shard_map/all_to_all | solution.py:238
  42.2 14.1 %all-to-all-done.1.total_ref = f32[4,72,128]{2,1,0:T(8,128)S(1)} async-done(((f32[4,72,128]{2,1,0:T(8,128)}), f32[4,72,128]{2,1,0:T(8,128)S(1)}, u32[]{:S(2)}, u32[]{:S(2)}) %all-to-all-start.1) | async-done | bytes 147488 | tf_op jit(solution)/shard_map/all_to_all | solution.py:238
  56.3 0.9 shard_map.96
  57.1 6.8 %all-to-all-start.2 = ((f32[16,64,128]{2,1,0:T(8,128)}), f32[16,64,128]{2,1,0:T(8,128)S(1)}, u32[]{:S(2)}, u32[]{:S(2)}) async-start(f32[16,64,128]{2,1,0:T(8,128)} %shard_map.96), calls=%async_computation.2 | async-start | bytes 1048576 | tf_op jit(solution)/shard_map/all_to_all | solution.py:238
  64.0 0.7 shard_map.93.inside_ref
  64.7 10.6 %all-to-all-done.2 = f32[16,64,128]{2,1,0:T(8,128)S(1)} async-done(((f32[16,64,128]{2,1,0:T(8,128)}), f32[16,64,128]{2,1,0:T(8,128)S(1)}, u32[]{:S(2)}, u32[]{:S(2)}) %all-to-all-start.2) | async-done | bytes 524320 | tf_op jit(solution)/shard_map/all_to_all | solution.py:238
  75.4 0.8 shard_map.97
  76.1 10.8 %all-gather.1.sums_ref = f32[8,2,128]{2,1,0:T(2,128)S(1)} all-gather(f32[1,2,128]{2,1,0:T(2,128)S(1)} %bitcast.17), channel_id=2, replica_groups=mesh['zh'=4,'zl'=4,'x'=4,'tp'=8] {'tp'}, dimensions={0}, use_global_device_ids=true | all-gather | bytes 9216 | tf_op jit(solution)/shard_map/all_gather | solution.py:285
  87.0 1.1 shard_map.98
  88.1 20.2 %all_to_all.31.piece_ref = f32[16,64,128]{2,1,0:T(8,128)S(1)} all-to-all(f32[16,64,128]{2,1,0:T(8,128)S(1)} %get-tuple-element.19), channel_id=1, replica_groups=mesh['zh'=4,'zl'=4,'x'=4,'tp'=8] {'zl','x'}, dimensions={0} | all-to-all | bytes 1048576 | tf_op jit(solution)/shard_map/all_to_all | solution.py:238
  108.3 20.0 %all_to_all.32.total_ref = f32[4,72,128]{2,1,0:T(8,128)S(1)} all-to-all(f32[4,72,128]{2,1,0:T(8,128)S(1)} %shard_map.100), channel_id=1, replica_groups=mesh['zh'=4,'zl'=4,'x'=4,'tp'=8] {'zh'}, dimensions={0} | all-to-all | bytes 294912 | tf_op jit(solution)/shard_map/all_to_all | solution.py:238
  128.3 0.9 shard_map.101
  129.2 4.4 %all-to-all-start.5 = ((f32[16,64,128]{2,1,0:T(8,128)}), f32[16,64,128]{2,1,0:T(8,128)S(1)}, u32[]{:S(2)}, u32[]{:S(2)}) async-start(f32[16,64,128]{2,1,0:T(8,128)} %shard_map.101), calls=%async_computation.5 | async-start | bytes 1048576 | tf_op jit(solution)/shard_map/all_to_all | solution.py:238
  133.6 3.2 %shard_map.99 = (bf16[128,1024]{1,0:T(8,128)(2,1)}, f32[128,1024]{1,0:T(8,128)S(1)}, f32[128,1024]{1,0:T(8,128)S(1)}) custom-call(bf16[128,1024]{1,0:T(8,128)(2,1)S(1)} %copy-done, bf16[128,1024]{1,0:T(8,128)(2,1)S(1)} %copy-done.2, bf16[128,1024]{1,0:T(8,128)(2,1)S(1)} %copy-done.4, f32[8,128]{1,0:T(8,128)S(1)} %bitcast.13, f32[8,128,128]{2,1,0:T(8,128)S(1)} %bitcast.7, ...), custom_call_target="tpu_custom_call" | custom-call | flops 436207616 | bytes 3149824 | tf_op jit(solution)/shard_map/pallas_call | solution.py:209
  136.8 0.8 copy-done.6
  137.6 7.9 %all-to-all-done.5 = f32[16,64,128]{2,1,0:T(8,128)S(1)} async-done(((f32[16,64,128]{2,1,0:T(8,128)}), f32[16,64,128]{2,1,0:T(8,128)S(1)}, u32[]{:S(2)}, u32[]{:S(2)}) %all-to-all-start.5) | async-done | bytes 524320 | tf_op jit(solution)/shard_map/all_to_all | solution.py:238
  145.6 1.0 copy-done.7
  146.6 1.5 shard_map.102
  (19 shorter events, 0.1 us)
Async XLA Ops:
  0.6 1.0 copy-start.1
  1.6 0.9 copy-start.3
  2.5 0.7 copy-start.8
  29.8 26.4 %all-to-all-start.1 = ((f32[4,72,128]{2,1,0:T(8,128)}), f32[4,72,128]{2,1,0:T(8,128)S(1)}, u32[]{:S(2)}, u32[]{:S(2)}) async-start(f32[4,72,128]{2,1,0:T(8,128)} %shard_map.95), calls=%async_computation.1 | async-start | bytes 294912 | tf_op jit(solution)/shard_map/all_to_all | solution.py:238
  57.1 6.8 %copy-start = (bf16[128,1024]{1,0:T(8,128)(2,1)S(1)}, bf16[128,1024]{1,0:T(8,128)(2,1)}, u32[]{:S(2)}) copy-start(bf16[128,1024]{1,0:T(8,128)(2,1)} %query_ref.7) | copy-start | bytes 786436
  57.1 6.8 %copy-start.2 = (bf16[128,1024]{1,0:T(8,128)(2,1)S(1)}, bf16[128,1024]{1,0:T(8,128)(2,1)}, u32[]{:S(2)}) copy-start(bf16[128,1024]{1,0:T(8,128)(2,1)} %key_ref.5) | copy-start | bytes 786436
  57.1 6.8 %copy-start.4 = (bf16[128,1024]{1,0:T(8,128)(2,1)S(1)}, bf16[128,1024]{1,0:T(8,128)(2,1)}, u32[]{:S(2)}) copy-start(bf16[128,1024]{1,0:T(8,128)(2,1)} %value_ref.5) | copy-start | bytes 786436
  57.1 6.9 %copy-start.9 = (f32[128,8]{0,1:T(8,128)S(1)}, f32[128,8]{0,1:T(8,128)}, u32[]{:S(2)}) copy-start(f32[128,8]{0,1:T(8,128)} %param.9) | copy-start | bytes 12292
  57.1 18.2 %all-to-all-start.2 = ((f32[16,64,128]{2,1,0:T(8,128)}), f32[16,64,128]{2,1,0:T(8,128)S(1)}, u32[]{:S(2)}, u32[]{:S(2)}) async-start(f32[16,64,128]{2,1,0:T(8,128)} %shard_map.96), calls=%async_computation.2 | async-start | bytes 1048576 | tf_op jit(solution)/shard_map/all_to_all | solution.py:238
  64.0 11.4 %copy-start.5 = (bf16[128,1024]{1,0:T(8,128)(2,1)S(1)}, bf16[128,1024]{1,0:T(8,128)(2,1)}, u32[]{:S(2)}) copy-start(bf16[128,1024]{1,0:T(8,128)(2,1)} %grad_ref.3) | copy-start | bytes 786436
  64.0 11.4 %copy-start.10 = (f32[1024]{0:T(1024)S(1)}, f32[1024]{0:T(1024)}, u32[]{:S(2)}) copy-start(f32[1024]{0:T(1024)} %param.10) | copy-start | bytes 12292
  129.2 16.4 %all-to-all-start.5 = ((f32[16,64,128]{2,1,0:T(8,128)}), f32[16,64,128]{2,1,0:T(8,128)S(1)}, u32[]{:S(2)}, u32[]{:S(2)}) async-start(f32[16,64,128]{2,1,0:T(8,128)} %shard_map.101), calls=%async_computation.5 | async-start | bytes 1048576 | tf_op jit(solution)/shard_map/all_to_all | solution.py:238
  136.8 0.8 copy-start.6
  145.6 1.0 copy-start.7

commit v3 on v2

--- a/solution.py
+++ b/solution.py
@@ -183,7 +183,7 @@
         grad_scores = product(slope, value, NT) * weights
         outer = product(slope, state_ref[head], NT) * rising[:, head : head + 1]
         grad_q_ref[:, here] = (product(grad_scores, key, NN) + outer).astype(bf16)
-        near_k_ref[:, here] = product(grad_scores, query, TN)
+        near_k_ref[head] = product(grad_scores, query, TN)
         near_v_ref[:, here] = product(scores, slope, TN)
 
 
@@ -195,22 +195,25 @@
         here = cols(head, size)
         late = trailing[:, head : head + 1]
         state = state_ref[head]
-        grad_k = near_k_ref[:, here] + product(value_ref[:, here], state, NT) * late
+        grad_k = near_k_ref[head] + product(value_ref[:, here], state, NT) * late
         grad_v = near_v_ref[:, here] + product(key_ref[:, here], state, NN) * late
         grad_k_ref[:, here] = grad_k.astype(bf16)
         grad_v_ref[:, here] = grad_v.astype(bf16)
 
 
-def call(kernel, outs, *args, scalars=0, flops=0, copied=()):
+def call(kernel, outs, *args, scalars=0, flops=0, copied=(), aliases=None):
     vmem = pl.BlockSpec(memory_space=pltpu.VMEM)
     hbm = pl.BlockSpec(memory_space=pltpu.HBM)
     smem = pl.BlockSpec(memory_space=pltpu.SMEM)
+    if copied:
+        args = [pltpu.with_memory_space_constraint(a, pltpu.HBM) for a in args]
     moved = sum(a.size * a.dtype.itemsize for a in (*args, *outs))
     return pl.pallas_call(
         kernel,
         out_shape=outs,
         in_specs=[smem] * scalars + [hbm if copied else vmem] * (len(args) - scalars),
         out_specs=[vmem] * len(outs),
+        input_output_aliases=aliases or {},
         scratch_shapes=[pltpu.VMEM(a.shape, a.dtype) for a in copied]
         + ([pltpu.SemaphoreType.DMA((len(copied),))] if copied else []),
         cost_estimate=pl.CostEstimate(flops=flops, bytes_accessed=moved, transcendentals=0),
@@ -297,7 +300,7 @@
     back_pieces = exchange(back, near)
     grad_q, near_k, near_v = call(
         bind(near_kernel, heads),
-        [narrow, wide, wide],
+        [narrow, shape((heads, size, size), f32), wide],
         queries,
         key_rows,
         value_rows,
@@ -305,6 +308,7 @@
         entry,
         slope,
         flops=13 * unit,
+        aliases={4: 1, 5: 2},
     )
     leaving = carried(back_pieces, marks, True)
     grad_k, grad_v = call(

time: 149 us -> 146 us (0.980)
  local copies, waits for them, and re-layouts: 4.45 us -> 0.03 us
    unnamed x22 -> x12, local copies, waits for them, and re-layouts: 4.44 us -> 0.03 us
where the time goes in v3:
time: 146 us; the launch traced here: 145 us
  blocking collectives  75.9 us (52%)
  waiting for transfers between devices  33.4 us (23%)
  starting transfers between devices  23.6 us (16%)
  Pallas kernels  11.5 us (8%)
    all_to_all x3, blocking collectives, exchange(): return lax.all_to_all(parts, axis, 0, 0)  65.1 us
    all_to_all x3, waiting for transfers between devices, exchange(): return lax.all_to_all(parts, axis, 0, 0)  33.4 us
    all_to_all x3, starting transfers between devices, exchange(): return lax.all_to_all(parts, axis, 0, 0)  23.6 us
    pallas_call x10, Pallas kernels, call(): pl.pallas_call(kernel, out_shape=outs, in_specs=[smem] * scalars + [hbm i...  11.5 us
    all_gather x1, blocking collectives, shards(): gathered = lax.all_gather(sums, tp)  10.8 us
  transfers between devices with their start and end apart: 3, of which 3 were waited for; matrix products, arithmetic and copies ran while one was open for 0% of the time, Pallas kernels for 3%

profile of v3, /device:TPU:32, one launch (start us, length us, event | category | flops | bytes accessed | tf_op | source)
XLA Modules:
  0.0 145.2 jit_solution(1327408896920357088)
XLA Ops:
  0.6 1.8 %shard_map.94 = f32[16,72,128]{2,1,0:T(8,128)S(1)} custom-call(bf16[128,1024]{1,0:T(8,128)(2,1)} %key_ref.5, bf16[128,1024]{1,0:T(8,128)(2,1)} %value_ref.5, f32[8,128]{1,0:T(8,128)} %bitcast.9), custom_call_target="tpu_custom_call" | custom-call | flops 67108864 | bytes 1118208 | tf_op jit(solution)/shard_map/pallas_call | solution.py:211
  2.4 24.9 %all_to_all.30.piece_ref = f32[16,72,128]{2,1,0:T(8,128)S(1)} all-to-all(f32[16,72,128]{2,1,0:T(8,128)S(1)} %shard_map.94), channel_id=1, replica_groups=mesh['zh'=4,'zl'=4,'x'=4,'tp'=8] {'zl','x'}, dimensions={0} | all-to-all | bytes 1179648 | tf_op jit(solution)/shard_map/all_to_all | solution.py:241
  27.3 0.7 shard_map.95
  28.0 12.4 %all-to-all-start.1 = ((f32[4,72,128]{2,1,0:T(8,128)}), f32[4,72,128]{2,1,0:T(8,128)S(1)}, u32[]{:S(2)}, u32[]{:S(2)}) async-start(f32[4,72,128]{2,1,0:T(8,128)} %shard_map.95), calls=%async_computation.1 | async-start | bytes 294912 | tf_op jit(solution)/shard_map/all_to_all | solution.py:241
  40.4 14.1 %all-to-all-done.1.total_ref = f32[4,72,128]{2,1,0:T(8,128)S(1)} async-done(((f32[4,72,128]{2,1,0:T(8,128)}), f32[4,72,128]{2,1,0:T(8,128)S(1)}, u32[]{:S(2)}, u32[]{:S(2)}) %all-to-all-start.1) | async-done | bytes 147488 | tf_op jit(solution)/shard_map/all_to_all | solution.py:241
  54.5 0.9 shard_map.96
  55.3 6.8 %all-to-all-start.2 = ((f32[16,64,128]{2,1,0:T(8,128)}), f32[16,64,128]{2,1,0:T(8,128)S(1)}, u32[]{:S(2)}, u32[]{:S(2)}) async-start(f32[16,64,128]{2,1,0:T(8,128)} %shard_map.96), calls=%async_computation.2 | async-start | bytes 1048576 | tf_op jit(solution)/shard_map/all_to_all | solution.py:241
  62.1 0.0 copy-done
  62.1 0.0 copy-done.1
  62.2 0.0 copy-start.3
  62.2 0.0 copy-start.5
  62.2 0.7 shard_map.93.inside_ref
  62.9 10.6 %all-to-all-done.2 = f32[16,64,128]{2,1,0:T(8,128)S(1)} async-done(((f32[16,64,128]{2,1,0:T(8,128)}), f32[16,64,128]{2,1,0:T(8,128)S(1)}, u32[]{:S(2)}, u32[]{:S(2)}) %all-to-all-start.2) | async-done | bytes 524320 | tf_op jit(solution)/shard_map/all_to_all | solution.py:241
  73.5 0.8 shard_map.97
  74.3 10.8 %all-gather.1.sums_ref = f32[8,2,128]{2,1,0:T(2,128)S(1)} all-gather(f32[1,2,128]{2,1,0:T(2,128)S(1)} %bitcast.17), channel_id=2, replica_groups=mesh['zh'=4,'zl'=4,'x'=4,'tp'=8] {'tp'}, dimensions={0}, use_global_device_ids=true | all-gather | bytes 9216 | tf_op jit(solution)/shard_map/all_gather | solution.py:288
  85.1 1.1 shard_map.98
  86.2 20.2 %all_to_all.31.piece_ref = f32[16,64,128]{2,1,0:T(8,128)S(1)} all-to-all(f32[16,64,128]{2,1,0:T(8,128)S(1)} %get-tuple-element.19), channel_id=1, replica_groups=mesh['zh'=4,'zl'=4,'x'=4,'tp'=8] {'zl','x'}, dimensions={0} | all-to-all | bytes 1048576 | tf_op jit(solution)/shard_map/all_to_all | solution.py:241
  106.4 0.1 shard_map.100
  106.5 20.0 %all_to_all.32.total_ref = f32[4,72,128]{2,1,0:T(8,128)S(1)} all-to-all(f32[4,72,128]{2,1,0:T(8,128)S(1)} %shard_map.100), channel_id=1, replica_groups=mesh['zh'=4,'zl'=4,'x'=4,'tp'=8] {'zh'}, dimensions={0} | all-to-all | bytes 294912 | tf_op jit(solution)/shard_map/all_to_all | solution.py:241
  126.5 0.9 shard_map.101
  127.4 4.4 %all-to-all-start.5 = ((f32[16,64,128]{2,1,0:T(8,128)}), f32[16,64,128]{2,1,0:T(8,128)S(1)}, u32[]{:S(2)}, u32[]{:S(2)}) async-start(f32[16,64,128]{2,1,0:T(8,128)} %shard_map.101), calls=%async_computation.5 | async-start | bytes 1048576 | tf_op jit(solution)/shard_map/all_to_all | solution.py:241
  131.8 3.2 %shard_map.99 = (bf16[128,1024]{1,0:T(8,128)(2,1)}, f32[8,128,128]{2,1,0:T(8,128)S(1)}, f32[128,1024]{1,0:T(8,128)S(1)}) custom-call(bf16[128,1024]{1,0:T(8,128)(2,1)S(1)} %copy-done, bf16[128,1024]{1,0:T(8,128)(2,1)S(1)} %copy-done.1, bf16[128,1024]{1,0:T(8,128)(2,1)S(1)} %copy-done.2, ...), custom_call_target="tpu_custom_call", output_to_operand_aliasing={{1}: (4, {}), {2}: (5, {})} | custom-call | flops 436207616 | bytes 3149824 | tf_op jit(solution)/shard_map/pallas_call | solution.py:211
  135.0 8.7 %all-to-all-done.5 = f32[16,64,128]{2,1,0:T(8,128)S(1)} async-done(((f32[16,64,128]{2,1,0:T(8,128)}), f32[16,64,128]{2,1,0:T(8,128)S(1)}, u32[]{:S(2)}, u32[]{:S(2)}) %all-to-all-start.5) | async-done | bytes 524320 | tf_op jit(solution)/shard_map/all_to_all | solution.py:241
  143.7 1.5 %shard_map.102 = (bf16[128,1024]{1,0:T(8,128)(2,1)}, bf16[128,1024]{1,0:T(8,128)(2,1)}) custom-call(bf16[128,1024]{1,0:T(8,128)(2,1)S(1)} %copy-done.1, bf16[128,1024]{1,0:T(8,128)(2,1)S(1)} %copy-done.2, f32[8,128]{1,0:T(8,128)S(1)} %bitcast.14, f32[8,128,128]{2,1,0:T(8,128)S(1)} %bitcast.8, f32[8,128,128]{2,1,0:T(8,128)S(1)} %get-tuple-element.20.near_k_ref, ...), custom_call_target="tpu_custom_call" | custom-call | flops 134217728 | bytes 2625536 | tf_op jit(solution)/shard_map/pallas_call | solution.py:211
  (9 shorter events, 0.0 us)
Async XLA Ops:
  28.0 26.4 %all-to-all-start.1 = ((f32[4,72,128]{2,1,0:T(8,128)}), f32[4,72,128]{2,1,0:T(8,128)S(1)}, u32[]{:S(2)}, u32[]{:S(2)}) async-start(f32[4,72,128]{2,1,0:T(8,128)} %shard_map.95), calls=%async_computation.1 | async-start | bytes 294912 | tf_op jit(solution)/shard_map/all_to_all | solution.py:241
  55.3 6.8 %copy-start = (bf16[128,1024]{1,0:T(8,128)(2,1)S(1)}, bf16[128,1024]{1,0:T(8,128)(2,1)}, u32[]{:S(2)}) copy-start(bf16[128,1024]{1,0:T(8,128)(2,1)} %query_ref.7) | copy-start | bytes 786436
  55.3 6.8 %copy-start.1 = (bf16[128,1024]{1,0:T(8,128)(2,1)S(1)}, bf16[128,1024]{1,0:T(8,128)(2,1)}, u32[]{:S(2)}) copy-start(bf16[128,1024]{1,0:T(8,128)(2,1)} %key_ref.5) | copy-start | bytes 786436
  55.3 6.8 %copy-start.2 = (bf16[128,1024]{1,0:T(8,128)(2,1)S(1)}, bf16[128,1024]{1,0:T(8,128)(2,1)}, u32[]{:S(2)}) copy-start(bf16[128,1024]{1,0:T(8,128)(2,1)} %value_ref.5) | copy-start | bytes 786436
  55.3 6.9 %copy-start.4 = (f32[128,8]{0,1:T(8,128)S(1)}, f32[128,8]{0,1:T(8,128)}, u32[]{:S(2)}) copy-start(f32[128,8]{0,1:T(8,128)} %param.9) | copy-start | bytes 12292
  55.3 18.2 %all-to-all-start.2 = ((f32[16,64,128]{2,1,0:T(8,128)}), f32[16,64,128]{2,1,0:T(8,128)S(1)}, u32[]{:S(2)}, u32[]{:S(2)}) async-start(f32[16,64,128]{2,1,0:T(8,128)} %shard_map.96), calls=%async_computation.2 | async-start | bytes 1048576 | tf_op jit(solution)/shard_map/all_to_all | solution.py:241
  62.2 11.4 %copy-start.3 = (bf16[128,1024]{1,0:T(8,128)(2,1)S(1)}, bf16[128,1024]{1,0:T(8,128)(2,1)}, u32[]{:S(2)}) copy-start(bf16[128,1024]{1,0:T(8,128)(2,1)} %grad_ref.3) | copy-start | bytes 786436
  62.2 11.4 %copy-start.5 = (f32[1024]{0:T(1024)S(1)}, f32[1024]{0:T(1024)}, u32[]{:S(2)}) copy-start(f32[1024]{0:T(1024)} %param.10) | copy-start | bytes 12292
  127.4 16.4 %all-to-all-start.5 = ((f32[16,64,128]{2,1,0:T(8,128)}), f32[16,64,128]{2,1,0:T(8,128)S(1)}, u32[]{:S(2)}, u32[]{:S(2)}) async-start(f32[16,64,128]{2,1,0:T(8,128)} %shard_map.101), calls=%async_computation.5 | async-start | bytes 1048576 | tf_op jit(solution)/shard_map/all_to_all | solution.py:241

commit v4 on v3

--- a/solution.py
+++ b/solution.py
@@ -5,7 +5,6 @@
 from jax import lax
 from jax.experimental import pallas as pl
 from jax.experimental.pallas import tpu as pltpu
-from jax.sharding import Mesh
 from jax.sharding import PartitionSpec as P
 
 epsilon = 1e-06
@@ -49,6 +48,15 @@
 def weights_of(tall, wide, mask, head):
     differences = tall[:, head : head + 1] - wide[head : head + 1, :]
     return jnp.where(mask, jnp.exp(jnp.where(mask, differences, 0.0)), 0.0)
+
+
+def group_here(heads):
+    return lax.div(lax.axis_index("ctx"), 2 * heads)
+
+
+def turned(head, heads):
+    half = lax.axis_size("ctx") // (2 * heads) // 2
+    return (head + jnp.where(group_here(heads) < half, 0, heads // 2)) & (heads - 1)
 
 
 def cols(head, size):
@@ -77,9 +85,10 @@
         key = key_ref[:, cols(head, size)].astype(f32) * trailing[:, head : head + 1]
         state = product(key, value_ref[:, cols(head, size)], TN)
         mark = jnp.broadcast_to(total[:, head : head + 1], (8, size))
+        first = turned(head, heads) * per
         for part in range(per):
-            out_ref[head * per + part, :rows, :] = state[part * rows : (part + 1) * rows, :]
-            out_ref[head * per + part, rows:, :] = mark
+            out_ref[first + part, :rows, :] = state[part * rows : (part + 1) * rows, :]
+            out_ref[first + part, rows:, :] = mark
 
 
 def times(gain, state):
@@ -100,8 +109,8 @@
         out_ref[copy, rows:, :] = whole
 
 
-def spread_kernel(members, groups, backward, rows, mine_ref, piece_ref, decay_ref, total_ref, out_ref):
-    mine = mine_ref[0]
+def spread_kernel(members, groups, backward, rows, piece_ref, decay_ref, total_ref, out_ref):
+    mine = group_here(members // 2)
     running = jnp.zeros((rows, piece_ref.shape[-1]), f32)
     for group in reversed(range(groups)) if backward else range(groups):
         longer = times(jnp.exp(total_ref[group, rows:, :]), running) + total_ref[group, :rows, :]
@@ -131,7 +140,7 @@
     products = jnp.zeros((rows, size), f32)
     for head in range(heads):
         here = cols(head, size)
-        outside = product(query_ref[:, here], state_ref[head], NN)
+        outside = product(query_ref[:, here], state_ref[turned(head, heads)], NN)
         mixed = inside_ref[:, here] + outside * rising[:, head : head + 1]
         out_ref[:, here] = mixed
         squares = squares + mixed * mixed
@@ -164,8 +173,9 @@
         slope = scale * (grad_ref[:, here].astype(f32) * gain) - pull * mixed
         slope_ref[:, here] = slope
         state = product(query_ref[:, here], slope * rising[:, head : head + 1], TN)
+        first = turned(head, heads) * per
         for part in range(per):
-            out_ref[head * per + part] = state[part * cut : (part + 1) * cut, :]
+            out_ref[first + part] = state[part * cut : (part + 1) * cut, :]
 
 
 def near_kernel(
@@ -181,9 +191,10 @@
         weights = weights_of(tall, wide, mask, head)
         scores = product(query, key, NT) * weights
         grad_scores = product(slope, value, NT) * weights
-        outer = product(slope, state_ref[head], NT) * rising[:, head : head + 1]
+        there = turned(head, heads)
+        outer = product(slope, state_ref[there], NT) * rising[:, head : head + 1]
         grad_q_ref[:, here] = (product(grad_scores, key, NN) + outer).astype(bf16)
-        near_k_ref[head] = product(grad_scores, query, TN)
+        near_k_ref[there] = product(grad_scores, query, TN)
         near_v_ref[:, here] = product(scores, slope, TN)
 
 
@@ -194,24 +205,24 @@
     for head in range(heads):
         here = cols(head, size)
         late = trailing[:, head : head + 1]
-        state = state_ref[head]
-        grad_k = near_k_ref[head] + product(value_ref[:, here], state, NT) * late
+        there = turned(head, heads)
+        state = state_ref[there]
+        grad_k = near_k_ref[there] + product(value_ref[:, here], state, NT) * late
         grad_v = near_v_ref[:, here] + product(key_ref[:, here], state, NN) * late
         grad_k_ref[:, here] = grad_k.astype(bf16)
         grad_v_ref[:, here] = grad_v.astype(bf16)
 
 
-def call(kernel, outs, *args, scalars=0, flops=0, copied=(), aliases=None):
+def call(kernel, outs, *args, flops=0, copied=(), aliases=None):
     vmem = pl.BlockSpec(memory_space=pltpu.VMEM)
     hbm = pl.BlockSpec(memory_space=pltpu.HBM)
-    smem = pl.BlockSpec(memory_space=pltpu.SMEM)
     if copied:
         args = [pltpu.with_memory_space_constraint(a, pltpu.HBM) for a in args]
     moved = sum(a.size * a.dtype.itemsize for a in (*args, *outs))
     return pl.pallas_call(
         kernel,
         out_shape=outs,
-        in_specs=[smem] * scalars + [hbm if copied else vmem] * (len(args) - scalars),
+        in_specs=[hbm if copied else vmem] * len(args),
         out_specs=[vmem] * len(outs),
         input_output_aliases=aliases or {},
         scratch_shapes=[pltpu.VMEM(a.shape, a.dtype) for a in copied]
@@ -221,24 +232,36 @@
     )(*args)
 
 
-def shards(groups, tp, queries, key_rows, value_rows, log_decay, norm_gain, grad_output):
-    near, far = ("zl", "x"), "zh"
-    members = lax.axis_size(near)
+def levels(count, heads):
+    members = 2 * heads
+    groups = count // members
+    near = [[group * members + member for member in range(members)] for group in range(groups)]
+    far = [
+        [
+            group * members + (piece + (members // 2 if group >= groups // 2 else 0)) % members
+            for group in range(groups)
+        ]
+        for piece in range(members)
+    ]
+    return groups, members, near, far
+
+
+def shards(queries, key_rows, value_rows, log_decay, norm_gain, grad_output):
     tok_rows, feat_width = queries.shape
     heads = log_decay.shape[1]
+    groups, members, near, far = levels(lax.axis_size("ctx"), heads)
     size = feat_width // heads
     rows = heads * size // members
     wide = jax.ShapeDtypeStruct((tok_rows, feat_width), f32)
     narrow = jax.ShapeDtypeStruct((tok_rows, feat_width), bf16)
     gain = norm_gain.reshape(1, feat_width)
     log_decay = log_decay.T
-    mine = lax.axis_index(far).astype(jnp.int32).reshape(1)
     bind = functools.partial
     shape = jax.ShapeDtypeStruct
     unit = 2 * heads * tok_rows * size * size
 
-    def exchange(parts, axis):
-        return lax.all_to_all(parts, axis, 0, 0)
+    def exchange(parts, lists):
+        return lax.all_to_all(parts, "ctx", 0, 0, axis_index_groups=lists)
 
     def carried(pieces, marks, backward):
         (total,) = call(
@@ -251,12 +274,10 @@
         (entering,) = call(
             bind(spread_kernel, members, groups, backward, rows),
             [shape((members, rows, size), f32)],
-            mine,
-            pieces,
+                pieces,
             marks,
             totals,
-            scalars=1,
-        )
+            )
         return exchange(entering, near).reshape(heads, size, size)
 
     (states,) = call(
@@ -285,9 +306,9 @@
         grad_output,
         flops=2 * unit,
     )
-    gathered = lax.all_gather(sums, tp)
+    gathered = lax.all_gather(sums, "tp")
     normed, slope, back = call(
-        bind(norm_kernel, heads, members, feat_width * lax.axis_size(tp)),
+        bind(norm_kernel, heads, members, feat_width * lax.axis_size("tp")),
         [narrow, wide, shape((members, rows, size), f32)],
         queries,
         log_decay,
@@ -326,12 +347,10 @@
 
 
 def solution(mesh):
-    groups = 4
-    folded = Mesh(mesh.devices.reshape(groups, 4, 4, -1), ("zh", "zl", "x", "tp"))
-    both = P(("zh", "zl", "x"), "tp")
+    both = P("ctx", "tp")
     return jax.shard_map(
-        functools.partial(shards, groups, "tp"),
-        mesh=folded,
+        shards,
+        mesh=mesh,
         in_specs=(both, both, both, both, P("tp"), both),
         out_specs=(both, both, both, both),
         check_vma=False,

time: 146 us -> 144 us (0.986)
  blocking collectives: 75.9 us -> 99.2 us
  starting transfers between devices: 23.6 us -> 9.56 us
  waiting for transfers between devices: 33.4 us -> 22.6 us
    all_to_all x3 -> x4, blocking collectives: 65.1 us -> 88.4 us  [exchange(): return lax.all_to_all(parts, 'ctx', 0, 0, axis_index_groups=lists)]
    all_to_all x3 -> x2, starting transfers between devices: 23.6 us -> 9.56 us  [exchange(): return lax.all_to_all(parts, 'ctx', 0, 0, axis_index_groups=lists)]
    all_to_all x3 -> x2, waiting for transfers between devices: 33.4 us -> 22.6 us  [exchange(): return lax.all_to_all(parts, 'ctx', 0, 0, axis_index_groups=lists)]
  transfers between devices with their start and end apart: 3 -> 2, of which waited for: 3 -> 2; matrix products, arithmetic and copies ran while one was open for 0% -> 0% of each run, Pallas kernels for 3% -> 3%
where the time goes in v4:
time: 144 us; the launch traced here: 143 us
  blocking collectives  99.2 us (69%)
  waiting for transfers between devices  22.6 us (16%)
  Pallas kernels  11.1 us (8%)
  starting transfers between devices  9.56 us (7%)
    all_to_all x4, blocking collectives, exchange(): return lax.all_to_all(parts, 'ctx', 0, 0, axis_index_groups=lists)  88.4 us
    all_to_all x2, waiting for transfers between devices, exchange(): return lax.all_to_all(parts, 'ctx', 0, 0, axis_index_groups=lists)  22.6 us
    pallas_call x10, Pallas kernels, call(): pl.pallas_call(kernel, out_shape=outs, in_specs=[hbm if copied else vmem]...  11.1 us
    all_gather x1, blocking collectives, shards(): gathered = lax.all_gather(sums, 'tp')  10.8 us
    all_to_all x2, starting transfers between devices, exchange(): return lax.all_to_all(parts, 'ctx', 0, 0, axis_index_groups=lists)  9.56 us
  transfers between devices with their start and end apart: 2, of which 2 were waited for; matrix products, arithmetic and copies ran while one was open for 0% of the time, Pallas kernels for 3%

profile of v4, /device:TPU:32, one launch (start us, length us, event | category | flops | bytes accessed | tf_op | source)
XLA Modules:
  0.0 143.2 jit_solution(368321872213007304)
XLA Ops:
  0.6 1.8 %shard_map.94 = f32[16,72,128]{2,1,0:T(8,128)S(1)} custom-call(bf16[128,1024]{1,0:T(8,128)(2,1)} %key_ref.5, bf16[128,1024]{1,0:T(8,128)(2,1)} %value_ref.5, f32[8,128]{1,0:T(8,128)} %bitcast.8), custom_call_target="tpu_custom_call" | custom-call | flops 67108864 | bytes 1118208 | tf_op jit(solution)/shard_map/pallas_call | solution.py:222
  2.4 24.9 %all_to_all.30.piece_ref = f32[16,72,128]{2,1,0:T(8,128)S(1)} all-to-all(f32[16,72,128]{2,1,0:T(8,128)S(1)} %shard_map.94), channel_id=1, replica_groups={{0,8,16,24,32,40,48,56,64,72,80,88,96,104,112,120},{128,136,144,152,160..., dimensions={0} | all-to-all | bytes 1179648 | tf_op jit(solution)/shard_map/all_to_all | solution.py:264
  27.3 0.1 shard_map.95
  27.4 25.4 %all_to_all.31.total_ref = f32[4,72,128]{2,1,0:T(8,128)S(1)} all-to-all(f32[4,72,128]{2,1,0:T(8,128)S(1)} %shard_map.95), channel_id=1, replica_groups={{0,128,320,448},{8,136,328,456},{16,144,336,464},{24,152,344,472},{32,1..., dimensions={0} | all-to-all | bytes 294912 | tf_op jit(solution)/shard_map/all_to_all | solution.py:264
  52.7 0.9 shard_map.96
  53.6 4.9 %all-to-all-start.2 = ((f32[16,64,128]{2,1,0:T(8,128)}), f32[16,64,128]{2,1,0:T(8,128)S(1)}, u32[]{:S(2)}, u32[]{:S(2)}) async-start(f32[16,64,128]{2,1,0:T(8,128)} %shard_map.96), calls=%async_computation.2 | async-start | bytes 1048576 | tf_op jit(solution)/shard_map/all_to_all | solution.py:264
  58.5 0.0 copy-done
  58.5 0.0 copy-done.1
  58.5 0.0 copy-start.3
  58.5 0.0 copy-start.5
  58.5 0.7 shard_map.93.inside_ref
  59.2 13.4 %all-to-all-done.2 = f32[16,64,128]{2,1,0:T(8,128)S(1)} async-done(((f32[16,64,128]{2,1,0:T(8,128)}), f32[16,64,128]{2,1,0:T(8,128)S(1)}, u32[]{:S(2)}, u32[]{:S(2)}) %all-to-all-start.2) | async-done | bytes 524320 | tf_op jit(solution)/shard_map/all_to_all | solution.py:264
  72.6 0.0 copy-done.5
  72.6 0.8 shard_map.97
  73.4 10.8 %all-gather.1.sums_ref = f32[8,2,128]{2,1,0:T(2,128)S(1)} all-gather(f32[1,2,128]{2,1,0:T(2,128)S(1)} %bitcast.16), channel_id=2, replica_groups=mesh['ctx'=64,'tp'=8] {'tp'}, dimensions={0}, use_global_device_ids=true | all-gather | bytes 9216 | tf_op jit(solution)/shard_map/all_gather | solution.py:309
  84.2 1.3 shard_map.98
  85.6 20.2 %all_to_all.32.piece_ref = f32[16,64,128]{2,1,0:T(8,128)S(1)} all-to-all(f32[16,64,128]{2,1,0:T(8,128)S(1)} %get-tuple-element.19), channel_id=1, replica_groups={{0,8,16,24,32,40,48,56,64,72,80,88,96,104,112,120},{128,136,144,152,160..., dimensions={0} | all-to-all | bytes 1048576 | tf_op jit(solution)/shard_map/all_to_all | solution.py:264
  105.7 0.1 shard_map.100
  105.8 17.9 %all_to_all.33.total_ref = f32[4,72,128]{2,1,0:T(8,128)S(1)} all-to-all(f32[4,72,128]{2,1,0:T(8,128)S(1)} %shard_map.100), channel_id=1, replica_groups={{0,128,320,448},{8,136,328,456},{16,144,336,464},{24,152,344,472},{32,1..., dimensions={0} | all-to-all | bytes 294912 | tf_op jit(solution)/shard_map/all_to_all | solution.py:264
  123.8 0.9 shard_map.101
  124.6 4.7 %all-to-all-start.5 = ((f32[16,64,128]{2,1,0:T(8,128)}), f32[16,64,128]{2,1,0:T(8,128)S(1)}, u32[]{:S(2)}, u32[]{:S(2)}) async-start(f32[16,64,128]{2,1,0:T(8,128)} %shard_map.101), calls=%async_computation.5 | async-start | bytes 1048576 | tf_op jit(solution)/shard_map/all_to_all | solution.py:264
  129.3 3.2 %shard_map.99 = (bf16[128,1024]{1,0:T(8,128)(2,1)}, f32[8,128,128]{2,1,0:T(8,128)S(1)}, f32[128,1024]{1,0:T(8,128)S(1)}) custom-call(bf16[128,1024]{1,0:T(8,128)(2,1)S(1)} %copy-done, bf16[128,1024]{1,0:T(8,128)(2,1)S(1)} %copy-done.1, bf16[128,1024]{1,0:T(8,128)(2,1)S(1)} %copy-done.2, ...), custom_call_target="tpu_custom_call", output_to_operand_aliasing={{1}: (4, {}), {2}: (5, {})} | custom-call | flops 436207616 | bytes 3149824 | tf_op jit(solution)/shard_map/pallas_call | solution.py:222
  132.5 9.2 %all-to-all-done.5 = f32[16,64,128]{2,1,0:T(8,128)S(1)} async-done(((f32[16,64,128]{2,1,0:T(8,128)}), f32[16,64,128]{2,1,0:T(8,128)S(1)}, u32[]{:S(2)}, u32[]{:S(2)}) %all-to-all-start.5) | async-done | bytes 524320 | tf_op jit(solution)/shard_map/all_to_all | solution.py:264
  141.8 1.4 shard_map.102
  (8 shorter events, 0.0 us)
Async XLA Ops:
  53.6 4.9 %copy-start = (bf16[128,1024]{1,0:T(8,128)(2,1)S(1)}, bf16[128,1024]{1,0:T(8,128)(2,1)}, u32[]{:S(2)}) copy-start(bf16[128,1024]{1,0:T(8,128)(2,1)} %query_ref.7) | copy-start | bytes 786436
  53.6 4.9 %copy-start.1 = (bf16[128,1024]{1,0:T(8,128)(2,1)S(1)}, bf16[128,1024]{1,0:T(8,128)(2,1)}, u32[]{:S(2)}) copy-start(bf16[128,1024]{1,0:T(8,128)(2,1)} %key_ref.5) | copy-start | bytes 786436
  53.6 4.9 %copy-start.2 = (bf16[128,1024]{1,0:T(8,128)(2,1)S(1)}, bf16[128,1024]{1,0:T(8,128)(2,1)}, u32[]{:S(2)}) copy-start(bf16[128,1024]{1,0:T(8,128)(2,1)} %value_ref.5) | copy-start | bytes 786436
  53.6 4.9 %copy-start.4 = (f32[128,8]{0,1:T(8,128)S(1)}, f32[128,8]{0,1:T(8,128)}, u32[]{:S(2)}) copy-start(f32[128,8]{0,1:T(8,128)} %param.9) | copy-start | bytes 12292
  53.6 19.0 %all-to-all-start.2 = ((f32[16,64,128]{2,1,0:T(8,128)}), f32[16,64,128]{2,1,0:T(8,128)S(1)}, u32[]{:S(2)}, u32[]{:S(2)}) async-start(f32[16,64,128]{2,1,0:T(8,128)} %shard_map.96), calls=%async_computation.2 | async-start | bytes 1048576 | tf_op jit(solution)/shard_map/all_to_all | solution.py:264
  58.5 14.1 %copy-start.3 = (bf16[128,1024]{1,0:T(8,128)(2,1)S(1)}, bf16[128,1024]{1,0:T(8,128)(2,1)}, u32[]{:S(2)}) copy-start(bf16[128,1024]{1,0:T(8,128)(2,1)} %grad_ref.3) | copy-start | bytes 786436
  58.5 14.1 %copy-start.5 = (f32[1024]{0:T(1024)S(1)}, f32[1024]{0:T(1024)}, u32[]{:S(2)}) copy-start(f32[1024]{0:T(1024)} %param.10) | copy-start | bytes 12292
  124.6 17.1 %all-to-all-start.5 = ((f32[16,64,128]{2,1,0:T(8,128)}), f32[16,64,128]{2,1,0:T(8,128)S(1)}, u32[]{:S(2)}, u32[]{:S(2)}) async-start(f32[16,64,128]{2,1,0:T(8,128)} %shard_map.101), calls=%async_computation.5 | async-start | bytes 1048576 | tf_op jit(solution)/shard_map/all_to_all | solution.py:264

commit v5 on v4

--- a/solution.py
+++ b/solution.py
@@ -54,41 +54,50 @@
     return lax.div(lax.axis_index("ctx"), 2 * heads)
 
 
+def rank(place):
+    return place % 4 * 4 + place // 4
+
+
 def turned(head, heads):
     half = lax.axis_size("ctx") // (2 * heads) // 2
-    return (head + jnp.where(group_here(heads) < half, 0, heads // 2)) & (heads - 1)
+    return head ^ jnp.where(group_here(heads) < half, 0, 1)
 
 
 def cols(head, size):
     return slice(head * size, (head + 1) * size)
 
 
-def states_kernel(heads, members, key_far, value_far, decay_far, out_ref, key_ref, value_ref, decay_ref, sems):
+def states_kernel(
+    heads, members, query_far, key_far, value_far, decay_far, out_ref, inside_ref, query_ref, key_ref, value_ref, decay_ref, sems
+):
     size = key_ref.shape[1] // heads
     per = members // heads
     rows = size // per
     copies = [
         pltpu.make_async_copy(source, target, sems.at[i])
         for i, (source, target) in enumerate(
-            ((decay_far, decay_ref), (key_far, key_ref), (value_far, value_ref))
+            ((decay_far, decay_ref), (key_far, key_ref), (value_far, value_ref), (query_far, query_ref))
         )
     ]
     for copy in copies:
         copy.start()
     copies[0].wait()
-    tall, _, _ = decays(decay_ref[...])
+    tall, wide, mask = decays(decay_ref[...])
     total = tall[-1:, :]
     trailing = jnp.exp(total - tall)
-    copies[1].wait()
-    copies[2].wait()
-    for head in range(heads):
-        key = key_ref[:, cols(head, size)].astype(f32) * trailing[:, head : head + 1]
-        state = product(key, value_ref[:, cols(head, size)], TN)
+    for copy in copies[1:]:
+        copy.wait()
+    for head in range(heads):
+        here = cols(head, size)
+        key, value = key_ref[:, here], value_ref[:, here]
+        state = product(key.astype(f32) * trailing[:, head : head + 1], value, TN)
         mark = jnp.broadcast_to(total[:, head : head + 1], (8, size))
         first = turned(head, heads) * per
         for part in range(per):
             out_ref[first + part, :rows, :] = state[part * rows : (part + 1) * rows, :]
             out_ref[first + part, rows:, :] = mark
+        scores = product(query_ref[:, here], key, NT) * weights_of(tall, wide, mask, head)
+        inside_ref[:, here] = product(scores, value, NN)
 
 
 def times(gain, state):
@@ -100,8 +109,8 @@
     order = reversed(range(members)) if backward else range(members)
     whole = jnp.zeros(decay_ref.shape[1:], f32)
     for member in order:
-        mark = decay_ref[member]
-        state = piece_ref[member, :rows, :]
+        mark = decay_ref[rank(member)]
+        state = piece_ref[rank(member), :rows, :]
         total = state if total is None else times(jnp.exp(mark), total) + state
         whole = whole + mark
     for copy in range(copies):
@@ -116,17 +125,9 @@
         longer = times(jnp.exp(total_ref[group, rows:, :]), running) + total_ref[group, :rows, :]
         running = jnp.where(group > mine if backward else group < mine, longer, running)
     for member in reversed(range(members)) if backward else range(members):
-        out_ref[member] = running
-        running = times(jnp.exp(decay_ref[member]), running) + piece_ref[member, :rows, :]
-
-
-def inside_kernel(heads, query_ref, key_ref, value_ref, decay_ref, out_ref):
-    size = key_ref.shape[1] // heads
-    tall, wide, mask = decays(decay_ref[...])
-    for head in range(heads):
-        here = cols(head, size)
-        scores = product(query_ref[:, here], key_ref[:, here], NT) * weights_of(tall, wide, mask, head)
-        out_ref[:, here] = product(scores, value_ref[:, here], NN)
+        place = rank(member)
+        out_ref[place] = running
+        running = times(jnp.exp(decay_ref[place]), running) + piece_ref[place, :rows, :]
 
 
 def mixed_kernel(
@@ -148,8 +149,9 @@
     ones = jnp.ones((8, size), f32)
     square = lax.dot_general(ones, squares, NT, precision=highest, preferred_element_type=f32)
     product_ = lax.dot_general(ones, products, NT, precision=highest, preferred_element_type=f32)
-    sums_ref[0:1, :] = square[0:1, :]
-    sums_ref[1:2, :] = product_[0:1, :]
+    for copy in range(sums_ref.shape[0]):
+        sums_ref[copy, 0:1, :] = square[0:1, :]
+        sums_ref[copy, 1:2, :] = product_[0:1, :]
 
 
 def norm_kernel(
@@ -235,12 +237,9 @@
 def levels(count, heads):
     members = 2 * heads
     groups = count // members
-    near = [[group * members + member for member in range(members)] for group in range(groups)]
+    near = [[group * members + rank(i) for i in range(members)] for group in range(groups)]
     far = [
-        [
-            group * members + (piece + (members // 2 if group >= groups // 2 else 0)) % members
-            for group in range(groups)
-        ]
+        [group * members + rank(piece ^ (2 if group >= groups // 2 else 0)) for group in range(groups)]
         for piece in range(members)
     ]
     return groups, members, near, far
@@ -280,24 +279,22 @@
             )
         return exchange(entering, near).reshape(heads, size, size)
 
-    (states,) = call(
+    states, inside = call(
         bind(states_kernel, heads, members),
-        [shape((members, rows + 8, size), f32)],
+        [shape((members, rows + 8, size), f32), wide],
+        queries,
         key_rows,
         value_rows,
         log_decay,
-        flops=2 * unit,
-        copied=(key_rows, value_rows, log_decay),
+        flops=5 * unit,
+        copied=(queries, key_rows, value_rows, log_decay),
     )
     pieces = exchange(states, near)
     marks = pieces[:, rows:, :]
-    (inside,) = call(
-        bind(inside_kernel, heads), [wide], queries, key_rows, value_rows, log_decay, flops=3 * unit
-    )
     entry = carried(pieces, marks, False)
     mixed, sums = call(
         bind(mixed_kernel, heads),
-        [wide, shape((2, tok_rows), f32)],
+        [wide, shape((lax.axis_size("tp"), 2, tok_rows), f32)],
         queries,
         log_decay,
         inside,
@@ -306,7 +303,7 @@
         grad_output,
         flops=2 * unit,
     )
-    gathered = lax.all_gather(sums, "tp")
+    gathered = lax.all_to_all(sums, "tp", 0, 0)
     normed, slope, back = call(
         bind(norm_kernel, heads, members, feat_width * lax.axis_size("tp")),
         [narrow, wide, shape((members, rows, size), f32)],

time: 144 us -> 142 us (0.986)
  the two profiles are of different devices: /device:TPU:32 before, /device:TPU:8 now
where the time goes in v5:
time: 142 us; the launch traced here: 141 us
  blocking collectives  115 us (81%)
  Pallas kernels  10.7 us (8%)
  waiting for transfers between devices  9.24 us (7%)
  starting transfers between devices  5.06 us (4%)
    all_to_all x5, blocking collectives, exchange(): return lax.all_to_all(parts, 'ctx', 0, 0, axis_index_groups=lists)  106 us
    pallas_call x9, Pallas kernels, call(): pl.pallas_call(kernel, out_shape=outs, in_specs=[hbm if copied else vmem]...  10.7 us
    all_to_all x1, waiting for transfers between devices, exchange(): return lax.all_to_all(parts, 'ctx', 0, 0, axis_index_groups=lists)  9.24 us
    all_to_all x1, blocking collectives, shards(): gathered = lax.all_to_all(sums, 'tp', 0, 0)  8.58 us
    all_to_all x1, starting transfers between devices, exchange(): return lax.all_to_all(parts, 'ctx', 0, 0, axis_index_groups=lists)  5.06 us
  transfers between devices with their start and end apart: 1, of which 1 were waited for; matrix products, arithmetic and copies ran while one was open for 0% of the time, Pallas kernels for 2%

profile of v5, /device:TPU:8, one launch (start us, length us, event | category | flops | bytes accessed | tf_op | source)
XLA Modules:
  0.0 141.5 jit_solution(14476426372863231359)
XLA Ops:
  0.6 2.8 %shard_map.93 = (f32[16,72,128]{2,1,0:T(8,128)S(1)}, f32[128,1024]{1,0:T(8,128)S(1)}) custom-call(bf16[128,1024]{1,0:T(8,128)(2,1)} %query_ref.5, bf16[128,1024]{1,0:T(8,128)(2,1)} %key_ref.3, bf16[128,1024]{1,0:T(8,128)(2,1)} %value_ref.3, f32[8,128]{1,0:T(8,128)} %bitcast.7), custom_call_target="tpu_custom_call" | custom-call | flops 167772160 | bytes 1904640 | tf_op jit(solution)/shard_map/pallas_call | solution.py:224
  3.4 26.2 %all_to_all.35.piece_ref = f32[16,72,128]{2,1,0:T(8,128)S(1)} all-to-all(f32[16,72,128]{2,1,0:T(8,128)S(1)} %get-tuple-element.17), channel_id=1, replica_groups={{0,32,64,96,8,40,72,104,16,48,80,112,24,56,88,120},{128,160,192,224,136..., dimensions={0} | all-to-all | bytes 1179648 | tf_op jit(solution)/shard_map/all_to_all | solution.py:263
  29.6 0.1 shard_map.94
  29.7 24.0 %all_to_all.36.total_ref = f32[4,72,128]{2,1,0:T(8,128)S(1)} all-to-all(f32[4,72,128]{2,1,0:T(8,128)S(1)} %shard_map.94), channel_id=1, replica_groups={{0,128,320,448},{32,160,352,480},{64,192,256,384},{96,224,288,416},{8,1..., dimensions={0} | all-to-all | bytes 294912 | tf_op jit(solution)/shard_map/all_to_all | solution.py:263
  53.6 0.1 shard_map.95
  53.7 0.0 copy-start
  53.7 0.0 copy-start.3
  53.7 0.0 copy-start.5
  53.7 20.6 %all_to_all.37 = f32[16,64,128]{2,1,0:T(8,128)S(1)} all-to-all(f32[16,64,128]{2,1,0:T(8,128)S(1)} %shard_map.95), channel_id=1, replica_groups={{0,32,64,96,8,40,72,104,16,48,80,112,24,56,88,120},{128,160,192,224,136..., dimensions={0} | all-to-all | bytes 1048576 | tf_op jit(solution)/shard_map/all_to_all | solution.py:263
  74.4 0.0 copy-done
  74.4 0.0 copy-done.5
  74.4 0.7 copy-done.4
  75.1 0.8 shard_map.96
  75.8 8.6 %all_to_all.38.sums_ref = f32[8,2,128]{2,1,0:T(2,128)S(1)} all-to-all(f32[8,2,128]{2,1,0:T(2,128)S(1)} %get-tuple-element.19), channel_id=1, replica_groups=mesh['ctx'=64,'tp'=8] {'tp'}, dimensions={0} | all-to-all | bytes 16384 | tf_op jit(solution)/shard_map/all_to_all | solution.py:306
  84.4 1.3 shard_map.97
  85.7 19.4 %all_to_all.39.piece_ref = f32[16,64,128]{2,1,0:T(8,128)S(1)} all-to-all(f32[16,64,128]{2,1,0:T(8,128)S(1)} %get-tuple-element.23), channel_id=1, replica_groups={{0,32,64,96,8,40,72,104,16,48,80,112,24,56,88,120},{128,160,192,224,136..., dimensions={0} | all-to-all | bytes 1048576 | tf_op jit(solution)/shard_map/all_to_all | solution.py:263
  105.1 0.1 shard_map.99
  105.2 16.3 %all_to_all.40.total_ref = f32[4,72,128]{2,1,0:T(8,128)S(1)} all-to-all(f32[4,72,128]{2,1,0:T(8,128)S(1)} %shard_map.99), channel_id=1, replica_groups={{0,128,320,448},{32,160,352,480},{64,192,256,384},{96,224,288,416},{8,1..., dimensions={0} | all-to-all | bytes 294912 | tf_op jit(solution)/shard_map/all_to_all | solution.py:263
  121.5 0.9 shard_map.100
  122.3 5.1 %all-to-all-start.6 = ((f32[16,64,128]{2,1,0:T(8,128)}), f32[16,64,128]{2,1,0:T(8,128)S(1)}, u32[]{:S(2)}, u32[]{:S(2)}) async-start(f32[16,64,128]{2,1,0:T(8,128)} %shard_map.100), calls=%async_computation.6 | async-start | bytes 1048576 | tf_op jit(solution)/shard_map/all_to_all | solution.py:263
  127.4 0.0 copy-done.1
  127.4 3.4 %shard_map.98 = (bf16[128,1024]{1,0:T(8,128)(2,1)}, f32[8,128,128]{2,1,0:T(8,128)S(1)}, f32[128,1024]{1,0:T(8,128)S(1)}) custom-call(bf16[128,1024]{1,0:T(8,128)(2,1)S(1)} %copy-done, bf16[128,1024]{1,0:T(8,128)(2,1)S(1)} %copy-done.1, bf16[128,1024]{1,0:T(8,128)(2,1)S(1)} %copy-done.2, ...), custom_call_target="tpu_custom_call", output_to_operand_aliasing={{1}: (4, {}), {2}: (5, {})} | custom-call | flops 436207616 | bytes 3149824 | tf_op jit(solution)/shard_map/pallas_call | solution.py:224
  130.8 9.2 %all-to-all-done.6 = f32[16,64,128]{2,1,0:T(8,128)S(1)} async-done(((f32[16,64,128]{2,1,0:T(8,128)}), f32[16,64,128]{2,1,0:T(8,128)S(1)}, u32[]{:S(2)}, u32[]{:S(2)}) %all-to-all-start.6) | async-done | bytes 524320 | tf_op jit(solution)/shard_map/all_to_all | solution.py:263
  140.0 1.4 %shard_map.101 = (bf16[128,1024]{1,0:T(8,128)(2,1)}, bf16[128,1024]{1,0:T(8,128)(2,1)}) custom-call(bf16[128,1024]{1,0:T(8,128)(2,1)S(1)} %copy-done.1, bf16[128,1024]{1,0:T(8,128)(2,1)S(1)} %copy-done.2, f32[8,128]{1,0:T(8,128)S(1)} %bitcast.11, f32[8,128,128]{2,1,0:T(8,128)S(1)} %bitcast.6, f32[8,128,128]{2,1,0:T(8,128)S(1)} %get-tuple-element.24.near_k_ref, ...), custom_call_target="tpu_custom_call" | custom-call | flops 134217728 | bytes 2625536 | tf_op jit(solution)/shard_map/pallas_call | solution.py:224
  (6 shorter events, 0.0 us)
Async XLA Ops:
  53.7 20.7 %copy-start = (bf16[128,1024]{1,0:T(8,128)(2,1)S(1)}, bf16[128,1024]{1,0:T(8,128)(2,1)}, u32[]{:S(2)}) copy-start(bf16[128,1024]{1,0:T(8,128)(2,1)} %query_ref.5) | copy-start | bytes 786436
  53.7 20.7 %copy-start.3 = (bf16[128,1024]{1,0:T(8,128)(2,1)S(1)}, bf16[128,1024]{1,0:T(8,128)(2,1)}, u32[]{:S(2)}) copy-start(bf16[128,1024]{1,0:T(8,128)(2,1)} %grad_ref.3) | copy-start | bytes 786436
  53.7 20.7 %copy-start.5 = (f32[1024]{0:T(1024)S(1)}, f32[1024]{0:T(1024)}, u32[]{:S(2)}) copy-start(f32[1024]{0:T(1024)} %param.10) | copy-start | bytes 12292
  74.4 0.7 copy-start.4
  122.3 5.1 %copy-start.1 = (bf16[128,1024]{1,0:T(8,128)(2,1)S(1)}, bf16[128,1024]{1,0:T(8,128)(2,1)}, u32[]{:S(2)}) copy-start(bf16[128,1024]{1,0:T(8,128)(2,1)} %key_ref.3) | copy-start | bytes 786436
  122.3 5.1 %copy-start.2 = (bf16[128,1024]{1,0:T(8,128)(2,1)S(1)}, bf16[128,1024]{1,0:T(8,128)(2,1)}, u32[]{:S(2)}) copy-start(bf16[128,1024]{1,0:T(8,128)(2,1)} %value_ref.3) | copy-start | bytes 786436
  122.3 17.7 %all-to-all-start.6 = ((f32[16,64,128]{2,1,0:T(8,128)}), f32[16,64,128]{2,1,0:T(8,128)S(1)}, u32[]{:S(2)}, u32[]{:S(2)}) async-start(f32[16,64,128]{2,1,0:T(8,128)} %shard_map.100), calls=%async_computation.6 | async-start | bytes 1048576 | tf_op jit(solution)/shard_map/all_to_all | solution.py:263

commit v6 on v5

--- a/solution.py
+++ b/solution.py
@@ -42,10 +42,14 @@
     lower = (above >= along).astype(f32)
     tall = lax.dot_general(lower, log_decay, NT, precision=highest, preferred_element_type=f32)
     wide = lax.dot_general(log_decay, upper, NN, precision=highest, preferred_element_type=f32)
-    return tall, wide, above >= along
-
-
-def weights_of(tall, wide, mask, head):
+    return tall, wide
+
+
+def weights_of(tall, wide, head):
+    rows = tall.shape[0]
+    above = lax.broadcasted_iota(jnp.int32, (rows, rows), 0)
+    along = lax.broadcasted_iota(jnp.int32, (rows, rows), 1)
+    mask = above >= along
     differences = tall[:, head : head + 1] - wide[head : head + 1, :]
     return jnp.where(mask, jnp.exp(jnp.where(mask, differences, 0.0)), 0.0)
 
@@ -68,7 +72,7 @@
 
 
 def states_kernel(
-    heads, members, query_far, key_far, value_far, decay_far, out_ref, inside_ref, query_ref, key_ref, value_ref, decay_ref, sems
+    heads, members, key_far, value_far, decay_far, out_ref, tall_ref, wide_ref, key_ref, value_ref, decay_ref, sems
 ):
     size = key_ref.shape[1] // heads
     per = members // heads
@@ -76,17 +80,19 @@
     copies = [
         pltpu.make_async_copy(source, target, sems.at[i])
         for i, (source, target) in enumerate(
-            ((decay_far, decay_ref), (key_far, key_ref), (value_far, value_ref), (query_far, query_ref))
+            ((decay_far, decay_ref), (key_far, key_ref), (value_far, value_ref))
         )
     ]
     for copy in copies:
         copy.start()
     copies[0].wait()
-    tall, wide, mask = decays(decay_ref[...])
+    tall, wide = decays(decay_ref[...])
+    tall_ref[...] = tall
+    wide_ref[...] = wide
     total = tall[-1:, :]
     trailing = jnp.exp(total - tall)
-    for copy in copies[1:]:
-        copy.wait()
+    copies[1].wait()
+    copies[2].wait()
     for head in range(heads):
         here = cols(head, size)
         key, value = key_ref[:, here], value_ref[:, here]
@@ -96,47 +102,77 @@
         for part in range(per):
             out_ref[first + part, :rows, :] = state[part * rows : (part + 1) * rows, :]
             out_ref[first + part, rows:, :] = mark
-        scores = product(query_ref[:, here], key, NT) * weights_of(tall, wide, mask, head)
-        inside_ref[:, here] = product(scores, value, NN)
 
 
 def times(gain, state):
     return (gain[None] * state.reshape(-1, 8, state.shape[-1])).reshape(state.shape)
 
 
-def group_kernel(members, copies, backward, rows, piece_ref, decay_ref, out_ref):
-    total = None
-    order = reversed(range(members)) if backward else range(members)
-    whole = jnp.zeros(decay_ref.shape[1:], f32)
-    for member in order:
-        mark = decay_ref[rank(member)]
-        state = piece_ref[rank(member), :rows, :]
-        total = state if total is None else times(jnp.exp(mark), total) + state
+def group_kernel(members, copies, rows, piece_ref, out_ref):
+    total = jnp.zeros((rows, piece_ref.shape[-1]), f32)
+    whole = jnp.zeros((8, piece_ref.shape[-1]), f32)
+    for member in range(members):
+        place = rank(member)
+        mark = piece_ref[place, rows:, :]
+        total = times(jnp.exp(mark), total) + piece_ref[place, :rows, :]
         whole = whole + mark
     for copy in range(copies):
         out_ref[copy, :rows, :] = total
         out_ref[copy, rows:, :] = whole
 
 
-def spread_kernel(members, groups, backward, rows, piece_ref, decay_ref, total_ref, out_ref):
+def spread_kernel(members, groups, rows, piece_ref, total_ref, out_ref, near_ref, far_ref):
     mine = group_here(members // 2)
     running = jnp.zeros((rows, piece_ref.shape[-1]), f32)
-    for group in reversed(range(groups)) if backward else range(groups):
-        longer = times(jnp.exp(total_ref[group, rows:, :]), running) + total_ref[group, :rows, :]
-        running = jnp.where(group > mine if backward else group < mine, longer, running)
-    for member in reversed(range(members)) if backward else range(members):
+    for group in range(groups):
+        gain = jnp.exp(total_ref[group, rows:, :])
+        far_ref[group] = gain
+        longer = times(gain, running) + total_ref[group, :rows, :]
+        running = jnp.where(group < mine, longer, running)
+    for member in range(members):
+        place = rank(member)
+        gain = jnp.exp(piece_ref[place, rows:, :])
+        near_ref[place] = gain
+        out_ref[place] = running
+        running = times(gain, running) + piece_ref[place, :rows, :]
+
+
+def back_group_kernel(members, copies, piece_ref, near_ref, out_ref):
+    total = jnp.zeros(piece_ref.shape[1:], f32)
+    for member in reversed(range(members)):
+        place = rank(member)
+        total = times(near_ref[place], total) + piece_ref[place]
+    for copy in range(copies):
+        out_ref[copy] = total
+
+
+def back_spread_kernel(members, groups, piece_ref, near_ref, total_ref, far_ref, out_ref):
+    mine = group_here(members // 2)
+    running = jnp.zeros(piece_ref.shape[1:], f32)
+    for group in reversed(range(groups)):
+        longer = times(far_ref[group], running) + total_ref[group]
+        running = jnp.where(group > mine, longer, running)
+    for member in reversed(range(members)):
         place = rank(member)
         out_ref[place] = running
-        running = times(jnp.exp(decay_ref[place]), running) + piece_ref[place, :rows, :]
+        running = times(near_ref[place], running) + piece_ref[place]
+
+
+def inside_kernel(heads, query_ref, key_ref, value_ref, tall_ref, wide_ref, out_ref):
+    size = key_ref.shape[1] // heads
+    tall, wide = tall_ref[...], wide_ref[...]
+    for head in range(heads):
+        here = cols(head, size)
+        scores = product(query_ref[:, here], key_ref[:, here], NT) * weights_of(tall, wide, head)
+        out_ref[:, here] = product(scores, value_ref[:, here], NN)
 
 
 def mixed_kernel(
-    heads, query_ref, decay_ref, inside_ref, state_ref, gain_ref, grad_ref, out_ref, sums_ref
+    heads, query_ref, tall_ref, inside_ref, state_ref, gain_ref, grad_ref, out_ref, sums_ref
 ):
     size = query_ref.shape[1] // heads
     rows = query_ref.shape[0]
-    tall, _, _ = decays(decay_ref[...])
-    rising = jnp.exp(tall)
+    rising = jnp.exp(tall_ref[...])
     squares = jnp.zeros((rows, size), f32)
     products = jnp.zeros((rows, size), f32)
     for head in range(heads):
@@ -154,26 +190,25 @@
         sums_ref[copy, 1:2, :] = product_[0:1, :]
 
 
-def norm_kernel(
-    heads, members, full_width, query_ref, decay_ref, mixed_ref, gain_ref, grad_ref, sums_ref, normed_ref, slope_ref, out_ref
+def row_factors(full_width, size, sums_ref):
+    ones = jnp.ones((sums_ref.shape[0], size), f32)
+    square = lax.dot_general(sums_ref[:, 0, :], ones, TN, precision=highest, preferred_element_type=f32)
+    product_ = lax.dot_general(sums_ref[:, 1, :], ones, TN, precision=highest, preferred_element_type=f32)
+    scale = lax.rsqrt(square / full_width + epsilon)
+    return scale, scale * scale * scale * (product_ / full_width)
+
+
+def back_kernel(
+    heads, members, full_width, query_ref, tall_ref, mixed_ref, gain_ref, grad_ref, sums_ref, out_ref
 ):
     size = query_ref.shape[1] // heads
     per = members // heads
     cut = size // per
-    tall, _, _ = decays(decay_ref[...])
-    rising = jnp.exp(tall)
-    ones = jnp.ones((sums_ref.shape[0], size), f32)
-    square = lax.dot_general(sums_ref[:, 0, :], ones, TN, precision=highest, preferred_element_type=f32)
-    product_ = lax.dot_general(sums_ref[:, 1, :], ones, TN, precision=highest, preferred_element_type=f32)
-    scale = lax.rsqrt(square / full_width + epsilon)
-    pull = scale * scale * scale * (product_ / full_width)
-    for head in range(heads):
-        here = cols(head, size)
-        mixed = mixed_ref[:, here]
-        gain = gain_ref[:, here]
-        normed_ref[:, here] = (mixed * scale * gain).astype(bf16)
-        slope = scale * (grad_ref[:, here].astype(f32) * gain) - pull * mixed
-        slope_ref[:, here] = slope
+    rising = jnp.exp(tall_ref[...])
+    scale, pull = row_factors(full_width, size, sums_ref)
+    for head in range(heads):
+        here = cols(head, size)
+        slope = scale * (grad_ref[:, here].astype(f32) * gain_ref[:, here]) - pull * mixed_ref[:, here]
         state = product(query_ref[:, here], slope * rising[:, head : head + 1], TN)
         first = turned(head, heads) * per
         for part in range(per):
@@ -181,16 +216,34 @@
 
 
 def near_kernel(
-    heads, query_ref, key_ref, value_ref, decay_ref, state_ref, slope_ref, grad_q_ref, near_k_ref, near_v_ref
+    heads,
+    full_width,
+    query_ref,
+    key_ref,
+    value_ref,
+    tall_ref,
+    wide_ref,
+    state_ref,
+    mixed_ref,
+    gain_ref,
+    grad_ref,
+    sums_ref,
+    normed_ref,
+    grad_q_ref,
+    near_k_ref,
+    near_v_ref,
 ):
     size = key_ref.shape[1] // heads
-    tall, wide, mask = decays(decay_ref[...])
+    tall, wide = tall_ref[...], wide_ref[...]
     rising = jnp.exp(tall)
+    scale, pull = row_factors(full_width, size, sums_ref)
     for head in range(heads):
         here = cols(head, size)
         query, key, value = query_ref[:, here], key_ref[:, here], value_ref[:, here]
-        slope = slope_ref[:, here]
-        weights = weights_of(tall, wide, mask, head)
+        gain, mixed = gain_ref[:, here], mixed_ref[:, here]
+        normed_ref[:, here] = (mixed * scale * gain).astype(bf16)
+        slope = scale * (grad_ref[:, here].astype(f32) * gain) - pull * mixed
+        weights = weights_of(tall, wide, head)
         scores = product(query, key, NT) * weights
         grad_scores = product(slope, value, NT) * weights
         there = turned(head, heads)
@@ -200,9 +253,9 @@
         near_v_ref[:, here] = product(scores, slope, TN)
 
 
-def far_kernel(heads, key_ref, value_ref, decay_ref, state_ref, near_k_ref, near_v_ref, grad_k_ref, grad_v_ref):
+def far_kernel(heads, key_ref, value_ref, tall_ref, state_ref, near_k_ref, near_v_ref, grad_k_ref, grad_v_ref):
     size = key_ref.shape[1] // heads
-    tall, _, _ = decays(decay_ref[...])
+    tall = tall_ref[...]
     trailing = jnp.exp(tall[-1:, :] - tall)
     for head in range(heads):
         here = cols(head, size)
@@ -262,41 +315,34 @@
     def exchange(parts, lists):
         return lax.all_to_all(parts, "ctx", 0, 0, axis_index_groups=lists)
 
-    def carried(pieces, marks, backward):
-        (total,) = call(
-            bind(group_kernel, members, groups, backward, rows),
-            [shape((groups, rows + 8, size), f32)],
-            pieces,
-            marks,
-        )
-        totals = exchange(total, far)
-        (entering,) = call(
-            bind(spread_kernel, members, groups, backward, rows),
-            [shape((members, rows, size), f32)],
-                pieces,
-            marks,
-            totals,
-            )
-        return exchange(entering, near).reshape(heads, size, size)
-
-    states, inside = call(
+    states, tall, across = call(
         bind(states_kernel, heads, members),
-        [shape((members, rows + 8, size), f32), wide],
-        queries,
+        [shape((members, rows + 8, size), f32), shape((tok_rows, heads), f32), shape((heads, tok_rows), f32)],
         key_rows,
         value_rows,
         log_decay,
-        flops=5 * unit,
-        copied=(queries, key_rows, value_rows, log_decay),
+        flops=2 * unit,
+        copied=(key_rows, value_rows, log_decay),
     )
     pieces = exchange(states, near)
-    marks = pieces[:, rows:, :]
-    entry = carried(pieces, marks, False)
+    (total,) = call(
+        bind(group_kernel, members, groups, rows), [shape((groups, rows + 8, size), f32)], pieces
+    )
+    (inside,) = call(
+        bind(inside_kernel, heads), [wide], queries, key_rows, value_rows, tall, across, flops=3 * unit
+    )
+    entering, near_gains, far_gains = call(
+        bind(spread_kernel, members, groups, rows),
+        [shape((members, rows, size), f32), shape((members, 8, size), f32), shape((groups, 8, size), f32)],
+        pieces,
+        exchange(total, far),
+    )
+    entry = exchange(entering, near).reshape(heads, size, size)
     mixed, sums = call(
         bind(mixed_kernel, heads),
         [wide, shape((lax.axis_size("tp"), 2, tok_rows), f32)],
         queries,
-        log_decay,
+        tall,
         inside,
         entry,
         gain,
@@ -304,11 +350,12 @@
         flops=2 * unit,
     )
     gathered = lax.all_to_all(sums, "tp", 0, 0)
-    normed, slope, back = call(
-        bind(norm_kernel, heads, members, feat_width * lax.axis_size("tp")),
-        [narrow, wide, shape((members, rows, size), f32)],
+    full_width = feat_width * lax.axis_size("tp")
+    (back,) = call(
+        bind(back_kernel, heads, members, full_width),
+        [shape((members, rows, size), f32)],
         queries,
-        log_decay,
+        tall,
         mixed,
         gain,
         grad_output,
@@ -316,25 +363,43 @@
         flops=2 * unit,
     )
     back_pieces = exchange(back, near)
-    grad_q, near_k, near_v = call(
-        bind(near_kernel, heads),
-        [narrow, shape((heads, size, size), f32), wide],
+    (back_total,) = call(
+        bind(back_group_kernel, members, groups),
+        [shape((groups, rows, size), f32)],
+        back_pieces,
+        near_gains,
+    )
+    (returning,) = call(
+        bind(back_spread_kernel, members, groups),
+        [shape((members, rows, size), f32)],
+        back_pieces,
+        near_gains,
+        exchange(back_total, far),
+        far_gains,
+    )
+    leaving = exchange(returning, near).reshape(heads, size, size)
+    normed, grad_q, near_k, near_v = call(
+        bind(near_kernel, heads, full_width),
+        [narrow, narrow, shape((heads, size, size), f32), wide],
         queries,
         key_rows,
         value_rows,
-        log_decay,
+        tall,
+        across,
         entry,
-        slope,
+        mixed,
+        gain,
+        grad_output,
+        gathered,
         flops=13 * unit,
-        aliases={4: 1, 5: 2},
-    )
-    leaving = carried(back_pieces, marks, True)
+        aliases={5: 2, 6: 3},
+    )
     grad_k, grad_v = call(
         bind(far_kernel, heads),
         [narrow, narrow],
         key_rows,
         value_rows,
-        log_decay,
+        tall,
         leaving,
         near_k,
         near_v,

time: 142 us -> 140 us (0.986)
  blocking collectives: 115 us -> 94.1 us
  waiting for transfers between devices: 9.24 us -> 24.6 us
  starting transfers between devices: 5.06 us -> 9.6 us
    all_to_all x5 -> x4, blocking collectives: 106 us -> 85.5 us  [exchange(): return lax.all_to_all(parts, 'ctx', 0, 0, axis_index_groups=lists)]
    all_to_all x1 -> x2, waiting for transfers between devices: 9.24 us -> 24.6 us  [exchange(): return lax.all_to_all(parts, 'ctx', 0, 0, axis_index_groups=lists)]
    all_to_all x1 -> x2, starting transfers between devices: 5.06 us -> 9.6 us  [exchange(): return lax.all_to_all(parts, 'ctx', 0, 0, axis_index_groups=lists)]
    pallas_call x9 -> x10, Pallas kernels: 10.7 us -> 10.5 us  [call(): pl.pallas_call(kernel, out_shape=outs, in_specs=[hbm if copied else vmem]...]
  transfers between devices with their start and end apart: 1 -> 2, of which waited for: 1 -> 2; matrix products, arithmetic and copies ran while one was open for 0% -> 0% of each run, Pallas kernels for 2% -> 3%
where the time goes in v6:
time: 140 us
  blocking collectives  94.1 us (67%)
  waiting for transfers between devices  24.6 us (18%)
  Pallas kernels  10.5 us (8%)
  starting transfers between devices  9.6 us (7%)
    all_to_all x4, blocking collectives, exchange(): return lax.all_to_all(parts, 'ctx', 0, 0, axis_index_groups=lists)  85.5 us
    all_to_all x2, waiting for transfers between devices, exchange(): return lax.all_to_all(parts, 'ctx', 0, 0, axis_index_groups=lists)  24.6 us
    pallas_call x10, Pallas kernels, call(): pl.pallas_call(kernel, out_shape=outs, in_specs=[hbm if copied else vmem]...  10.5 us
    all_to_all x2, starting transfers between devices, exchange(): return lax.all_to_all(parts, 'ctx', 0, 0, axis_index_groups=lists)  9.6 us
    all_to_all x1, blocking collectives, shards(): gathered = lax.all_to_all(sums, 'tp', 0, 0)  8.57 us
  transfers between devices with their start and end apart: 2, of which 2 were waited for; matrix products, arithmetic and copies ran while one was open for 0% of the time, Pallas kernels for 3%

profile of v6, /device:TPU:8, one launch (start us, length us, event | category | flops | bytes accessed | tf_op | source)
XLA Modules:
  0.0 139.5 jit_solution(5747811945518411166)
XLA Ops:
  0.6 1.7 %shard_map.93 = (f32[16,72,128]{2,1,0:T(8,128)S(1)}, f32[128,8]{1,0:T(8,128)S(1)}, f32[8,128]{1,0:T(8,128)S(1)}) custom-call(bf16[128,1024]{1,0:T(8,128)(2,1)} %key_ref.5, bf16[128,1024]{1,0:T(8,128)(2,1)} %value_ref.5, f32[8,128]{1,0:T(8,128)} %bitcast.10), custom_call_target="tpu_custom_call" | custom-call | flops 67108864 | bytes 1126400 | tf_op jit(solution)/shard_map/pallas_call | solution.py:277
  2.4 26.2 %all_to_all.35.piece_ref = f32[16,72,128]{2,1,0:T(8,128)S(1)} all-to-all(f32[16,72,128]{2,1,0:T(8,128)S(1)} %get-tuple-element.20), channel_id=1, replica_groups={{0,32,64,96,8,40,72,104,16,48,80,112,24,56,88,120},{128,160,192,224,136..., dimensions={0} | all-to-all | bytes 1179648 | tf_op jit(solution)/shard_map/all_to_all | solution.py:316
  28.6 0.1 shard_map.94
  28.6 24.0 %all_to_all.36.total_ref = f32[4,72,128]{2,1,0:T(8,128)S(1)} all-to-all(f32[4,72,128]{2,1,0:T(8,128)S(1)} %shard_map.94), channel_id=1, replica_groups={{0,128,320,448},{32,160,352,480},{64,192,256,384},{96,224,288,416},{8,1..., dimensions={0} | all-to-all | bytes 294912 | tf_op jit(solution)/shard_map/all_to_all | solution.py:316
  52.6 0.9 shard_map.95
  53.5 4.8 %all-to-all-start.2 = ((f32[16,64,128]{2,1,0:T(8,128)}), f32[16,64,128]{2,1,0:T(8,128)S(1)}, u32[]{:S(2)}, u32[]{:S(2)}) async-start(f32[16,64,128]{2,1,0:T(8,128)} %get-tuple-element.21), calls=%async_computation.2 | async-start | bytes 1048576 | tf_op jit(solution)/shard_map/all_to_all | solution.py:316
  58.3 0.0 copy-done
  58.3 0.0 copy-done.1
  58.3 0.0 copy-done.2
  58.3 0.0 copy-start.3
  58.3 0.0 copy-start.4
  58.3 0.6 shard_map.96.inside_ref
  58.9 15.4 %all-to-all-done.2 = f32[16,64,128]{2,1,0:T(8,128)S(1)} async-done(((f32[16,64,128]{2,1,0:T(8,128)}), f32[16,64,128]{2,1,0:T(8,128)S(1)}, u32[]{:S(2)}, u32[]{:S(2)}) %all-to-all-start.2) | async-done | bytes 524320 | tf_op jit(solution)/shard_map/all_to_all | solution.py:316
  74.3 0.6 shard_map.97
  74.9 8.6 %all_to_all.37.sums_ref = f32[8,2,128]{2,1,0:T(2,128)S(1)} all-to-all(f32[8,2,128]{2,1,0:T(2,128)S(1)} %get-tuple-element.23), channel_id=1, replica_groups=mesh['ctx'=64,'tp'=8] {'tp'}, dimensions={0} | all-to-all | bytes 16384 | tf_op jit(solution)/shard_map/all_to_all | solution.py:352
  83.5 0.7 shard_map.99
  84.2 19.4 %all_to_all.38.piece_ref = f32[16,64,128]{2,1,0:T(8,128)S(1)} all-to-all(f32[16,64,128]{2,1,0:T(8,128)S(1)} %shard_map.99), channel_id=1, replica_groups={{0,32,64,96,8,40,72,104,16,48,80,112,24,56,88,120},{128,160,192,224,136..., dimensions={0} | all-to-all | bytes 1048576 | tf_op jit(solution)/shard_map/all_to_all | solution.py:316
  103.6 0.1 shard_map.100
  103.6 16.0 %all_to_all.39.total_ref = f32[4,64,128]{2,1,0:T(8,128)S(1)} all-to-all(f32[4,64,128]{2,1,0:T(8,128)S(1)} %shard_map.100), channel_id=1, replica_groups={{0,128,320,448},{32,160,352,480},{64,192,256,384},{96,224,288,416},{8,1..., dimensions={0} | all-to-all | bytes 262144 | tf_op jit(solution)/shard_map/all_to_all | solution.py:316
  119.6 0.9 shard_map.101
  120.5 4.8 %all-to-all-start.6 = ((f32[16,64,128]{2,1,0:T(8,128)}), f32[16,64,128]{2,1,0:T(8,128)S(1)}, u32[]{:S(2)}, u32[]{:S(2)}) async-start(f32[16,64,128]{2,1,0:T(8,128)} %shard_map.101), calls=%async_computation.6 | async-start | bytes 1048576 | tf_op jit(solution)/shard_map/all_to_all | solution.py:316
  125.3 3.6 %shard_map.98 = (bf16[128,1024]{1,0:T(8,128)(2,1)}, bf16[128,1024]{1,0:T(8,128)(2,1)}, f32[8,128,128]{2,1,0:T(8,128)S(1)}, f32[128,1024]{1,0:T(8,128)S(1)}) custom-call(bf16[128,1024]{1,0:T(8,128)(2,1)S(1)} %copy-done, bf16[128,1024]{1,0:T(8,128)(2,1)S(1)} %copy-done.1, ...), custom_call_target="tpu_custom_call", output_to_operand_aliasing={{2}: (5, {}), {3}: (6, {})} | custom-call | flops 436207616 | bytes 3690496 | tf_op jit(solution)/shard_map/pallas_call | solution.py:277
  128.9 9.2 %all-to-all-done.6 = f32[16,64,128]{2,1,0:T(8,128)S(1)} async-done(((f32[16,64,128]{2,1,0:T(8,128)}), f32[16,64,128]{2,1,0:T(8,128)S(1)}, u32[]{:S(2)}, u32[]{:S(2)}) %all-to-all-start.6) | async-done | bytes 524320 | tf_op jit(solution)/shard_map/all_to_all | solution.py:316
  138.1 1.4 %shard_map.102 = (bf16[128,1024]{1,0:T(8,128)(2,1)}, bf16[128,1024]{1,0:T(8,128)(2,1)}) custom-call(bf16[128,1024]{1,0:T(8,128)(2,1)S(1)} %copy-done.1, bf16[128,1024]{1,0:T(8,128)(2,1)S(1)} %copy-done.2, f32[128,8]{1,0:T(8,128)S(1)} %get-tuple-element.18.tall_ref, f32[8,128,128]{2,1,0:T(8,128)S(1)} %bitcast.6, ...), custom_call_target="tpu_custom_call" | custom-call | flops 134217728 | bytes 2625536 | tf_op jit(solution)/shard_map/pallas_call | solution.py:277
  (5 shorter events, 0.0 us)
Async XLA Ops:
  53.5 4.8 %copy-start = (bf16[128,1024]{1,0:T(8,128)(2,1)S(1)}, bf16[128,1024]{1,0:T(8,128)(2,1)}, u32[]{:S(2)}) copy-start(bf16[128,1024]{1,0:T(8,128)(2,1)} %query_ref.7) | copy-start | bytes 786436
  53.5 4.8 %copy-start.1 = (bf16[128,1024]{1,0:T(8,128)(2,1)S(1)}, bf16[128,1024]{1,0:T(8,128)(2,1)}, u32[]{:S(2)}) copy-start(bf16[128,1024]{1,0:T(8,128)(2,1)} %key_ref.5) | copy-start | bytes 786436
  53.5 4.8 %copy-start.2 = (bf16[128,1024]{1,0:T(8,128)(2,1)S(1)}, bf16[128,1024]{1,0:T(8,128)(2,1)}, u32[]{:S(2)}) copy-start(bf16[128,1024]{1,0:T(8,128)(2,1)} %value_ref.5) | copy-start | bytes 786436
  53.5 20.8 %all-to-all-start.2 = ((f32[16,64,128]{2,1,0:T(8,128)}), f32[16,64,128]{2,1,0:T(8,128)S(1)}, u32[]{:S(2)}, u32[]{:S(2)}) async-start(f32[16,64,128]{2,1,0:T(8,128)} %get-tuple-element.21), calls=%async_computation.2 | async-start | bytes 1048576 | tf_op jit(solution)/shard_map/all_to_all | solution.py:316
  58.3 16.0 %copy-start.3 = (bf16[128,1024]{1,0:T(8,128)(2,1)S(1)}, bf16[128,1024]{1,0:T(8,128)(2,1)}, u32[]{:S(2)}) copy-start(bf16[128,1024]{1,0:T(8,128)(2,1)} %grad_ref.5) | copy-start | bytes 786436
  58.3 16.0 %copy-start.4 = (f32[1024]{0:T(1024)S(1)}, f32[1024]{0:T(1024)}, u32[]{:S(2)}) copy-start(f32[1024]{0:T(1024)} %param.10) | copy-start | bytes 12292
  120.5 17.6 %all-to-all-start.6 = ((f32[16,64,128]{2,1,0:T(8,128)}), f32[16,64,128]{2,1,0:T(8,128)S(1)}, u32[]{:S(2)}, u32[]{:S(2)}) async-start(f32[16,64,128]{2,1,0:T(8,128)} %shard_map.101), calls=%async_computation.6 | async-start | bytes 1048576 | tf_op jit(solution)/shard_map/all_to_all | solution.py:316

commit v7 on v6

--- a/solution.py
+++ b/solution.py
@@ -54,17 +54,22 @@
     return jnp.where(mask, jnp.exp(jnp.where(mask, differences, 0.0)), 0.0)
 
 
-def group_here(heads):
-    return lax.div(lax.axis_index("ctx"), 2 * heads)
-
-
-def rank(place):
-    return place % 4 * 4 + place // 4
+def whereabouts(heads):
+    span = 2 * heads // 4
+    z_rows = lax.axis_size("ctx") // 4
+    shift = (lax.axis_index("tp") & 1) * (span // 2)
+    group = lax.div((lax.div(lax.axis_index("ctx"), 4) - shift) & (z_rows - 1), span)
+    cut = jnp.logical_and(shift > 0, group == z_rows // span - 1)
+    return group, shift, cut
 
 
 def turned(head, heads):
     half = lax.axis_size("ctx") // (2 * heads) // 2
-    return head ^ jnp.where(group_here(heads) < half, 0, 1)
+    return head ^ jnp.where(whereabouts(heads)[0] < half, 0, 1)
+
+
+def rank(member, cut):
+    return member % 4 * 4 + ((member // 4) ^ jnp.where(cut, 2, 0))
 
 
 def cols(head, size):
@@ -109,28 +114,39 @@
 
 
 def group_kernel(members, copies, rows, piece_ref, out_ref):
+    _, _, cut = whereabouts(members // 2)
     total = jnp.zeros((rows, piece_ref.shape[-1]), f32)
     whole = jnp.zeros((8, piece_ref.shape[-1]), f32)
+    early = total
     for member in range(members):
-        place = rank(member)
+        if member == members // 2:
+            early = total
+        place = rank(member, cut)
         mark = piece_ref[place, rows:, :]
         total = times(jnp.exp(mark), total) + piece_ref[place, :rows, :]
         whole = whole + mark
+    total = jnp.where(cut, early, total)
     for copy in range(copies):
         out_ref[copy, :rows, :] = total
         out_ref[copy, rows:, :] = whole
 
 
 def spread_kernel(members, groups, rows, piece_ref, total_ref, out_ref, near_ref, far_ref):
-    mine = group_here(members // 2)
-    running = jnp.zeros((rows, piece_ref.shape[-1]), f32)
-    for group in range(groups):
+    mine, shift, cut = whereabouts(members // 2)
+    first = jnp.where(shift > 0, groups - 1, 0)
+    before = jnp.where(cut, 0, mine + jnp.where(shift > 0, 1, 0))
+    every = jnp.zeros((rows, piece_ref.shape[-1]), f32)
+    running = every
+    for step in range(groups):
+        group = (step + first) & (groups - 1)
         gain = jnp.exp(total_ref[group, rows:, :])
         far_ref[group] = gain
-        longer = times(gain, running) + total_ref[group, :rows, :]
-        running = jnp.where(group < mine, longer, running)
+        every = times(gain, every) + total_ref[group, :rows, :]
+        running = jnp.where(step < before, every, running)
     for member in range(members):
-        place = rank(member)
+        if member == members // 2:
+            running = jnp.where(cut, every, running)
+        place = rank(member, cut)
         gain = jnp.exp(piece_ref[place, rows:, :])
         near_ref[place] = gain
         out_ref[place] = running
@@ -138,24 +154,32 @@
 
 
 def back_group_kernel(members, copies, piece_ref, near_ref, out_ref):
+    _, _, cut = whereabouts(members // 2)
     total = jnp.zeros(piece_ref.shape[1:], f32)
+    late = total
     for member in reversed(range(members)):
-        place = rank(member)
+        place = rank(member, cut)
         total = times(near_ref[place], total) + piece_ref[place]
+        if member == members // 2:
+            late = total
+    total = jnp.where(cut, late, total)
     for copy in range(copies):
         out_ref[copy] = total
 
 
 def back_spread_kernel(members, groups, piece_ref, near_ref, total_ref, far_ref, out_ref):
-    mine = group_here(members // 2)
-    running = jnp.zeros(piece_ref.shape[1:], f32)
+    mine, _, cut = whereabouts(members // 2)
+    every = jnp.zeros(piece_ref.shape[1:], f32)
+    running = every
     for group in reversed(range(groups)):
-        longer = times(far_ref[group], running) + total_ref[group]
-        running = jnp.where(group > mine, longer, running)
+        every = times(far_ref[group], every) + total_ref[group]
+        running = jnp.where(group > mine, every, running)
     for member in reversed(range(members)):
-        place = rank(member)
+        place = rank(member, cut)
         out_ref[place] = running
         running = times(near_ref[place], running) + piece_ref[place]
+        if member == members // 2:
+            running = jnp.where(cut, every, running)
 
 
 def inside_kernel(heads, query_ref, key_ref, value_ref, tall_ref, wide_ref, out_ref):
@@ -287,21 +311,31 @@
     )(*args)
 
 
-def levels(count, heads):
+def levels(count, tp, heads):
     members = 2 * heads
+    span = members // 4
     groups = count // members
-    near = [[group * members + rank(i) for i in range(members)] for group in range(groups)]
-    far = [
-        [group * members + rank(piece ^ (2 if group >= groups // 2 else 0)) for group in range(groups)]
-        for piece in range(members)
-    ]
+    near, far = [], []
+    for index in range(tp):
+        shift = index % 2 * (span // 2)
+
+        def device(group, place):
+            z = (group * span + shift + place % 4) % (count // 4)
+            return (z * 4 + place // 4) * tp + index
+
+        for group in range(groups):
+            near.append([device(group, place) for place in range(members)])
+        for piece in range(members):
+            far.append(
+                [device(group, piece ^ (2 if group >= groups // 2 else 0)) for group in range(groups)]
+            )
     return groups, members, near, far
 
 
 def shards(queries, key_rows, value_rows, log_decay, norm_gain, grad_output):
     tok_rows, feat_width = queries.shape
     heads = log_decay.shape[1]
-    groups, members, near, far = levels(lax.axis_size("ctx"), heads)
+    groups, members, near, far = levels(lax.axis_size("ctx"), lax.axis_size("tp"), heads)
     size = feat_width // heads
     rows = heads * size // members
     wide = jax.ShapeDtypeStruct((tok_rows, feat_width), f32)
@@ -313,7 +347,7 @@
     unit = 2 * heads * tok_rows * size * size
 
     def exchange(parts, lists):
-        return lax.all_to_all(parts, "ctx", 0, 0, axis_index_groups=lists)
+        return lax.all_to_all(parts, ("ctx", "tp"), 0, 0, axis_index_groups=lists)
 
     states, tall, across = call(
         bind(states_kernel, heads, members),

time: 140 us -> 136 us (0.971)
  the two profiles are of different devices: /device:TPU:8 before, /device:TPU:1 now
where the time goes in v7:
time: 136 us; the launch traced here: 134 us
  blocking collectives  90.6 us (67%)
  starting transfers between devices  16.8 us (12%)
  waiting for transfers between devices  15.2 us (11%)
  Pallas kernels  10.5 us (8%)
    all_to_all x4, blocking collectives, exchange(): return lax.all_to_all(parts, ('ctx', 'tp'), 0, 0, axis_index_groups=lists)  76.1 us
    all_to_all x2, starting transfers between devices, exchange(): return lax.all_to_all(parts, ('ctx', 'tp'), 0, 0, axis_index_groups=lists)  16.8 us
    all_to_all x2, waiting for transfers between devices, exchange(): return lax.all_to_all(parts, ('ctx', 'tp'), 0, 0, axis_index_groups=lists)  15.2 us
    all_to_all x1, blocking collectives, shards(): gathered = lax.all_to_all(sums, 'tp', 0, 0)  14.5 us
    pallas_call x10, Pallas kernels, call(): pl.pallas_call(kernel, out_shape=outs, in_specs=[hbm if copied else vmem]...  10.5 us
  transfers between devices with their start and end apart: 2, of which 2 were waited for; matrix products, arithmetic and copies ran while one was open for 0% of the time, Pallas kernels for 3%

profile of v7, /device:TPU:1, one launch (start us, length us, event | category | flops | bytes accessed | tf_op | source)
XLA Modules:
  0.0 133.9 jit_solution(14884015112155033777)
XLA Ops:
  0.6 1.7 %shard_map.93 = (f32[16,72,128]{2,1,0:T(8,128)S(1)}, f32[128,8]{1,0:T(8,128)S(1)}, f32[8,128]{1,0:T(8,128)S(1)}) custom-call(bf16[128,1024]{1,0:T(8,128)(2,1)} %key_ref.5, bf16[128,1024]{1,0:T(8,128)(2,1)} %value_ref.5, f32[8,128]{1,0:T(8,128)} %bitcast.10), custom_call_target="tpu_custom_call" | custom-call | flops 67108864 | bytes 1126400 | tf_op jit(solution)/shard_map/pallas_call | solution.py:301
  2.4 25.8 %all_to_all.35.piece_ref = f32[16,72,128]{2,1,0:T(8,128)S(1)} all-to-all(f32[16,72,128]{2,1,0:T(8,128)S(1)} %get-tuple-element.20), channel_id=1, replica_groups={{0,32,64,96,8,40,72,104,16,48,80,112,24,56,88,120},{128,160,192,224,136..., dimensions={0} | all-to-all | bytes 1179648 | tf_op jit(solution)/shard_map/all_to_all | solution.py:350
  28.2 0.1 shard_map.94
  28.2 20.2 %all_to_all.36.total_ref = f32[4,72,128]{2,1,0:T(8,128)S(1)} all-to-all(f32[4,72,128]{2,1,0:T(8,128)S(1)} %shard_map.94), channel_id=1, replica_groups={{0,128,320,448},{32,160,352,480},{64,192,256,384},{96,224,288,416},{8,1..., dimensions={0} | all-to-all | bytes 294912 | tf_op jit(solution)/shard_map/all_to_all | solution.py:350
  48.4 0.9 shard_map.95
  49.3 5.5 %all-to-all-start.2 = ((f32[16,64,128]{2,1,0:T(8,128)}), f32[16,64,128]{2,1,0:T(8,128)S(1)}, u32[]{:S(2)}, u32[]{:S(2)}) async-start(f32[16,64,128]{2,1,0:T(8,128)} %get-tuple-element.21), calls=%async_computation.2 | async-start | bytes 1048576 | tf_op jit(solution)/shard_map/all_to_all | solution.py:350
  54.7 0.0 copy-done
  54.7 0.0 copy-done.1
  54.8 0.0 copy-start.3
  54.8 0.0 copy-start.4
  54.8 0.6 shard_map.96.inside_ref
  55.4 8.4 %all-to-all-done.2 = f32[16,64,128]{2,1,0:T(8,128)S(1)} async-done(((f32[16,64,128]{2,1,0:T(8,128)}), f32[16,64,128]{2,1,0:T(8,128)S(1)}, u32[]{:S(2)}, u32[]{:S(2)}) %all-to-all-start.2) | async-done | bytes 524320 | tf_op jit(solution)/shard_map/all_to_all | solution.py:350
  63.8 0.0 copy-done.4
  63.8 0.6 shard_map.97
  64.4 14.5 %all_to_all.37.sums_ref = f32[8,2,128]{2,1,0:T(2,128)S(1)} all-to-all(f32[8,2,128]{2,1,0:T(2,128)S(1)} %get-tuple-element.23), channel_id=1, replica_groups=mesh['ctx'=64,'tp'=8] {'tp'}, dimensions={0} | all-to-all | bytes 16384 | tf_op jit(solution)/shard_map/all_to_all | solution.py:386
  78.9 0.7 shard_map.99
  79.6 17.7 %all_to_all.38.piece_ref = f32[16,64,128]{2,1,0:T(8,128)S(1)} all-to-all(f32[16,64,128]{2,1,0:T(8,128)S(1)} %shard_map.99), channel_id=1, replica_groups={{0,32,64,96,8,40,72,104,16,48,80,112,24,56,88,120},{128,160,192,224,136..., dimensions={0} | all-to-all | bytes 1048576 | tf_op jit(solution)/shard_map/all_to_all | solution.py:350
  97.2 0.1 shard_map.100
  97.3 12.5 %all_to_all.39.total_ref = f32[4,64,128]{2,1,0:T(8,128)S(1)} all-to-all(f32[4,64,128]{2,1,0:T(8,128)S(1)} %shard_map.100), channel_id=1, replica_groups={{0,128,320,448},{32,160,352,480},{64,192,256,384},{96,224,288,416},{8,1..., dimensions={0} | all-to-all | bytes 262144 | tf_op jit(solution)/shard_map/all_to_all | solution.py:350
  109.8 0.9 shard_map.101
  110.7 11.4 %all-to-all-start.6 = ((f32[16,64,128]{2,1,0:T(8,128)}), f32[16,64,128]{2,1,0:T(8,128)S(1)}, u32[]{:S(2)}, u32[]{:S(2)}) async-start(f32[16,64,128]{2,1,0:T(8,128)} %shard_map.101), calls=%async_computation.6 | async-start | bytes 1048576 | tf_op jit(solution)/shard_map/all_to_all | solution.py:350
  122.0 3.6 %shard_map.98 = (bf16[128,1024]{1,0:T(8,128)(2,1)}, bf16[128,1024]{1,0:T(8,128)(2,1)}, f32[8,128,128]{2,1,0:T(8,128)S(1)}, f32[128,1024]{1,0:T(8,128)S(1)}) custom-call(bf16[128,1024]{1,0:T(8,128)(2,1)S(1)} %copy-done, bf16[128,1024]{1,0:T(8,128)(2,1)S(1)} %copy-done.1, ...), custom_call_target="tpu_custom_call", output_to_operand_aliasing={{2}: (5, {}), {3}: (6, {})} | custom-call | flops 436207616 | bytes 3690496 | tf_op jit(solution)/shard_map/pallas_call | solution.py:301
  125.6 6.8 %all-to-all-done.6 = f32[16,64,128]{2,1,0:T(8,128)S(1)} async-done(((f32[16,64,128]{2,1,0:T(8,128)}), f32[16,64,128]{2,1,0:T(8,128)S(1)}, u32[]{:S(2)}, u32[]{:S(2)}) %all-to-all-start.6) | async-done | bytes 524320 | tf_op jit(solution)/shard_map/all_to_all | solution.py:350
  132.4 1.4 %shard_map.102 = (bf16[128,1024]{1,0:T(8,128)(2,1)}, bf16[128,1024]{1,0:T(8,128)(2,1)}) custom-call(bf16[128,1024]{1,0:T(8,128)(2,1)S(1)} %copy-done.1, bf16[128,1024]{1,0:T(8,128)(2,1)S(1)} %copy-done.2, f32[128,8]{1,0:T(8,128)S(1)} %get-tuple-element.18.tall_ref, f32[8,128,128]{2,1,0:T(8,128)S(1)} %bitcast.6, ...), custom_call_target="tpu_custom_call" | custom-call | flops 134217728 | bytes 2625536 | tf_op jit(solution)/shard_map/pallas_call | solution.py:301
  (5 shorter events, 0.0 us)
Async XLA Ops:
  49.3 5.5 %copy-start = (bf16[128,1024]{1,0:T(8,128)(2,1)S(1)}, bf16[128,1024]{1,0:T(8,128)(2,1)}, u32[]{:S(2)}) copy-start(bf16[128,1024]{1,0:T(8,128)(2,1)} %query_ref.7) | copy-start | bytes 786436
  49.3 5.5 %copy-start.1 = (bf16[128,1024]{1,0:T(8,128)(2,1)S(1)}, bf16[128,1024]{1,0:T(8,128)(2,1)}, u32[]{:S(2)}) copy-start(bf16[128,1024]{1,0:T(8,128)(2,1)} %key_ref.5) | copy-start | bytes 786436
  49.3 5.5 %copy-start.2 = (bf16[128,1024]{1,0:T(8,128)(2,1)S(1)}, bf16[128,1024]{1,0:T(8,128)(2,1)}, u32[]{:S(2)}) copy-start(bf16[128,1024]{1,0:T(8,128)(2,1)} %value_ref.5) | copy-start | bytes 786436
  49.3 14.5 %all-to-all-start.2 = ((f32[16,64,128]{2,1,0:T(8,128)}), f32[16,64,128]{2,1,0:T(8,128)S(1)}, u32[]{:S(2)}, u32[]{:S(2)}) async-start(f32[16,64,128]{2,1,0:T(8,128)} %get-tuple-element.21), calls=%async_computation.2 | async-start | bytes 1048576 | tf_op jit(solution)/shard_map/all_to_all | solution.py:350
  54.8 9.0 %copy-start.3 = (bf16[128,1024]{1,0:T(8,128)(2,1)S(1)}, bf16[128,1024]{1,0:T(8,128)(2,1)}, u32[]{:S(2)}) copy-start(bf16[128,1024]{1,0:T(8,128)(2,1)} %grad_ref.5) | copy-start | bytes 786436
  54.8 9.0 %copy-start.4 = (f32[1024]{0:T(1024)S(1)}, f32[1024]{0:T(1024)}, u32[]{:S(2)}) copy-start(f32[1024]{0:T(1024)} %param.10) | copy-start | bytes 12292
  110.7 21.8 %all-to-all-start.6 = ((f32[16,64,128]{2,1,0:T(8,128)}), f32[16,64,128]{2,1,0:T(8,128)S(1)}, u32[]{:S(2)}, u32[]{:S(2)}) async-start(f32[16,64,128]{2,1,0:T(8,128)} %shard_map.101), calls=%async_computation.6 | async-start | bytes 1048576 | tf_op jit(solution)/shard_map/all_to_all | solution.py:350

commit v8 on v7

--- a/solution.py
+++ b/solution.py
@@ -76,37 +76,46 @@
     return slice(head * size, (head + 1) * size)
 
 
+def parted(heads, size):
+    return [slice(2 * pair * size, 2 * (pair + 1) * size) for pair in range(heads // 2)]
+
+
 def states_kernel(
     heads, members, key_far, value_far, decay_far, out_ref, tall_ref, wide_ref, key_ref, value_ref, decay_ref, sems
 ):
     size = key_ref.shape[1] // heads
     per = members // heads
     rows = size // per
-    copies = [
-        pltpu.make_async_copy(source, target, sems.at[i])
-        for i, (source, target) in enumerate(
-            ((decay_far, decay_ref), (key_far, key_ref), (value_far, value_ref))
+    first = pltpu.make_async_copy(decay_far, decay_ref, sems.at[heads])
+    first.start()
+    copies = []
+    for pair, part in enumerate(parted(heads, size)):
+        copies.append(
+            (
+                pltpu.make_async_copy(key_far.at[:, part], key_ref.at[:, part], sems.at[2 * pair]),
+                pltpu.make_async_copy(value_far.at[:, part], value_ref.at[:, part], sems.at[2 * pair + 1]),
+            )
         )
-    ]
-    for copy in copies:
-        copy.start()
-    copies[0].wait()
+        for copy in copies[-1]:
+            copy.start()
+    first.wait()
     tall, wide = decays(decay_ref[...])
     tall_ref[...] = tall
     wide_ref[...] = wide
     total = tall[-1:, :]
     trailing = jnp.exp(total - tall)
-    copies[1].wait()
-    copies[2].wait()
     for head in range(heads):
+        if head % 2 == 0:
+            for copy in copies[head // 2]:
+                copy.wait()
         here = cols(head, size)
         key, value = key_ref[:, here], value_ref[:, here]
         state = product(key.astype(f32) * trailing[:, head : head + 1], value, TN)
         mark = jnp.broadcast_to(total[:, head : head + 1], (8, size))
-        first = turned(head, heads) * per
+        place = turned(head, heads) * per
         for part in range(per):
-            out_ref[first + part, :rows, :] = state[part * rows : (part + 1) * rows, :]
-            out_ref[first + part, rows:, :] = mark
+            out_ref[place + part, :rows, :] = state[part * rows : (part + 1) * rows, :]
+            out_ref[place + part, rows:, :] = mark
 
 
 def times(gain, state):
@@ -182,27 +191,21 @@
             running = jnp.where(cut, every, running)
 
 
-def inside_kernel(heads, query_ref, key_ref, value_ref, tall_ref, wide_ref, out_ref):
-    size = key_ref.shape[1] // heads
-    tall, wide = tall_ref[...], wide_ref[...]
-    for head in range(heads):
-        here = cols(head, size)
-        scores = product(query_ref[:, here], key_ref[:, here], NT) * weights_of(tall, wide, head)
-        out_ref[:, here] = product(scores, value_ref[:, here], NN)
-
-
 def mixed_kernel(
-    heads, query_ref, tall_ref, inside_ref, state_ref, gain_ref, grad_ref, out_ref, sums_ref
+    heads, query_ref, key_ref, value_ref, tall_ref, wide_ref, state_ref, gain_ref, grad_ref, out_ref, sums_ref
 ):
     size = query_ref.shape[1] // heads
     rows = query_ref.shape[0]
-    rising = jnp.exp(tall_ref[...])
+    tall, wide = tall_ref[...], wide_ref[...]
+    rising = jnp.exp(tall)
     squares = jnp.zeros((rows, size), f32)
     products = jnp.zeros((rows, size), f32)
     for head in range(heads):
         here = cols(head, size)
-        outside = product(query_ref[:, here], state_ref[turned(head, heads)], NN)
-        mixed = inside_ref[:, here] + outside * rising[:, head : head + 1]
+        query = query_ref[:, here]
+        scores = product(query, key_ref[:, here], NT) * weights_of(tall, wide, head)
+        outside = product(query, state_ref[turned(head, heads)], NN)
+        mixed = product(scores, value_ref[:, here], NN) + outside * rising[:, head : head + 1]
         out_ref[:, here] = mixed
         squares = squares + mixed * mixed
         products = products + grad_ref[:, here].astype(f32) * gain_ref[:, here] * mixed
@@ -277,10 +280,24 @@
         near_v_ref[:, here] = product(scores, slope, TN)
 
 
-def far_kernel(heads, key_ref, value_ref, tall_ref, state_ref, near_k_ref, near_v_ref, grad_k_ref, grad_v_ref):
+def far_kernel(
+    heads,
+    key_ref,
+    value_ref,
+    tall_ref,
+    state_ref,
+    near_k_ref,
+    near_v_ref,
+    far_k,
+    far_v,
+    grad_k_ref,
+    grad_v_ref,
+    sems,
+):
     size = key_ref.shape[1] // heads
     tall = tall_ref[...]
     trailing = jnp.exp(tall[-1:, :] - tall)
+    copies = []
     for head in range(heads):
         here = cols(head, size)
         late = trailing[:, head : head + 1]
@@ -290,9 +307,19 @@
         grad_v = near_v_ref[:, here] + product(key_ref[:, here], state, NN) * late
         grad_k_ref[:, here] = grad_k.astype(bf16)
         grad_v_ref[:, here] = grad_v.astype(bf16)
-
-
-def call(kernel, outs, *args, flops=0, copied=(), aliases=None):
+        if head % 2 == 1:
+            part = parted(heads, size)[head // 2]
+            copies += [
+                pltpu.make_async_copy(grad_k_ref.at[:, part], far_k.at[:, part], sems.at[head - 1]),
+                pltpu.make_async_copy(grad_v_ref.at[:, part], far_v.at[:, part], sems.at[head]),
+            ]
+            for copy in copies[-2:]:
+                copy.start()
+    for copy in copies:
+        copy.wait()
+
+
+def call(kernel, outs, *args, flops=0, copied=(), written=(), copies=0, aliases=None):
     vmem = pl.BlockSpec(memory_space=pltpu.VMEM)
     hbm = pl.BlockSpec(memory_space=pltpu.HBM)
     if copied:
@@ -302,10 +329,10 @@
         kernel,
         out_shape=outs,
         in_specs=[hbm if copied else vmem] * len(args),
-        out_specs=[vmem] * len(outs),
+        out_specs=[hbm if written else vmem] * len(outs),
         input_output_aliases=aliases or {},
-        scratch_shapes=[pltpu.VMEM(a.shape, a.dtype) for a in copied]
-        + ([pltpu.SemaphoreType.DMA((len(copied),))] if copied else []),
+        scratch_shapes=[pltpu.VMEM(a.shape, a.dtype) for a in (*copied, *written)]
+        + ([pltpu.SemaphoreType.DMA((copies,))] if copies else []),
         cost_estimate=pl.CostEstimate(flops=flops, bytes_accessed=moved, transcendentals=0),
         compiler_params=pltpu.CompilerParams(vmem_limit_bytes=12 * 1024 * 1024),
     )(*args)
@@ -357,13 +384,11 @@
         log_decay,
         flops=2 * unit,
         copied=(key_rows, value_rows, log_decay),
+        copies=heads + 1,
     )
     pieces = exchange(states, near)
     (total,) = call(
         bind(group_kernel, members, groups, rows), [shape((groups, rows + 8, size), f32)], pieces
-    )
-    (inside,) = call(
-        bind(inside_kernel, heads), [wide], queries, key_rows, value_rows, tall, across, flops=3 * unit
     )
     entering, near_gains, far_gains = call(
         bind(spread_kernel, members, groups, rows),
@@ -376,12 +401,14 @@
         bind(mixed_kernel, heads),
         [wide, shape((lax.axis_size("tp"), 2, tok_rows), f32)],
         queries,
+        key_rows,
+        value_rows,
         tall,
-        inside,
+        across,
         entry,
         gain,
         grad_output,
-        flops=2 * unit,
+        flops=5 * unit,
     )
     gathered = lax.all_to_all(sums, "tp", 0, 0)
     full_width = feat_width * lax.axis_size("tp")
@@ -438,6 +465,8 @@
         near_k,
         near_v,
         flops=4 * unit,
+        written=(narrow, narrow),
+        copies=heads,
     )
     return normed, grad_q, grad_k, grad_v
 

time: 136 us -> 136 us (level)
  blocking collectives: 90.6 us -> 105 us
  waiting for transfers between devices: 15.2 us -> 6.82 us
  starting transfers between devices: 16.8 us -> 11.3 us
    all_to_all x4 -> x5, blocking collectives: 76.1 us -> 90.8 us  [exchange(): return lax.all_to_all(parts, ('ctx', 'tp'), 0, 0, axis_index_groups=lists)]
    all_to_all x2 -> x1, waiting for transfers between devices: 15.2 us -> 6.82 us  [exchange(): return lax.all_to_all(parts, ('ctx', 'tp'), 0, 0, axis_index_groups=lists)]
    all_to_all x2 -> x1, starting transfers between devices: 16.8 us -> 11.3 us  [exchange(): return lax.all_to_all(parts, ('ctx', 'tp'), 0, 0, axis_index_groups=lists)]
    pallas_call x10 -> x9, Pallas kernels: 10.5 us -> 10.3 us  [call(): pl.pallas_call(kernel, out_shape=outs, in_specs=[hbm if copied else vmem]...]
  transfers between devices with their start and end apart: 2 -> 1, of which waited for: 2 -> 1; matrix products, arithmetic and copies ran while one was open for 0% -> 0% of each run, Pallas kernels for 3% -> 3%
where the time goes in v8:
time: 136 us; the launch traced here: 135 us
  blocking collectives  105 us (77%)
  starting transfers between devices  11.3 us (8%)
  Pallas kernels  10.3 us (8%)
  waiting for transfers between devices  6.82 us (5%)
    all_to_all x5, blocking collectives, exchange(): return lax.all_to_all(parts, ('ctx', 'tp'), 0, 0, axis_index_groups=lists)  90.8 us
    all_to_all x1, blocking collectives, shards(): gathered = lax.all_to_all(sums, 'tp', 0, 0)  14.2 us
    all_to_all x1, starting transfers between devices, exchange(): return lax.all_to_all(parts, ('ctx', 'tp'), 0, 0, axis_index_groups=lists)  11.3 us
    pallas_call x9, Pallas kernels, call(): pl.pallas_call(kernel, out_shape=outs, in_specs=[hbm if copied else vmem]...  10.3 us
    all_to_all x1, waiting for transfers between devices, exchange(): return lax.all_to_all(parts, ('ctx', 'tp'), 0, 0, axis_index_groups=lists)  6.82 us
  transfers between devices with their start and end apart: 1, of which 1 were waited for; matrix products, arithmetic and copies ran while one was open for 0% of the time, Pallas kernels for 3%

profile of v8, /device:TPU:1, one launch (start us, length us, event | category | flops | bytes accessed | tf_op | source)
XLA Modules:
  0.0 134.7 jit_solution(5994495772436920142)
XLA Ops:
  0.6 2.3 %shard_map.93 = (f32[16,72,128]{2,1,0:T(8,128)S(1)}, f32[128,8]{1,0:T(8,128)S(1)}, f32[8,128]{1,0:T(8,128)S(1)}) custom-call(bf16[128,1024]{1,0:T(8,128)(2,1)} %key_ref.5, bf16[128,1024]{1,0:T(8,128)(2,1)} %value_ref.5, f32[8,128]{1,0:T(8,128)} %bitcast.10), custom_call_target="tpu_custom_call" | custom-call | flops 67108864 | bytes 1126400 | tf_op jit(solution)/shard_map/pallas_call | solution.py:328
  2.9 25.8 %all_to_all.35.piece_ref = f32[16,72,128]{2,1,0:T(8,128)S(1)} all-to-all(f32[16,72,128]{2,1,0:T(8,128)S(1)} %get-tuple-element.20), channel_id=1, replica_groups={{0,32,64,96,8,40,72,104,16,48,80,112,24,56,88,120},{128,160,192,224,136..., dimensions={0} | all-to-all | bytes 1179648 | tf_op jit(solution)/shard_map/all_to_all | solution.py:377
  28.7 0.1 shard_map.94
  28.8 20.2 %all_to_all.36.total_ref = f32[4,72,128]{2,1,0:T(8,128)S(1)} all-to-all(f32[4,72,128]{2,1,0:T(8,128)S(1)} %shard_map.94), channel_id=1, replica_groups={{0,128,320,448},{32,160,352,480},{64,192,256,384},{96,224,288,416},{8,1..., dimensions={0} | all-to-all | bytes 294912 | tf_op jit(solution)/shard_map/all_to_all | solution.py:377
  49.0 0.1 shard_map.95
  49.0 0.0 copy-start
  49.0 0.0 copy-start.1
  49.1 0.0 copy-start.2
  49.1 0.0 copy-start.3
  49.1 14.5 %all_to_all.37 = f32[16,64,128]{2,1,0:T(8,128)S(1)} all-to-all(f32[16,64,128]{2,1,0:T(8,128)S(1)} %get-tuple-element.21), channel_id=1, replica_groups={{0,32,64,96,8,40,72,104,16,48,80,112,24,56,88,120},{128,160,192,224,136..., dimensions={0} | all-to-all | bytes 1048576 | tf_op jit(solution)/shard_map/all_to_all | solution.py:377
  63.6 0.0 copy-done
  63.6 0.0 copy-done.1
  63.6 0.7 copy-done.4
  64.3 1.3 shard_map.96
  65.6 14.2 %all_to_all.38.sums_ref = f32[8,2,128]{2,1,0:T(2,128)S(1)} all-to-all(f32[8,2,128]{2,1,0:T(2,128)S(1)} %get-tuple-element.23), channel_id=1, replica_groups=mesh['ctx'=64,'tp'=8] {'tp'}, dimensions={0} | all-to-all | bytes 16384 | tf_op jit(solution)/shard_map/all_to_all | solution.py:413
  79.9 0.7 shard_map.98
  80.5 17.7 %all_to_all.39.piece_ref = f32[16,64,128]{2,1,0:T(8,128)S(1)} all-to-all(f32[16,64,128]{2,1,0:T(8,128)S(1)} %shard_map.98), channel_id=1, replica_groups={{0,32,64,96,8,40,72,104,16,48,80,112,24,56,88,120},{128,160,192,224,136..., dimensions={0} | all-to-all | bytes 1048576 | tf_op jit(solution)/shard_map/all_to_all | solution.py:377
  98.2 0.1 shard_map.99
  98.3 12.6 %all_to_all.40.total_ref = f32[4,64,128]{2,1,0:T(8,128)S(1)} all-to-all(f32[4,64,128]{2,1,0:T(8,128)S(1)} %shard_map.99), channel_id=1, replica_groups={{0,128,320,448},{32,160,352,480},{64,192,256,384},{96,224,288,416},{8,1..., dimensions={0} | all-to-all | bytes 262144 | tf_op jit(solution)/shard_map/all_to_all | solution.py:377
  110.9 0.9 shard_map.100
  111.7 11.3 %all-to-all-start.6 = ((f32[16,64,128]{2,1,0:T(8,128)}), f32[16,64,128]{2,1,0:T(8,128)S(1)}, u32[]{:S(2)}, u32[]{:S(2)}) async-start(f32[16,64,128]{2,1,0:T(8,128)} %shard_map.100), calls=%async_computation.6 | async-start | bytes 1048576 | tf_op jit(solution)/shard_map/all_to_all | solution.py:377
  123.0 3.6 %shard_map.97 = (bf16[128,1024]{1,0:T(8,128)(2,1)}, bf16[128,1024]{1,0:T(8,128)(2,1)}, f32[8,128,128]{2,1,0:T(8,128)S(1)}, f32[128,1024]{1,0:T(8,128)S(1)}) custom-call(bf16[128,1024]{1,0:T(8,128)(2,1)S(1)} %copy-done.2, bf16[128,1024]{1,0:T(8,128)(2,1)S(1)} %copy-done, ...), custom_call_target="tpu_custom_call", output_to_operand_aliasing={{2}: (5, {}), {3}: (6, {})} | custom-call | flops 436207616 | bytes 3690496 | tf_op jit(solution)/shard_map/pallas_call | solution.py:328
  126.6 6.8 %all-to-all-done.6 = f32[16,64,128]{2,1,0:T(8,128)S(1)} async-done(((f32[16,64,128]{2,1,0:T(8,128)}), f32[16,64,128]{2,1,0:T(8,128)S(1)}, u32[]{:S(2)}, u32[]{:S(2)}) %all-to-all-start.6) | async-done | bytes 524320 | tf_op jit(solution)/shard_map/all_to_all | solution.py:377
  133.4 1.4 %shard_map.101 = (bf16[128,1024]{1,0:T(8,128)(2,1)}, bf16[128,1024]{1,0:T(8,128)(2,1)}) custom-call(bf16[128,1024]{1,0:T(8,128)(2,1)S(1)} %copy-done, bf16[128,1024]{1,0:T(8,128)(2,1)S(1)} %copy-done.1, f32[128,8]{1,0:T(8,128)S(1)} %get-tuple-element.18.tall_ref, f32[8,128,128]{2,1,0:T(8,128)S(1)} %bitcast.6, ...), custom_call_target="tpu_custom_call" | custom-call | flops 134217728 | bytes 2625536 | tf_op jit(solution)/shard_map/pallas_call | solution.py:328
  (3 shorter events, 0.0 us)
Async XLA Ops:
  49.0 14.6 %copy-start = (bf16[128,1024]{1,0:T(8,128)(2,1)S(1)}, bf16[128,1024]{1,0:T(8,128)(2,1)}, u32[]{:S(2)}) copy-start(bf16[128,1024]{1,0:T(8,128)(2,1)} %key_ref.5) | copy-start | bytes 786436
  49.0 14.6 %copy-start.1 = (bf16[128,1024]{1,0:T(8,128)(2,1)S(1)}, bf16[128,1024]{1,0:T(8,128)(2,1)}, u32[]{:S(2)}) copy-start(bf16[128,1024]{1,0:T(8,128)(2,1)} %value_ref.5) | copy-start | bytes 786436
  49.1 14.6 %copy-start.2 = (bf16[128,1024]{1,0:T(8,128)(2,1)S(1)}, bf16[128,1024]{1,0:T(8,128)(2,1)}, u32[]{:S(2)}) copy-start(bf16[128,1024]{1,0:T(8,128)(2,1)} %query_ref.5) | copy-start | bytes 786436
  49.1 14.6 %copy-start.3 = (bf16[128,1024]{1,0:T(8,128)(2,1)S(1)}, bf16[128,1024]{1,0:T(8,128)(2,1)}, u32[]{:S(2)}) copy-start(bf16[128,1024]{1,0:T(8,128)(2,1)} %grad_ref.5) | copy-start | bytes 786436
  63.6 0.7 copy-start.4
  111.7 21.7 %all-to-all-start.6 = ((f32[16,64,128]{2,1,0:T(8,128)}), f32[16,64,128]{2,1,0:T(8,128)S(1)}, u32[]{:S(2)}, u32[]{:S(2)}) async-start(f32[16,64,128]{2,1,0:T(8,128)} %shard_map.100), calls=%async_computation.6 | async-start | bytes 1048576 | tf_op jit(solution)/shard_map/all_to_all | solution.py:377

commit v9 on v7

--- a/solution.py
+++ b/solution.py
@@ -23,15 +23,14 @@
 
 
 def product(left, right, dims):
+    (left_axes, right_axes), _ = dims
     lefts = halves(left) if left.dtype == f32 else (left,)
     rights = halves(right) if right.dtype == f32 else (right,)
-    total = None
-    for i, a in enumerate(lefts):
-        for j, b in enumerate(rights):
-            if i + j < 2:
-                term = lax.dot_general(a, b, dims, preferred_element_type=f32)
-                total = term if total is None else total + term
-    return total
+    pairs = [(a, b) for i, a in enumerate(lefts) for j, b in enumerate(rights) if i + j < 2]
+    if len(pairs) > 1:
+        left = jnp.concatenate([a for a, _ in pairs], axis=left_axes[0])
+        right = jnp.concatenate([b for _, b in pairs], axis=right_axes[0])
+    return lax.dot_general(left, right, dims, preferred_element_type=f32)
 
 
 def decays(log_decay):
@@ -113,7 +112,7 @@
     return (gain[None] * state.reshape(-1, 8, state.shape[-1])).reshape(state.shape)
 
 
-def group_kernel(members, copies, rows, piece_ref, out_ref):
+def group_kernel(members, rows, piece_ref, out_ref):
     _, _, cut = whereabouts(members // 2)
     total = jnp.zeros((rows, piece_ref.shape[-1]), f32)
     whole = jnp.zeros((8, piece_ref.shape[-1]), f32)
@@ -125,24 +124,23 @@
         mark = piece_ref[place, rows:, :]
         total = times(jnp.exp(mark), total) + piece_ref[place, :rows, :]
         whole = whole + mark
-    total = jnp.where(cut, early, total)
-    for copy in range(copies):
-        out_ref[copy, :rows, :] = total
-        out_ref[copy, rows:, :] = whole
-
-
-def spread_kernel(members, groups, rows, piece_ref, total_ref, out_ref, near_ref, far_ref):
+    out_ref[:rows, :] = jnp.where(cut, early, total)
+    out_ref[rows:, :] = whole
+
+
+def spread_kernel(members, rows, piece_ref, own_ref, *refs):
+    *total_refs, out_ref, near_ref, far_ref = refs
     mine, shift, cut = whereabouts(members // 2)
-    first = jnp.where(shift > 0, groups - 1, 0)
-    before = jnp.where(cut, 0, mine + jnp.where(shift > 0, 1, 0))
-    every = jnp.zeros((rows, piece_ref.shape[-1]), f32)
-    running = every
-    for step in range(groups):
-        group = (step + first) & (groups - 1)
-        gain = jnp.exp(total_ref[group, rows:, :])
-        far_ref[group] = gain
-        every = times(gain, every) + total_ref[group, :rows, :]
-        running = jnp.where(step < before, every, running)
+    before = mine + jnp.where(shift > 0, 1, 0)
+    nothing = jnp.zeros((rows, piece_ref.shape[-1]), f32)
+    every = jnp.where(cut, own_ref[:rows, :], nothing)
+    for distance in range(len(total_refs), 0, -1):
+        total_ref = total_refs[distance - 1]
+        gain = jnp.exp(total_ref[rows:, :])
+        far_ref[distance] = gain
+        longer = times(gain, every) + total_ref[:rows, :]
+        every = jnp.where(jnp.logical_or(cut, distance <= before), longer, every)
+    running = jnp.where(cut, nothing, every)
     for member in range(members):
         if member == members // 2:
             running = jnp.where(cut, every, running)
@@ -153,7 +151,7 @@
         running = times(gain, running) + piece_ref[place, :rows, :]
 
 
-def back_group_kernel(members, copies, piece_ref, near_ref, out_ref):
+def back_group_kernel(members, piece_ref, near_ref, out_ref):
     _, _, cut = whereabouts(members // 2)
     total = jnp.zeros(piece_ref.shape[1:], f32)
     late = total
@@ -162,18 +160,19 @@
         total = times(near_ref[place], total) + piece_ref[place]
         if member == members // 2:
             late = total
-    total = jnp.where(cut, late, total)
-    for copy in range(copies):
-        out_ref[copy] = total
-
-
-def back_spread_kernel(members, groups, piece_ref, near_ref, total_ref, far_ref, out_ref):
+    out_ref[...] = jnp.where(cut, late, total)
+
+
+def back_spread_kernel(members, piece_ref, near_ref, far_ref, own_ref, *refs):
+    *total_refs, out_ref = refs
+    groups = len(total_refs) + 1
     mine, _, cut = whereabouts(members // 2)
-    every = jnp.zeros(piece_ref.shape[1:], f32)
-    running = every
-    for group in reversed(range(groups)):
-        every = times(far_ref[group], every) + total_ref[group]
-        running = jnp.where(group > mine, every, running)
+    nothing = jnp.zeros(piece_ref.shape[1:], f32)
+    every = jnp.where(cut, own_ref[...], nothing)
+    for distance in range(groups - 1, 0, -1):
+        longer = times(far_ref[groups - distance], every) + total_refs[distance - 1][...]
+        every = jnp.where(jnp.logical_or(cut, distance < groups - mine), longer, every)
+    running = jnp.where(cut, nothing, every)
     for member in reversed(range(members)):
         place = rank(member, cut)
         out_ref[place] = running
@@ -349,6 +348,16 @@
     def exchange(parts, lists):
         return lax.all_to_all(parts, ("ctx", "tp"), 0, 0, axis_index_groups=lists)
 
+    def passed_on(total, way):
+        return [
+            lax.ppermute(
+                total,
+                ("ctx", "tp"),
+                [(line[g], line[(g + way * distance) % groups]) for line in far for g in range(groups)],
+            )
+            for distance in range(1, groups)
+        ]
+
     states, tall, across = call(
         bind(states_kernel, heads, members),
         [shape((members, rows + 8, size), f32), shape((tok_rows, heads), f32), shape((heads, tok_rows), f32)],
@@ -359,17 +368,16 @@
         copied=(key_rows, value_rows, log_decay),
     )
     pieces = exchange(states, near)
-    (total,) = call(
-        bind(group_kernel, members, groups, rows), [shape((groups, rows + 8, size), f32)], pieces
-    )
+    (total,) = call(bind(group_kernel, members, rows), [shape((rows + 8, size), f32)], pieces)
     (inside,) = call(
         bind(inside_kernel, heads), [wide], queries, key_rows, value_rows, tall, across, flops=3 * unit
     )
     entering, near_gains, far_gains = call(
-        bind(spread_kernel, members, groups, rows),
+        bind(spread_kernel, members, rows),
         [shape((members, rows, size), f32), shape((members, 8, size), f32), shape((groups, 8, size), f32)],
         pieces,
-        exchange(total, far),
+        total,
+        *passed_on(total, 1),
     )
     entry = exchange(entering, near).reshape(heads, size, size)
     mixed, sums = call(
@@ -398,18 +406,19 @@
     )
     back_pieces = exchange(back, near)
     (back_total,) = call(
-        bind(back_group_kernel, members, groups),
-        [shape((groups, rows, size), f32)],
+        bind(back_group_kernel, members),
+        [shape((rows, size), f32)],
         back_pieces,
         near_gains,
     )
     (returning,) = call(
-        bind(back_spread_kernel, members, groups),
+        bind(back_spread_kernel, members),
         [shape((members, rows, size), f32)],
         back_pieces,
         near_gains,
-        exchange(back_total, far),
         far_gains,
+        back_total,
+        *passed_on(back_total, -1),
     )
     leaving = exchange(returning, near).reshape(heads, size, size)
     normed, grad_q, near_k, near_v = call(

time: 136 us -> 142 us (1.044)
  blocking collectives: 90.6 us -> 54.2 us
  starting transfers between devices: 16.8 us -> 53 us
  waiting for transfers between devices: 15.2 us -> 22.3 us
    ppermute x0 -> x6, starting transfers between devices: none -> 36.8 us  [passed_on(): lax.ppermute(total, ('ctx', 'tp'), [(line[g], line[(g + way * distance) %...]
    all_to_all x4 -> x2, blocking collectives: 76.1 us -> 43.8 us  [exchange(): return lax.all_to_all(parts, ('ctx', 'tp'), 0, 0, axis_index_groups=lists)]
    ppermute x0 -> x6, waiting for transfers between devices: none -> 6.62 us  [passed_on(): lax.ppermute(total, ('ctx', 'tp'), [(line[g], line[(g + way * distance) %...]
    all_to_all x1, blocking collectives: 14.5 us -> 10.4 us  [shards(): gathered = lax.all_to_all(sums, 'tp', 0, 0)]
  transfers between devices with their start and end apart: 2 -> 8, of which waited for: 2 -> 4; matrix products, arithmetic and copies ran while one was open for 0% -> 0% of each run, Pallas kernels for 3% -> 3%
where the time goes in v9:
time: 142 us; the launch traced here: 141 us
  blocking collectives  54.2 us (38%)
  starting transfers between devices  53 us (37%)
  waiting for transfers between devices  22.3 us (16%)
  Pallas kernels  11 us (8%)
    all_to_all x2, blocking collectives, exchange(): return lax.all_to_all(parts, ('ctx', 'tp'), 0, 0, axis_index_groups=lists)  43.8 us
    ppermute x6, starting transfers between devices, passed_on(): lax.ppermute(total, ('ctx', 'tp'), [(line[g], line[(g + way * distance) %...  36.8 us
    all_to_all x2, starting transfers between devices, exchange(): return lax.all_to_all(parts, ('ctx', 'tp'), 0, 0, axis_index_groups=lists)  16.2 us
    all_to_all x2, waiting for transfers between devices, exchange(): return lax.all_to_all(parts, ('ctx', 'tp'), 0, 0, axis_index_groups=lists)  15.7 us
    pallas_call x10, Pallas kernels, call(): pl.pallas_call(kernel, out_shape=outs, in_specs=[hbm if copied else vmem]...  11 us
    all_to_all x1, blocking collectives, shards(): gathered = lax.all_to_all(sums, 'tp', 0, 0)  10.4 us
    ppermute x6, waiting for transfers between devices, passed_on(): lax.ppermute(total, ('ctx', 'tp'), [(line[g], line[(g + way * distance) %...  6.62 us
  transfers between devices with their start and end apart: 8, of which 4 were waited for; matrix products, arithmetic and copies ran while one was open for 0% of the time, Pallas kernels for 3%

profile of v9, /device:TPU:1, one launch (start us, length us, event | category | flops | bytes accessed | tf_op | source)
XLA Modules:
  0.0 141.3 jit_solution(10627648708792843429)
XLA Ops:
  0.6 1.8 %shard_map.93 = (f32[16,72,128]{2,1,0:T(8,128)S(1)}, f32[128,8]{1,0:T(8,128)S(1)}, f32[8,128]{1,0:T(8,128)S(1)}) custom-call(bf16[128,1024]{1,0:T(8,128)(2,1)} %key_ref.5, bf16[128,1024]{1,0:T(8,128)(2,1)} %value_ref.5, f32[8,128]{1,0:T(8,128)} %bitcast.10), custom_call_target="tpu_custom_call" | custom-call | flops 67108864 | bytes 1126400 | tf_op jit(solution)/shard_map/pallas_call | solution.py:300
  2.4 25.8 %all_to_all.25.piece_ref = f32[16,72,128]{2,1,0:T(8,128)S(1)} all-to-all(f32[16,72,128]{2,1,0:T(8,128)S(1)} %get-tuple-element.20), channel_id=1, replica_groups={{0,32,64,96,8,40,72,104,16,48,80,112,24,56,88,120},{128,160,192,224,136..., dimensions={0} | all-to-all | bytes 1179648 | tf_op jit(solution)/shard_map/all_to_all | solution.py:349
  28.2 0.1 shard_map.94.own_ref
  28.3 8.4 %collective-permute-start.2 = (f32[72,128]{1,0:T(8,128)S(1)}, f32[72,128]{1,0:T(8,128)S(1)}, u32[]{:S(2)}, u32[]{:S(2)}) collective-permute-start(f32[72,128]{1,0:T(8,128)S(1)} %shard_map.94.own_ref), channel_id=1, source_target_pairs={{0,448},{128,0},{320,128},{448,320},{32,480},{160,32},{352,160},{4... | collective-permute-start | bytes 110600 | tf_op jit(solution)/shard_map/ppermute | solution.py:353
  36.7 4.9 %collective-permute-start.1 = (f32[72,128]{1,0:T(8,128)S(1)}, f32[72,128]{1,0:T(8,128)S(1)}, u32[]{:S(2)}, u32[]{:S(2)}) collective-permute-start(f32[72,128]{1,0:T(8,128)S(1)} %shard_map.94.own_ref), channel_id=1, source_target_pairs={{0,320},{128,448},{320,0},{448,128},{32,352},{160,480},{352,32},{4... | collective-permute-start | bytes 110600 | tf_op jit(solution)/shard_map/ppermute | solution.py:353
  41.6 7.3 %collective-permute-start = (f32[72,128]{1,0:T(8,128)S(1)}, f32[72,128]{1,0:T(8,128)S(1)}, u32[]{:S(2)}, u32[]{:S(2)}) collective-permute-start(f32[72,128]{1,0:T(8,128)S(1)} %shard_map.94.own_ref), channel_id=1, source_target_pairs={{0,128},{128,320},{320,448},{448,0},{32,160},{160,352},{352,480},{... | collective-permute-start | bytes 110600 | tf_op jit(solution)/shard_map/ppermute | solution.py:353
  48.9 4.0 %collective-permute-done.refs_0_ = f32[72,128]{1,0:T(8,128)S(1)} collective-permute-done((f32[72,128]{1,0:T(8,128)S(1)}, f32[72,128]{1,0:T(8,128)S(1)}, u32[]{:S(2)}, u32[]{:S(2)}) %collective-permute-start) | collective-permute-done | bytes 36896 | tf_op jit(solution)/shard_map/ppermute | solution.py:353
  52.9 0.9 shard_map.95
  53.8 5.6 %all-to-all-start.1 = ((f32[16,64,128]{2,1,0:T(8,128)}), f32[16,64,128]{2,1,0:T(8,128)S(1)}, u32[]{:S(2)}, u32[]{:S(2)}) async-start(f32[16,64,128]{2,1,0:T(8,128)} %get-tuple-element.21), calls=%async_computation.1 | async-start | bytes 1048576 | tf_op jit(solution)/shard_map/all_to_all | solution.py:349
  59.4 1.4 shard_map.96.inside_ref
  60.8 9.0 %all-to-all-done.1 = f32[16,64,128]{2,1,0:T(8,128)S(1)} async-done(((f32[16,64,128]{2,1,0:T(8,128)}), f32[16,64,128]{2,1,0:T(8,128)S(1)}, u32[]{:S(2)}, u32[]{:S(2)}) %all-to-all-start.1) | async-done | bytes 524320 | tf_op jit(solution)/shard_map/all_to_all | solution.py:349
  69.8 0.6 shard_map.97
  70.4 10.4 %all_to_all.26.sums_ref = f32[8,2,128]{2,1,0:T(2,128)S(1)} all-to-all(f32[8,2,128]{2,1,0:T(2,128)S(1)} %get-tuple-element.23), channel_id=1, replica_groups=mesh['ctx'=64,'tp'=8] {'tp'}, dimensions={0} | all-to-all | bytes 16384 | tf_op jit(solution)/shard_map/all_to_all | solution.py:394
  80.8 0.7 shard_map.99
  81.5 18.0 %all_to_all.27.piece_ref = f32[16,64,128]{2,1,0:T(8,128)S(1)} all-to-all(f32[16,64,128]{2,1,0:T(8,128)S(1)} %shard_map.99), channel_id=1, replica_groups={{0,32,64,96,8,40,72,104,16,48,80,112,24,56,88,120},{128,160,192,224,136..., dimensions={0} | all-to-all | bytes 1048576 | tf_op jit(solution)/shard_map/all_to_all | solution.py:349
  99.5 4.0 %collective-permute-start.5 = (f32[64,128]{1,0:T(8,128)S(1)}, f32[64,128]{1,0:T(8,128)S(1)}, u32[]{:S(2)}, u32[]{:S(2)}) collective-permute-start(f32[64,128]{1,0:T(8,128)S(1)} %shard_map.100.own_ref), channel_id=1, source_target_pairs={{0,128},{128,320},{320,448},{448,0},{32,160},{160,352},{352,480},{... | collective-permute-start | bytes 98312 | tf_op jit(solution)/shard_map/ppermute | solution.py:353
  103.6 9.3 %collective-permute-start.4 = (f32[64,128]{1,0:T(8,128)S(1)}, f32[64,128]{1,0:T(8,128)S(1)}, u32[]{:S(2)}, u32[]{:S(2)}) collective-permute-start(f32[64,128]{1,0:T(8,128)S(1)} %shard_map.100.own_ref), channel_id=1, source_target_pairs={{0,320},{128,448},{320,0},{448,128},{32,352},{160,480},{352,32},{4... | collective-permute-start | bytes 98312 | tf_op jit(solution)/shard_map/ppermute | solution.py:353
  112.9 3.0 %collective-permute-start.3 = (f32[64,128]{1,0:T(8,128)S(1)}, f32[64,128]{1,0:T(8,128)S(1)}, u32[]{:S(2)}, u32[]{:S(2)}) collective-permute-start(f32[64,128]{1,0:T(8,128)S(1)} %shard_map.100.own_ref), channel_id=1, source_target_pairs={{0,448},{128,0},{320,128},{448,320},{32,480},{160,32},{352,160},{4... | collective-permute-start | bytes 98312 | tf_op jit(solution)/shard_map/ppermute | solution.py:353
  115.8 2.6 %collective-permute-done.3.refs_0_ = f32[64,128]{1,0:T(8,128)S(1)} collective-permute-done((f32[64,128]{1,0:T(8,128)S(1)}, f32[64,128]{1,0:T(8,128)S(1)}, u32[]{:S(2)}, u32[]{:S(2)}) %collective-permute-start.3) | collective-permute-done | bytes 32800 | tf_op jit(solution)/shard_map/ppermute | solution.py:353
  118.4 0.9 shard_map.101
  119.3 10.6 %all-to-all-start.4 = ((f32[16,64,128]{2,1,0:T(8,128)}), f32[16,64,128]{2,1,0:T(8,128)S(1)}, u32[]{:S(2)}, u32[]{:S(2)}) async-start(f32[16,64,128]{2,1,0:T(8,128)} %shard_map.101), calls=%async_computation.4 | async-start | bytes 1048576 | tf_op jit(solution)/shard_map/all_to_all | solution.py:349
  129.9 3.4 %shard_map.98 = (bf16[128,1024]{1,0:T(8,128)(2,1)}, bf16[128,1024]{1,0:T(8,128)(2,1)}, f32[8,128,128]{2,1,0:T(8,128)S(1)}, f32[128,1024]{1,0:T(8,128)S(1)}) custom-call(bf16[128,1024]{1,0:T(8,128)(2,1)S(1)} %copy-done, bf16[128,1024]{1,0:T(8,128)(2,1)S(1)} %copy-done.1, ...), custom_call_target="tpu_custom_call", output_to_operand_aliasing={{2}: (5, {}), {3}: (6, {})} | custom-call | flops 436207616 | bytes 3690496 | tf_op jit(solution)/shard_map/pallas_call | solution.py:300
  133.3 6.8 %all-to-all-done.4 = f32[16,64,128]{2,1,0:T(8,128)S(1)} async-done(((f32[16,64,128]{2,1,0:T(8,128)}), f32[16,64,128]{2,1,0:T(8,128)S(1)}, u32[]{:S(2)}, u32[]{:S(2)}) %all-to-all-start.4) | async-done | bytes 524320 | tf_op jit(solution)/shard_map/all_to_all | solution.py:349
  140.0 1.2 shard_map.102
  (15 shorter events, 0.1 us)
Async XLA Ops:
  28.3 20.6 %collective-permute-start.2 = (f32[72,128]{1,0:T(8,128)S(1)}, f32[72,128]{1,0:T(8,128)S(1)}, u32[]{:S(2)}, u32[]{:S(2)}) collective-permute-start(f32[72,128]{1,0:T(8,128)S(1)} %shard_map.94.own_ref), channel_id=1, source_target_pairs={{0,448},{128,0},{320,128},{448,320},{32,480},{160,32},{352,160},{4... | collective-permute-start | bytes 110600 | tf_op jit(solution)/shard_map/ppermute | solution.py:353
  36.7 12.2 %collective-permute-start.1 = (f32[72,128]{1,0:T(8,128)S(1)}, f32[72,128]{1,0:T(8,128)S(1)}, u32[]{:S(2)}, u32[]{:S(2)}) collective-permute-start(f32[72,128]{1,0:T(8,128)S(1)} %shard_map.94.own_ref), channel_id=1, source_target_pairs={{0,320},{128,448},{320,0},{448,128},{32,352},{160,480},{352,32},{4... | collective-permute-start | bytes 110600 | tf_op jit(solution)/shard_map/ppermute | solution.py:353
  41.6 11.3 %collective-permute-start = (f32[72,128]{1,0:T(8,128)S(1)}, f32[72,128]{1,0:T(8,128)S(1)}, u32[]{:S(2)}, u32[]{:S(2)}) collective-permute-start(f32[72,128]{1,0:T(8,128)S(1)} %shard_map.94.own_ref), channel_id=1, source_target_pairs={{0,128},{128,320},{320,448},{448,0},{32,160},{160,352},{352,480},{... | collective-permute-start | bytes 110600 | tf_op jit(solution)/shard_map/ppermute | solution.py:353
  53.8 5.6 %copy-start = (bf16[128,1024]{1,0:T(8,128)(2,1)S(1)}, bf16[128,1024]{1,0:T(8,128)(2,1)}, u32[]{:S(2)}) copy-start(bf16[128,1024]{1,0:T(8,128)(2,1)} %query_ref.7) | copy-start | bytes 786436
  53.8 5.6 %copy-start.1 = (bf16[128,1024]{1,0:T(8,128)(2,1)S(1)}, bf16[128,1024]{1,0:T(8,128)(2,1)}, u32[]{:S(2)}) copy-start(bf16[128,1024]{1,0:T(8,128)(2,1)} %key_ref.5) | copy-start | bytes 786436
  53.8 5.6 %copy-start.2 = (bf16[128,1024]{1,0:T(8,128)(2,1)S(1)}, bf16[128,1024]{1,0:T(8,128)(2,1)}, u32[]{:S(2)}) copy-start(bf16[128,1024]{1,0:T(8,128)(2,1)} %value_ref.5) | copy-start | bytes 786436
  53.8 16.0 %all-to-all-start.1 = ((f32[16,64,128]{2,1,0:T(8,128)}), f32[16,64,128]{2,1,0:T(8,128)S(1)}, u32[]{:S(2)}, u32[]{:S(2)}) async-start(f32[16,64,128]{2,1,0:T(8,128)} %get-tuple-element.21), calls=%async_computation.1 | async-start | bytes 1048576 | tf_op jit(solution)/shard_map/all_to_all | solution.py:349
  59.4 10.4 %copy-start.3 = (bf16[128,1024]{1,0:T(8,128)(2,1)S(1)}, bf16[128,1024]{1,0:T(8,128)(2,1)}, u32[]{:S(2)}) copy-start(bf16[128,1024]{1,0:T(8,128)(2,1)} %grad_ref.5) | copy-start | bytes 786436
  59.4 10.4 %copy-start.4 = (f32[1024]{0:T(1024)S(1)}, f32[1024]{0:T(1024)}, u32[]{:S(2)}) copy-start(f32[1024]{0:T(1024)} %param.10) | copy-start | bytes 12292
  99.5 16.3 %collective-permute-start.5 = (f32[64,128]{1,0:T(8,128)S(1)}, f32[64,128]{1,0:T(8,128)S(1)}, u32[]{:S(2)}, u32[]{:S(2)}) collective-permute-start(f32[64,128]{1,0:T(8,128)S(1)} %shard_map.100.own_ref), channel_id=1, source_target_pairs={{0,128},{128,320},{320,448},{448,0},{32,160},{160,352},{352,480},{... | collective-permute-start | bytes 98312 | tf_op jit(solution)/shard_map/ppermute | solution.py:353
  103.6 12.2 %collective-permute-start.4 = (f32[64,128]{1,0:T(8,128)S(1)}, f32[64,128]{1,0:T(8,128)S(1)}, u32[]{:S(2)}, u32[]{:S(2)}) collective-permute-start(f32[64,128]{1,0:T(8,128)S(1)} %shard_map.100.own_ref), channel_id=1, source_target_pairs={{0,320},{128,448},{320,0},{448,128},{32,352},{160,480},{352,32},{4... | collective-permute-start | bytes 98312 | tf_op jit(solution)/shard_map/ppermute | solution.py:353
  112.9 5.6 %collective-permute-start.3 = (f32[64,128]{1,0:T(8,128)S(1)}, f32[64,128]{1,0:T(8,128)S(1)}, u32[]{:S(2)}, u32[]{:S(2)}) collective-permute-start(f32[64,128]{1,0:T(8,128)S(1)} %shard_map.100.own_ref), channel_id=1, source_target_pairs={{0,448},{128,0},{320,128},{448,320},{32,480},{160,32},{352,160},{4... | collective-permute-start | bytes 98312 | tf_op jit(solution)/shard_map/ppermute | solution.py:353
  119.3 20.8 %all-to-all-start.4 = ((f32[16,64,128]{2,1,0:T(8,128)}), f32[16,64,128]{2,1,0:T(8,128)S(1)}, u32[]{:S(2)}, u32[]{:S(2)}) async-start(f32[16,64,128]{2,1,0:T(8,128)} %shard_map.101), calls=%async_computation.4 | async-start | bytes 1048576 | tf_op jit(solution)/shard_map/all_to_all | solution.py:349

commit v10 on v7

--- a/solution.py
+++ b/solution.py
@@ -22,15 +22,19 @@
     return high, (wide - high.astype(f32)).astype(bf16)
 
 
-def product(left, right, dims):
+def product(left, right, dims, deep=False):
+    (left_axes, right_axes), _ = dims
     lefts = halves(left) if left.dtype == f32 else (left,)
     rights = halves(right) if right.dtype == f32 else (right,)
+    pairs = [(a, b) for i, a in enumerate(lefts) for j, b in enumerate(rights) if i + j < 2]
+    if deep and len(pairs) > 1:
+        left = jnp.concatenate([a for a, _ in pairs], axis=left_axes[0])
+        right = jnp.concatenate([b for _, b in pairs], axis=right_axes[0])
+        pairs = [(left, right)]
     total = None
-    for i, a in enumerate(lefts):
-        for j, b in enumerate(rights):
-            if i + j < 2:
-                term = lax.dot_general(a, b, dims, preferred_element_type=f32)
-                total = term if total is None else total + term
+    for a, b in pairs:
+        term = lax.dot_general(a, b, dims, preferred_element_type=f32)
+        total = term if total is None else total + term
     return total
 
 
@@ -64,12 +68,14 @@
 
 
 def turned(head, heads):
+    group, shift, _ = whereabouts(heads)
     half = lax.axis_size("ctx") // (2 * heads) // 2
-    return head ^ jnp.where(whereabouts(heads)[0] < half, 0, 1)
-
-
-def rank(member, cut):
-    return member % 4 * 4 + ((member // 4) ^ jnp.where(cut, 2, 0))
+    return head ^ jnp.where(group < half, 0, jnp.where(shift > 0, 4, 1))
+
+
+def rank(member, shift, cut):
+    x, z = member % 4, (member // 4) ^ jnp.where(cut, 2, 0)
+    return jnp.where(shift > 0, z * 4 + x, x * 4 + z)
 
 
 def cols(head, size):
@@ -114,14 +120,14 @@
 
 
 def group_kernel(members, copies, rows, piece_ref, out_ref):
-    _, _, cut = whereabouts(members // 2)
+    _, shift, cut = whereabouts(members // 2)
     total = jnp.zeros((rows, piece_ref.shape[-1]), f32)
     whole = jnp.zeros((8, piece_ref.shape[-1]), f32)
     early = total
     for member in range(members):
         if member == members // 2:
             early = total
-        place = rank(member, cut)
+        place = rank(member, shift, cut)
         mark = piece_ref[place, rows:, :]
         total = times(jnp.exp(mark), total) + piece_ref[place, :rows, :]
         whole = whole + mark
@@ -146,7 +152,7 @@
     for member in range(members):
         if member == members // 2:
             running = jnp.where(cut, every, running)
-        place = rank(member, cut)
+        place = rank(member, shift, cut)
         gain = jnp.exp(piece_ref[place, rows:, :])
         near_ref[place] = gain
         out_ref[place] = running
@@ -154,11 +160,11 @@
 
 
 def back_group_kernel(members, copies, piece_ref, near_ref, out_ref):
-    _, _, cut = whereabouts(members // 2)
+    _, shift, cut = whereabouts(members // 2)
     total = jnp.zeros(piece_ref.shape[1:], f32)
     late = total
     for member in reversed(range(members)):
-        place = rank(member, cut)
+        place = rank(member, shift, cut)
         total = times(near_ref[place], total) + piece_ref[place]
         if member == members // 2:
             late = total
@@ -168,14 +174,14 @@
 
 
 def back_spread_kernel(members, groups, piece_ref, near_ref, total_ref, far_ref, out_ref):
-    mine, _, cut = whereabouts(members // 2)
+    mine, shift, cut = whereabouts(members // 2)
     every = jnp.zeros(piece_ref.shape[1:], f32)
     running = every
     for group in reversed(range(groups)):
         every = times(far_ref[group], every) + total_ref[group]
         running = jnp.where(group > mine, every, running)
     for member in reversed(range(members)):
-        place = rank(member, cut)
+        place = rank(member, shift, cut)
         out_ref[place] = running
         running = times(near_ref[place], running) + piece_ref[place]
         if member == members // 2:
@@ -268,13 +274,13 @@
         normed_ref[:, here] = (mixed * scale * gain).astype(bf16)
         slope = scale * (grad_ref[:, here].astype(f32) * gain) - pull * mixed
         weights = weights_of(tall, wide, head)
-        scores = product(query, key, NT) * weights
-        grad_scores = product(slope, value, NT) * weights
+        scores = product(query, key, NT, True) * weights
+        grad_scores = product(slope, value, NT, True) * weights
         there = turned(head, heads)
-        outer = product(slope, state_ref[there], NT) * rising[:, head : head + 1]
-        grad_q_ref[:, here] = (product(grad_scores, key, NN) + outer).astype(bf16)
-        near_k_ref[there] = product(grad_scores, query, TN)
-        near_v_ref[:, here] = product(scores, slope, TN)
+        outer = product(slope, state_ref[there], NT, True) * rising[:, head : head + 1]
+        grad_q_ref[:, here] = (product(grad_scores, key, NN, True) + outer).astype(bf16)
+        near_k_ref[there] = product(grad_scores, query, TN, True)
+        near_v_ref[:, here] = product(scores, slope, TN, True)
 
 
 def far_kernel(heads, key_ref, value_ref, tall_ref, state_ref, near_k_ref, near_v_ref, grad_k_ref, grad_v_ref):
@@ -286,8 +292,8 @@
         late = trailing[:, head : head + 1]
         there = turned(head, heads)
         state = state_ref[there]
-        grad_k = near_k_ref[there] + product(value_ref[:, here], state, NT) * late
-        grad_v = near_v_ref[:, here] + product(key_ref[:, here], state, NN) * late
+        grad_k = near_k_ref[there] + product(value_ref[:, here], state, NT, True) * late
+        grad_v = near_v_ref[:, here] + product(key_ref[:, here], state, NN, True) * late
         grad_k_ref[:, here] = grad_k.astype(bf16)
         grad_v_ref[:, here] = grad_v.astype(bf16)
 
@@ -320,14 +326,17 @@
         shift = index % 2 * (span // 2)
 
         def device(group, place):
-            z = (group * span + shift + place % 4) % (count // 4)
-            return (z * 4 + place // 4) * tp + index
+            x, z = (place % 4, place // 4) if shift else (place // 4, place % 4)
+            return ((group * span + shift + z) % (count // 4) * 4 + x) * tp + index
 
         for group in range(groups):
             near.append([device(group, place) for place in range(members)])
         for piece in range(members):
             far.append(
-                [device(group, piece ^ (2 if group >= groups // 2 else 0)) for group in range(groups)]
+                [
+                    device(group, piece ^ ((8 if shift else 2) if group >= groups // 2 else 0))
+                    for group in range(groups)
+                ]
             )
     return groups, members, near, far
 

time: 136 us -> 137 us (level)
  waiting for transfers between devices: 15.2 us -> 18 us
  starting transfers between devices: 16.8 us -> 14.4 us
  blocking collectives: 90.6 us -> 92.3 us
    all_to_all x4, blocking collectives: 76.1 us -> 79.8 us  [exchange(): return lax.all_to_all(parts, ('ctx', 'tp'), 0, 0, axis_index_groups=lists)]
    all_to_all x2, waiting for transfers between devices: 15.2 us -> 18 us  [exchange(): return lax.all_to_all(parts, ('ctx', 'tp'), 0, 0, axis_index_groups=lists)]
    all_to_all x2, starting transfers between devices: 16.8 us -> 14.4 us  [exchange(): return lax.all_to_all(parts, ('ctx', 'tp'), 0, 0, axis_index_groups=lists)]
    all_to_all x1, blocking collectives: 14.5 us -> 12.5 us  [shards(): gathered = lax.all_to_all(sums, 'tp', 0, 0)]
where the time goes in v10:
time: 137 us; the launch traced here: 136 us
  blocking collectives  92.3 us (67%)
  waiting for transfers between devices  18 us (13%)
  starting transfers between devices  14.4 us (11%)
  Pallas kernels  10.1 us (7%)
    all_to_all x4, blocking collectives, exchange(): return lax.all_to_all(parts, ('ctx', 'tp'), 0, 0, axis_index_groups=lists)  79.8 us
    all_to_all x2, waiting for transfers between devices, exchange(): return lax.all_to_all(parts, ('ctx', 'tp'), 0, 0, axis_index_groups=lists)  18 us
    all_to_all x2, starting transfers between devices, exchange(): return lax.all_to_all(parts, ('ctx', 'tp'), 0, 0, axis_index_groups=lists)  14.4 us
    all_to_all x1, blocking collectives, shards(): gathered = lax.all_to_all(sums, 'tp', 0, 0)  12.5 us
    pallas_call x10, Pallas kernels, call(): pl.pallas_call(kernel, out_shape=outs, in_specs=[hbm if copied else vmem]...  10.1 us
  transfers between devices with their start and end apart: 2, of which 2 were waited for; matrix products, arithmetic and copies ran while one was open for 0% of the time, Pallas kernels for 3%

profile of v10, /device:TPU:1, one launch (start us, length us, event | category | flops | bytes accessed | tf_op | source)
XLA Modules:
  0.0 135.5 jit_solution(3773251933879751902)
XLA Ops:
  0.6 1.7 %shard_map.93 = (f32[16,72,128]{2,1,0:T(8,128)S(1)}, f32[128,8]{1,0:T(8,128)S(1)}, f32[8,128]{1,0:T(8,128)S(1)}) custom-call(bf16[128,1024]{1,0:T(8,128)(2,1)} %key_ref.5, bf16[128,1024]{1,0:T(8,128)(2,1)} %value_ref.5, f32[8,128]{1,0:T(8,128)} %bitcast.10), custom_call_target="tpu_custom_call" | custom-call | flops 67108864 | bytes 1126400 | tf_op jit(solution)/shard_map/pallas_call | solution.py:307
  2.4 26.2 %all_to_all.35.piece_ref = f32[16,72,128]{2,1,0:T(8,128)S(1)} all-to-all(f32[16,72,128]{2,1,0:T(8,128)S(1)} %get-tuple-element.20), channel_id=1, replica_groups={{0,32,64,96,8,40,72,104,16,48,80,112,24,56,88,120},{128,160,192,224,136..., dimensions={0} | all-to-all | bytes 1179648 | tf_op jit(solution)/shard_map/all_to_all | solution.py:359
  28.5 0.1 shard_map.94
  28.6 20.5 %all_to_all.36.total_ref = f32[4,72,128]{2,1,0:T(8,128)S(1)} all-to-all(f32[4,72,128]{2,1,0:T(8,128)S(1)} %shard_map.94), channel_id=1, replica_groups={{0,128,320,448},{32,160,352,480},{64,192,256,384},{96,224,288,416},{8,1..., dimensions={0} | all-to-all | bytes 294912 | tf_op jit(solution)/shard_map/all_to_all | solution.py:359
  49.1 0.9 shard_map.95
  50.0 5.9 %all-to-all-start.2 = ((f32[16,64,128]{2,1,0:T(8,128)}), f32[16,64,128]{2,1,0:T(8,128)S(1)}, u32[]{:S(2)}, u32[]{:S(2)}) async-start(f32[16,64,128]{2,1,0:T(8,128)} %get-tuple-element.21), calls=%async_computation.2 | async-start | bytes 1048576 | tf_op jit(solution)/shard_map/all_to_all | solution.py:359
  55.8 0.0 copy-done
  55.8 0.0 copy-done.1
  55.8 0.0 copy-done.2
  55.8 0.0 copy-start.3
  55.9 0.0 copy-start.4
  55.9 0.6 shard_map.96.inside_ref
  56.4 9.5 %all-to-all-done.2 = f32[16,64,128]{2,1,0:T(8,128)S(1)} async-done(((f32[16,64,128]{2,1,0:T(8,128)}), f32[16,64,128]{2,1,0:T(8,128)S(1)}, u32[]{:S(2)}, u32[]{:S(2)}) %all-to-all-start.2) | async-done | bytes 524320 | tf_op jit(solution)/shard_map/all_to_all | solution.py:359
  65.9 0.0 copy-done.3
  65.9 0.6 shard_map.97
  66.5 12.5 %all_to_all.37.sums_ref = f32[8,2,128]{2,1,0:T(2,128)S(1)} all-to-all(f32[8,2,128]{2,1,0:T(2,128)S(1)} %get-tuple-element.23), channel_id=1, replica_groups=mesh['ctx'=64,'tp'=8] {'tp'}, dimensions={0} | all-to-all | bytes 16384 | tf_op jit(solution)/shard_map/all_to_all | solution.py:395
  79.1 0.7 shard_map.99
  79.7 19.1 %all_to_all.38.piece_ref = f32[16,64,128]{2,1,0:T(8,128)S(1)} all-to-all(f32[16,64,128]{2,1,0:T(8,128)S(1)} %shard_map.99), channel_id=1, replica_groups={{0,32,64,96,8,40,72,104,16,48,80,112,24,56,88,120},{128,160,192,224,136..., dimensions={0} | all-to-all | bytes 1048576 | tf_op jit(solution)/shard_map/all_to_all | solution.py:359
  98.9 14.0 %all_to_all.39.total_ref = f32[4,64,128]{2,1,0:T(8,128)S(1)} all-to-all(f32[4,64,128]{2,1,0:T(8,128)S(1)} %shard_map.100), channel_id=1, replica_groups={{0,128,320,448},{32,160,352,480},{64,192,256,384},{96,224,288,416},{8,1..., dimensions={0} | all-to-all | bytes 262144 | tf_op jit(solution)/shard_map/all_to_all | solution.py:359
  112.9 0.9 shard_map.101
  113.8 8.6 %all-to-all-start.6 = ((f32[16,64,128]{2,1,0:T(8,128)}), f32[16,64,128]{2,1,0:T(8,128)S(1)}, u32[]{:S(2)}, u32[]{:S(2)}) async-start(f32[16,64,128]{2,1,0:T(8,128)} %shard_map.101), calls=%async_computation.6 | async-start | bytes 1048576 | tf_op jit(solution)/shard_map/all_to_all | solution.py:359
  122.4 3.4 %shard_map.98 = (bf16[128,1024]{1,0:T(8,128)(2,1)}, bf16[128,1024]{1,0:T(8,128)(2,1)}, f32[8,128,128]{2,1,0:T(8,128)S(1)}, f32[128,1024]{1,0:T(8,128)S(1)}) custom-call(bf16[128,1024]{1,0:T(8,128)(2,1)S(1)} %copy-done, bf16[128,1024]{1,0:T(8,128)(2,1)S(1)} %copy-done.1, ...), custom_call_target="tpu_custom_call", output_to_operand_aliasing={{2}: (5, {}), {3}: (6, {})} | custom-call | flops 436207616 | bytes 3690496 | tf_op jit(solution)/shard_map/pallas_call | solution.py:307
  125.8 8.5 %all-to-all-done.6 = f32[16,64,128]{2,1,0:T(8,128)S(1)} async-done(((f32[16,64,128]{2,1,0:T(8,128)}), f32[16,64,128]{2,1,0:T(8,128)S(1)}, u32[]{:S(2)}, u32[]{:S(2)}) %all-to-all-start.6) | async-done | bytes 524320 | tf_op jit(solution)/shard_map/all_to_all | solution.py:359
  134.3 1.2 shard_map.102
  (5 shorter events, 0.1 us)
Async XLA Ops:
  50.0 5.9 %copy-start = (bf16[128,1024]{1,0:T(8,128)(2,1)S(1)}, bf16[128,1024]{1,0:T(8,128)(2,1)}, u32[]{:S(2)}) copy-start(bf16[128,1024]{1,0:T(8,128)(2,1)} %query_ref.7) | copy-start | bytes 786436
  50.0 5.9 %copy-start.1 = (bf16[128,1024]{1,0:T(8,128)(2,1)S(1)}, bf16[128,1024]{1,0:T(8,128)(2,1)}, u32[]{:S(2)}) copy-start(bf16[128,1024]{1,0:T(8,128)(2,1)} %key_ref.5) | copy-start | bytes 786436
  50.0 5.9 %copy-start.2 = (bf16[128,1024]{1,0:T(8,128)(2,1)S(1)}, bf16[128,1024]{1,0:T(8,128)(2,1)}, u32[]{:S(2)}) copy-start(bf16[128,1024]{1,0:T(8,128)(2,1)} %value_ref.5) | copy-start | bytes 786436
  50.0 15.9 %all-to-all-start.2 = ((f32[16,64,128]{2,1,0:T(8,128)}), f32[16,64,128]{2,1,0:T(8,128)S(1)}, u32[]{:S(2)}, u32[]{:S(2)}) async-start(f32[16,64,128]{2,1,0:T(8,128)} %get-tuple-element.21), calls=%async_computation.2 | async-start | bytes 1048576 | tf_op jit(solution)/shard_map/all_to_all | solution.py:359
  55.8 10.1 %copy-start.3 = (bf16[128,1024]{1,0:T(8,128)(2,1)S(1)}, bf16[128,1024]{1,0:T(8,128)(2,1)}, u32[]{:S(2)}) copy-start(bf16[128,1024]{1,0:T(8,128)(2,1)} %grad_ref.5) | copy-start | bytes 786436
  55.9 10.1 %copy-start.4 = (f32[1024]{0:T(1024)S(1)}, f32[1024]{0:T(1024)}, u32[]{:S(2)}) copy-start(f32[1024]{0:T(1024)} %param.10) | copy-start | bytes 12292
  113.8 20.5 %all-to-all-start.6 = ((f32[16,64,128]{2,1,0:T(8,128)}), f32[16,64,128]{2,1,0:T(8,128)S(1)}, u32[]{:S(2)}, u32[]{:S(2)}) async-start(f32[16,64,128]{2,1,0:T(8,128)} %shard_map.101), calls=%async_computation.6 | async-start | bytes 1048576 | tf_op jit(solution)/shard_map/all_to_all | solution.py:359

commit v11 on v10

--- a/solution.py
+++ b/solution.py
@@ -61,21 +61,19 @@
 def whereabouts(heads):
     span = 2 * heads // 4
     z_rows = lax.axis_size("ctx") // 4
-    shift = (lax.axis_index("tp") & 1) * (span // 2)
+    shift = (1 - (lax.axis_index("tp") & 1)) * (span // 2)
     group = lax.div((lax.div(lax.axis_index("ctx"), 4) - shift) & (z_rows - 1), span)
     cut = jnp.logical_and(shift > 0, group == z_rows // span - 1)
     return group, shift, cut
 
 
 def turned(head, heads):
-    group, shift, _ = whereabouts(heads)
     half = lax.axis_size("ctx") // (2 * heads) // 2
-    return head ^ jnp.where(group < half, 0, jnp.where(shift > 0, 4, 1))
-
-
-def rank(member, shift, cut):
-    x, z = member % 4, (member // 4) ^ jnp.where(cut, 2, 0)
-    return jnp.where(shift > 0, z * 4 + x, x * 4 + z)
+    return head ^ jnp.where(whereabouts(heads)[0] < half, 0, 1)
+
+
+def rank(member, cut):
+    return member % 4 * 4 + ((member // 4) ^ jnp.where(cut, 2, 0))
 
 
 def cols(head, size):
@@ -120,14 +118,14 @@
 
 
 def group_kernel(members, copies, rows, piece_ref, out_ref):
-    _, shift, cut = whereabouts(members // 2)
+    _, _, cut = whereabouts(members // 2)
     total = jnp.zeros((rows, piece_ref.shape[-1]), f32)
     whole = jnp.zeros((8, piece_ref.shape[-1]), f32)
     early = total
     for member in range(members):
         if member == members // 2:
             early = total
-        place = rank(member, shift, cut)
+        place = rank(member, cut)
         mark = piece_ref[place, rows:, :]
         total = times(jnp.exp(mark), total) + piece_ref[place, :rows, :]
         whole = whole + mark
@@ -152,7 +150,7 @@
     for member in range(members):
         if member == members // 2:
             running = jnp.where(cut, every, running)
-        place = rank(member, shift, cut)
+        place = rank(member, cut)
         gain = jnp.exp(piece_ref[place, rows:, :])
         near_ref[place] = gain
         out_ref[place] = running
@@ -160,11 +158,11 @@
 
 
 def back_group_kernel(members, copies, piece_ref, near_ref, out_ref):
-    _, shift, cut = whereabouts(members // 2)
+    _, _, cut = whereabouts(members // 2)
     total = jnp.zeros(piece_ref.shape[1:], f32)
     late = total
     for member in reversed(range(members)):
-        place = rank(member, shift, cut)
+        place = rank(member, cut)
         total = times(near_ref[place], total) + piece_ref[place]
         if member == members // 2:
             late = total
@@ -174,14 +172,14 @@
 
 
 def back_spread_kernel(members, groups, piece_ref, near_ref, total_ref, far_ref, out_ref):
-    mine, shift, cut = whereabouts(members // 2)
+    mine, _, cut = whereabouts(members // 2)
     every = jnp.zeros(piece_ref.shape[1:], f32)
     running = every
     for group in reversed(range(groups)):
         every = times(far_ref[group], every) + total_ref[group]
         running = jnp.where(group > mine, every, running)
     for member in reversed(range(members)):
-        place = rank(member, shift, cut)
+        place = rank(member, cut)
         out_ref[place] = running
         running = times(near_ref[place], running) + piece_ref[place]
         if member == members // 2:
@@ -323,20 +321,17 @@
     groups = count // members
     near, far = [], []
     for index in range(tp):
-        shift = index % 2 * (span // 2)
+        shift = (1 - index % 2) * (span // 2)
 
         def device(group, place):
-            x, z = (place % 4, place // 4) if shift else (place // 4, place % 4)
-            return ((group * span + shift + z) % (count // 4) * 4 + x) * tp + index
+            z = (group * span + shift + place % 4) % (count // 4)
+            return (z * 4 + place // 4) * tp + index
 
         for group in range(groups):
             near.append([device(group, place) for place in range(members)])
         for piece in range(members):
             far.append(
-                [
-                    device(group, piece ^ ((8 if shift else 2) if group >= groups // 2 else 0))
-                    for group in range(groups)
-                ]
+                [device(group, piece ^ (2 if group >= groups // 2 else 0)) for group in range(groups)]
             )
     return groups, members, near, far
 

time: 137 us -> 135 us (0.985)
  blocking collectives: 92.3 us -> 90.6 us
    all_to_all x1, blocking collectives: 12.5 us -> 10.4 us  [shards(): gathered = lax.all_to_all(sums, 'tp', 0, 0)]
where the time goes in v11:
time: 135 us; the launch traced here: 132 us
  blocking collectives  90.6 us (67%)
  waiting for transfers between devices  17.6 us (13%)
  starting transfers between devices  13.4 us (10%)
  Pallas kernels  10.1 us (7%)
    all_to_all x4, blocking collectives, exchange(): return lax.all_to_all(parts, ('ctx', 'tp'), 0, 0, axis_index_groups=lists)  80.2 us
    all_to_all x2, waiting for transfers between devices, exchange(): return lax.all_to_all(parts, ('ctx', 'tp'), 0, 0, axis_index_groups=lists)  17.6 us
    all_to_all x2, starting transfers between devices, exchange(): return lax.all_to_all(parts, ('ctx', 'tp'), 0, 0, axis_index_groups=lists)  13.4 us
    all_to_all x1, blocking collectives, shards(): gathered = lax.all_to_all(sums, 'tp', 0, 0)  10.4 us
    pallas_call x10, Pallas kernels, call(): pl.pallas_call(kernel, out_shape=outs, in_specs=[hbm if copied else vmem]...  10.1 us
  transfers between devices with their start and end apart: 2, of which 2 were waited for; matrix products, arithmetic and copies ran while one was open for 0% of the time, Pallas kernels for 3%

profile of v11, /device:TPU:1, one launch (start us, length us, event | category | flops | bytes accessed | tf_op | source)
XLA Modules:
  0.0 132.4 jit_solution(9466394248462399911)
XLA Ops:
  0.6 1.7 %shard_map.93 = (f32[16,72,128]{2,1,0:T(8,128)S(1)}, f32[128,8]{1,0:T(8,128)S(1)}, f32[8,128]{1,0:T(8,128)S(1)}) custom-call(bf16[128,1024]{1,0:T(8,128)(2,1)} %key_ref.5, bf16[128,1024]{1,0:T(8,128)(2,1)} %value_ref.5, f32[8,128]{1,0:T(8,128)} %bitcast.10), custom_call_target="tpu_custom_call" | custom-call | flops 67108864 | bytes 1126400 | tf_op jit(solution)/shard_map/pallas_call | solution.py:305
  2.4 21.3 %all_to_all.35.piece_ref = f32[16,72,128]{2,1,0:T(8,128)S(1)} all-to-all(f32[16,72,128]{2,1,0:T(8,128)S(1)} %get-tuple-element.20), channel_id=1, replica_groups={{64,96,128,160,72,104,136,168,80,112,144,176,88,120,152,184},{192,224,2..., dimensions={0} | all-to-all | bytes 1179648 | tf_op jit(solution)/shard_map/all_to_all | solution.py:354
  23.6 0.1 shard_map.94
  23.7 27.4 %all_to_all.36.total_ref = f32[4,72,128]{2,1,0:T(8,128)S(1)} all-to-all(f32[4,72,128]{2,1,0:T(8,128)S(1)} %shard_map.94), channel_id=1, replica_groups={{64,192,384,0},{96,224,416,32},{128,256,320,448},{160,288,352,480},{72,..., dimensions={0} | all-to-all | bytes 294912 | tf_op jit(solution)/shard_map/all_to_all | solution.py:354
  51.1 0.9 shard_map.95
  52.0 3.7 %all-to-all-start.2 = ((f32[16,64,128]{2,1,0:T(8,128)}), f32[16,64,128]{2,1,0:T(8,128)S(1)}, u32[]{:S(2)}, u32[]{:S(2)}) async-start(f32[16,64,128]{2,1,0:T(8,128)} %get-tuple-element.21), calls=%async_computation.2 | async-start | bytes 1048576 | tf_op jit(solution)/shard_map/all_to_all | solution.py:354
  55.7 0.0 copy-done
  55.7 0.0 copy-done.1
  55.8 0.0 copy-start.3
  55.8 0.0 copy-start.4
  55.8 0.6 shard_map.96.inside_ref
  56.4 10.2 %all-to-all-done.2 = f32[16,64,128]{2,1,0:T(8,128)S(1)} async-done(((f32[16,64,128]{2,1,0:T(8,128)}), f32[16,64,128]{2,1,0:T(8,128)S(1)}, u32[]{:S(2)}, u32[]{:S(2)}) %all-to-all-start.2) | async-done | bytes 524320 | tf_op jit(solution)/shard_map/all_to_all | solution.py:354
  66.6 0.0 copy-done.3
  66.6 0.6 shard_map.97
  67.2 10.4 %all_to_all.37.sums_ref = f32[8,2,128]{2,1,0:T(2,128)S(1)} all-to-all(f32[8,2,128]{2,1,0:T(2,128)S(1)} %get-tuple-element.23), channel_id=1, replica_groups=mesh['ctx'=64,'tp'=8] {'tp'}, dimensions={0} | all-to-all | bytes 16384 | tf_op jit(solution)/shard_map/all_to_all | solution.py:390
  77.6 0.7 shard_map.99
  78.3 16.5 %all_to_all.38.piece_ref = f32[16,64,128]{2,1,0:T(8,128)S(1)} all-to-all(f32[16,64,128]{2,1,0:T(8,128)S(1)} %shard_map.99), channel_id=1, replica_groups={{64,96,128,160,72,104,136,168,80,112,144,176,88,120,152,184},{192,224,2..., dimensions={0} | all-to-all | bytes 1048576 | tf_op jit(solution)/shard_map/all_to_all | solution.py:354
  94.8 0.1 shard_map.100
  94.8 15.0 %all_to_all.39.total_ref = f32[4,64,128]{2,1,0:T(8,128)S(1)} all-to-all(f32[4,64,128]{2,1,0:T(8,128)S(1)} %shard_map.100), channel_id=1, replica_groups={{64,192,384,0},{96,224,416,32},{128,256,320,448},{160,288,352,480},{72,..., dimensions={0} | all-to-all | bytes 262144 | tf_op jit(solution)/shard_map/all_to_all | solution.py:354
  109.8 0.9 shard_map.101
  110.7 9.7 %all-to-all-start.6 = ((f32[16,64,128]{2,1,0:T(8,128)}), f32[16,64,128]{2,1,0:T(8,128)S(1)}, u32[]{:S(2)}, u32[]{:S(2)}) async-start(f32[16,64,128]{2,1,0:T(8,128)} %shard_map.101), calls=%async_computation.6 | async-start | bytes 1048576 | tf_op jit(solution)/shard_map/all_to_all | solution.py:354
  120.4 3.4 %shard_map.98 = (bf16[128,1024]{1,0:T(8,128)(2,1)}, bf16[128,1024]{1,0:T(8,128)(2,1)}, f32[8,128,128]{2,1,0:T(8,128)S(1)}, f32[128,1024]{1,0:T(8,128)S(1)}) custom-call(bf16[128,1024]{1,0:T(8,128)(2,1)S(1)} %copy-done, bf16[128,1024]{1,0:T(8,128)(2,1)S(1)} %copy-done.1, ...), custom_call_target="tpu_custom_call", output_to_operand_aliasing={{2}: (5, {}), {3}: (6, {})} | custom-call | flops 436207616 | bytes 3690496 | tf_op jit(solution)/shard_map/pallas_call | solution.py:305
  123.8 7.3 %all-to-all-done.6 = f32[16,64,128]{2,1,0:T(8,128)S(1)} async-done(((f32[16,64,128]{2,1,0:T(8,128)}), f32[16,64,128]{2,1,0:T(8,128)S(1)}, u32[]{:S(2)}, u32[]{:S(2)}) %all-to-all-start.6) | async-done | bytes 524320 | tf_op jit(solution)/shard_map/all_to_all | solution.py:354
  131.1 1.2 shard_map.102
  (5 shorter events, 0.0 us)
Async XLA Ops:
  52.0 3.7 %copy-start = (bf16[128,1024]{1,0:T(8,128)(2,1)S(1)}, bf16[128,1024]{1,0:T(8,128)(2,1)}, u32[]{:S(2)}) copy-start(bf16[128,1024]{1,0:T(8,128)(2,1)} %query_ref.7) | copy-start | bytes 786436
  52.0 3.7 %copy-start.1 = (bf16[128,1024]{1,0:T(8,128)(2,1)S(1)}, bf16[128,1024]{1,0:T(8,128)(2,1)}, u32[]{:S(2)}) copy-start(bf16[128,1024]{1,0:T(8,128)(2,1)} %key_ref.5) | copy-start | bytes 786436
  52.0 3.7 %copy-start.2 = (bf16[128,1024]{1,0:T(8,128)(2,1)S(1)}, bf16[128,1024]{1,0:T(8,128)(2,1)}, u32[]{:S(2)}) copy-start(bf16[128,1024]{1,0:T(8,128)(2,1)} %value_ref.5) | copy-start | bytes 786436
  52.0 14.6 %all-to-all-start.2 = ((f32[16,64,128]{2,1,0:T(8,128)}), f32[16,64,128]{2,1,0:T(8,128)S(1)}, u32[]{:S(2)}, u32[]{:S(2)}) async-start(f32[16,64,128]{2,1,0:T(8,128)} %get-tuple-element.21), calls=%async_computation.2 | async-start | bytes 1048576 | tf_op jit(solution)/shard_map/all_to_all | solution.py:354
  55.8 10.8 %copy-start.3 = (bf16[128,1024]{1,0:T(8,128)(2,1)S(1)}, bf16[128,1024]{1,0:T(8,128)(2,1)}, u32[]{:S(2)}) copy-start(bf16[128,1024]{1,0:T(8,128)(2,1)} %grad_ref.5) | copy-start | bytes 786436
  55.8 10.8 %copy-start.4 = (f32[1024]{0:T(1024)S(1)}, f32[1024]{0:T(1024)}, u32[]{:S(2)}) copy-start(f32[1024]{0:T(1024)} %param.10) | copy-start | bytes 12292
  110.7 20.4 %all-to-all-start.6 = ((f32[16,64,128]{2,1,0:T(8,128)}), f32[16,64,128]{2,1,0:T(8,128)S(1)}, u32[]{:S(2)}, u32[]{:S(2)}) async-start(f32[16,64,128]{2,1,0:T(8,128)} %shard_map.101), calls=%async_computation.6 | async-start | bytes 1048576 | tf_op jit(solution)/shard_map/all_to_all | solution.py:354

commit v12 on v11

--- a/solution.py
+++ b/solution.py
@@ -61,7 +61,7 @@
 def whereabouts(heads):
     span = 2 * heads // 4
     z_rows = lax.axis_size("ctx") // 4
-    shift = (1 - (lax.axis_index("tp") & 1)) * (span // 2)
+    shift = (lax.axis_index("tp") & 1) * (span // 2)
     group = lax.div((lax.div(lax.axis_index("ctx"), 4) - shift) & (z_rows - 1), span)
     cut = jnp.logical_and(shift > 0, group == z_rows // span - 1)
     return group, shift, cut
@@ -213,9 +213,8 @@
     ones = jnp.ones((8, size), f32)
     square = lax.dot_general(ones, squares, NT, precision=highest, preferred_element_type=f32)
     product_ = lax.dot_general(ones, products, NT, precision=highest, preferred_element_type=f32)
-    for copy in range(sums_ref.shape[0]):
-        sums_ref[copy, 0:1, :] = square[0:1, :]
-        sums_ref[copy, 1:2, :] = product_[0:1, :]
+    sums_ref[0:1, :] = square[0:1, :]
+    sums_ref[1:2, :] = product_[0:1, :]
 
 
 def row_factors(full_width, size, sums_ref):
@@ -321,7 +320,7 @@
     groups = count // members
     near, far = [], []
     for index in range(tp):
-        shift = (1 - index % 2) * (span // 2)
+        shift = index % 2 * (span // 2)
 
         def device(group, place):
             z = (group * span + shift + place % 4) % (count // 4)
@@ -378,7 +377,7 @@
     entry = exchange(entering, near).reshape(heads, size, size)
     mixed, sums = call(
         bind(mixed_kernel, heads),
-        [wide, shape((lax.axis_size("tp"), 2, tok_rows), f32)],
+        [wide, shape((2, tok_rows), f32)],
         queries,
         tall,
         inside,
@@ -387,7 +386,7 @@
         grad_output,
         flops=2 * unit,
     )
-    gathered = lax.all_to_all(sums, "tp", 0, 0)
+    gathered = lax.all_gather(sums, "tp")
     full_width = feat_width * lax.axis_size("tp")
     (back,) = call(
         bind(back_kernel, heads, members, full_width),

time: 135 us -> 136 us (level)
  the two profiles are of different devices: /device:TPU:1 before, /device:TPU:97 now
where the time goes in v12:
time: 136 us
  blocking collectives  81.2 us (60%)
  waiting for transfers between devices  25.6 us (19%)
  starting transfers between devices  18 us (13%)
  Pallas kernels  10.1 us (7%)
    all_to_all x4, blocking collectives, exchange(): return lax.all_to_all(parts, ('ctx', 'tp'), 0, 0, axis_index_groups=lists)  72.4 us
    all_to_all x2, waiting for transfers between devices, exchange(): return lax.all_to_all(parts, ('ctx', 'tp'), 0, 0, axis_index_groups=lists)  25.6 us
    all_to_all x2, starting transfers between devices, exchange(): return lax.all_to_all(parts, ('ctx', 'tp'), 0, 0, axis_index_groups=lists)  18 us
    pallas_call x10, Pallas kernels, call(): pl.pallas_call(kernel, out_shape=outs, in_specs=[hbm if copied else vmem]...  10.1 us
    all_gather x1, blocking collectives, shards(): gathered = lax.all_gather(sums, 'tp')  8.81 us
  transfers between devices with their start and end apart: 2, of which 2 were waited for; matrix products, arithmetic and copies ran while one was open for 0% of the time, Pallas kernels for 3%

profile of v12, /device:TPU:97, one launch (start us, length us, event | category | flops | bytes accessed | tf_op | source)
XLA Modules:
  0.0 135.6 jit_solution(795605805708612123)
XLA Ops:
  0.6 1.7 %shard_map.93 = (f32[16,72,128]{2,1,0:T(8,128)S(1)}, f32[128,8]{1,0:T(8,128)S(1)}, f32[8,128]{1,0:T(8,128)S(1)}) custom-call(bf16[128,1024]{1,0:T(8,128)(2,1)} %key_ref.5, bf16[128,1024]{1,0:T(8,128)(2,1)} %value_ref.5, f32[8,128]{1,0:T(8,128)} %bitcast.12), custom_call_target="tpu_custom_call" | custom-call | flops 67108864 | bytes 1126400 | tf_op jit(solution)/shard_map/pallas_call | solution.py:304
  2.4 24.5 %all_to_all.30.piece_ref = f32[16,72,128]{2,1,0:T(8,128)S(1)} all-to-all(f32[16,72,128]{2,1,0:T(8,128)S(1)} %get-tuple-element.20), channel_id=1, replica_groups={{0,32,64,96,8,40,72,104,16,48,80,112,24,56,88,120},{128,160,192,224,136..., dimensions={0} | all-to-all | bytes 1179648 | tf_op jit(solution)/shard_map/all_to_all | solution.py:353
  26.9 0.1 shard_map.94
  26.9 16.0 %all_to_all.31.total_ref = f32[4,72,128]{2,1,0:T(8,128)S(1)} all-to-all(f32[4,72,128]{2,1,0:T(8,128)S(1)} %shard_map.94), channel_id=1, replica_groups={{0,128,320,448},{32,160,352,480},{64,192,256,384},{96,224,288,416},{8,1..., dimensions={0} | all-to-all | bytes 294912 | tf_op jit(solution)/shard_map/all_to_all | solution.py:353
  42.9 0.9 shard_map.95
  43.8 8.9 %all-to-all-start.2 = ((f32[16,64,128]{2,1,0:T(8,128)}), f32[16,64,128]{2,1,0:T(8,128)S(1)}, u32[]{:S(2)}, u32[]{:S(2)}) async-start(f32[16,64,128]{2,1,0:T(8,128)} %get-tuple-element.21), calls=%async_computation.2 | async-start | bytes 1048576 | tf_op jit(solution)/shard_map/all_to_all | solution.py:353
  52.8 0.0 copy-done
  52.8 0.0 copy-done.1
  52.8 0.0 copy-start.3
  52.8 0.0 copy-start.4
  52.8 0.6 shard_map.96.inside_ref
  53.4 14.4 %all-to-all-done.2 = f32[16,64,128]{2,1,0:T(8,128)S(1)} async-done(((f32[16,64,128]{2,1,0:T(8,128)}), f32[16,64,128]{2,1,0:T(8,128)S(1)}, u32[]{:S(2)}, u32[]{:S(2)}) %all-to-all-start.2) | async-done | bytes 524320 | tf_op jit(solution)/shard_map/all_to_all | solution.py:353
  67.8 0.0 copy-done.4
  67.8 0.6 shard_map.97
  68.4 8.8 %all-gather.1.sums_ref = f32[8,2,128]{2,1,0:T(2,128)S(1)} all-gather(f32[1,2,128]{2,1,0:T(2,128)S(1)} %bitcast.11), channel_id=2, replica_groups=mesh['ctx'=64,'tp'=8] {'tp'}, dimensions={0}, use_global_device_ids=true | all-gather | bytes 9216 | tf_op jit(solution)/shard_map/all_gather | solution.py:389
  77.2 0.7 shard_map.99
  77.9 20.3 %all_to_all.32.piece_ref = f32[16,64,128]{2,1,0:T(8,128)S(1)} all-to-all(f32[16,64,128]{2,1,0:T(8,128)S(1)} %shard_map.99), channel_id=1, replica_groups={{0,32,64,96,8,40,72,104,16,48,80,112,24,56,88,120},{128,160,192,224,136..., dimensions={0} | all-to-all | bytes 1048576 | tf_op jit(solution)/shard_map/all_to_all | solution.py:353
  98.2 0.1 shard_map.100
  98.2 11.6 %all_to_all.33.total_ref = f32[4,64,128]{2,1,0:T(8,128)S(1)} all-to-all(f32[4,64,128]{2,1,0:T(8,128)S(1)} %shard_map.100), channel_id=1, replica_groups={{0,128,320,448},{32,160,352,480},{64,192,256,384},{96,224,288,416},{8,1..., dimensions={0} | all-to-all | bytes 262144 | tf_op jit(solution)/shard_map/all_to_all | solution.py:353
  109.9 0.9 shard_map.101
  110.7 9.0 %all-to-all-start.5 = ((f32[16,64,128]{2,1,0:T(8,128)}), f32[16,64,128]{2,1,0:T(8,128)S(1)}, u32[]{:S(2)}, u32[]{:S(2)}) async-start(f32[16,64,128]{2,1,0:T(8,128)} %shard_map.101), calls=%async_computation.5 | async-start | bytes 1048576 | tf_op jit(solution)/shard_map/all_to_all | solution.py:353
  119.8 3.4 %shard_map.98 = (bf16[128,1024]{1,0:T(8,128)(2,1)}, bf16[128,1024]{1,0:T(8,128)(2,1)}, f32[8,128,128]{2,1,0:T(8,128)S(1)}, f32[128,1024]{1,0:T(8,128)S(1)}) custom-call(bf16[128,1024]{1,0:T(8,128)(2,1)S(1)} %copy-done, bf16[128,1024]{1,0:T(8,128)(2,1)S(1)} %copy-done.1, ...), custom_call_target="tpu_custom_call", output_to_operand_aliasing={{2}: (5, {}), {3}: (6, {})} | custom-call | flops 436207616 | bytes 3690496 | tf_op jit(solution)/shard_map/pallas_call | solution.py:304
  123.2 11.2 %all-to-all-done.5 = f32[16,64,128]{2,1,0:T(8,128)S(1)} async-done(((f32[16,64,128]{2,1,0:T(8,128)}), f32[16,64,128]{2,1,0:T(8,128)S(1)}, u32[]{:S(2)}, u32[]{:S(2)}) %all-to-all-start.5) | async-done | bytes 524320 | tf_op jit(solution)/shard_map/all_to_all | solution.py:353
  134.4 1.2 shard_map.102
  (5 shorter events, 0.0 us)
Async XLA Ops:
  43.8 9.0 %copy-start = (bf16[128,1024]{1,0:T(8,128)(2,1)S(1)}, bf16[128,1024]{1,0:T(8,128)(2,1)}, u32[]{:S(2)}) copy-start(bf16[128,1024]{1,0:T(8,128)(2,1)} %query_ref.7) | copy-start | bytes 786436
  43.8 9.0 %copy-start.1 = (bf16[128,1024]{1,0:T(8,128)(2,1)S(1)}, bf16[128,1024]{1,0:T(8,128)(2,1)}, u32[]{:S(2)}) copy-start(bf16[128,1024]{1,0:T(8,128)(2,1)} %key_ref.5) | copy-start | bytes 786436
  43.8 9.0 %copy-start.2 = (bf16[128,1024]{1,0:T(8,128)(2,1)S(1)}, bf16[128,1024]{1,0:T(8,128)(2,1)}, u32[]{:S(2)}) copy-start(bf16[128,1024]{1,0:T(8,128)(2,1)} %value_ref.5) | copy-start | bytes 786436
  43.8 24.0 %all-to-all-start.2 = ((f32[16,64,128]{2,1,0:T(8,128)}), f32[16,64,128]{2,1,0:T(8,128)S(1)}, u32[]{:S(2)}, u32[]{:S(2)}) async-start(f32[16,64,128]{2,1,0:T(8,128)} %get-tuple-element.21), calls=%async_computation.2 | async-start | bytes 1048576 | tf_op jit(solution)/shard_map/all_to_all | solution.py:353
  52.8 15.0 %copy-start.3 = (bf16[128,1024]{1,0:T(8,128)(2,1)S(1)}, bf16[128,1024]{1,0:T(8,128)(2,1)}, u32[]{:S(2)}) copy-start(bf16[128,1024]{1,0:T(8,128)(2,1)} %grad_ref.5) | copy-start | bytes 786436
  52.8 15.0 %copy-start.4 = (f32[1024]{0:T(1024)S(1)}, f32[1024]{0:T(1024)}, u32[]{:S(2)}) copy-start(f32[1024]{0:T(1024)} %param.10) | copy-start | bytes 12292
  110.7 23.6 %all-to-all-start.5 = ((f32[16,64,128]{2,1,0:T(8,128)}), f32[16,64,128]{2,1,0:T(8,128)S(1)}, u32[]{:S(2)}, u32[]{:S(2)}) async-start(f32[16,64,128]{2,1,0:T(8,128)} %shard_map.101), calls=%async_computation.5 | async-start | bytes 1048576 | tf_op jit(solution)/shard_map/all_to_all | solution.py:353

commit v13 on v11

--- a/solution.py
+++ b/solution.py
@@ -61,7 +61,7 @@
 def whereabouts(heads):
     span = 2 * heads // 4
     z_rows = lax.axis_size("ctx") // 4
-    shift = (1 - (lax.axis_index("tp") & 1)) * (span // 2)
+    shift = (lax.axis_index("tp") & 1) * (span // 2)
     group = lax.div((lax.div(lax.axis_index("ctx"), 4) - shift) & (z_rows - 1), span)
     cut = jnp.logical_and(shift > 0, group == z_rows // span - 1)
     return group, shift, cut
@@ -321,7 +321,7 @@
     groups = count // members
     near, far = [], []
     for index in range(tp):
-        shift = (1 - index % 2) * (span // 2)
+        shift = index % 2 * (span // 2)
 
         def device(group, place):
             z = (group * span + shift + place % 4) % (count // 4)

time: 135 us -> 135 us (level)
  starting transfers between devices: 13.4 us -> 16.8 us
  waiting for transfers between devices: 17.6 us -> 15.4 us
    all_to_all x1, blocking collectives: 10.4 us -> 14.5 us  [shards(): gathered = lax.all_to_all(sums, 'tp', 0, 0)]
    all_to_all x4, blocking collectives: 80.2 us -> 76.1 us  [exchange(): return lax.all_to_all(parts, ('ctx', 'tp'), 0, 0, axis_index_groups=lists)]
    all_to_all x2, starting transfers between devices: 13.4 us -> 16.8 us  [exchange(): return lax.all_to_all(parts, ('ctx', 'tp'), 0, 0, axis_index_groups=lists)]
    all_to_all x2, waiting for transfers between devices: 17.6 us -> 15.4 us  [exchange(): return lax.all_to_all(parts, ('ctx', 'tp'), 0, 0, axis_index_groups=lists)]
where the time goes in v13:
time: 135 us; the launch traced here: 134 us
  blocking collectives  90.6 us (67%)
  starting transfers between devices  16.8 us (12%)
  waiting for transfers between devices  15.4 us (11%)
  Pallas kernels  10.1 us (7%)
    all_to_all x4, blocking collectives, exchange(): return lax.all_to_all(parts, ('ctx', 'tp'), 0, 0, axis_index_groups=lists)  76.1 us
    all_to_all x2, starting transfers between devices, exchange(): return lax.all_to_all(parts, ('ctx', 'tp'), 0, 0, axis_index_groups=lists)  16.8 us
    all_to_all x2, waiting for transfers between devices, exchange(): return lax.all_to_all(parts, ('ctx', 'tp'), 0, 0, axis_index_groups=lists)  15.4 us
    all_to_all x1, blocking collectives, shards(): gathered = lax.all_to_all(sums, 'tp', 0, 0)  14.5 us
    pallas_call x10, Pallas kernels, call(): pl.pallas_call(kernel, out_shape=outs, in_specs=[hbm if copied else vmem]...  10.1 us
  transfers between devices with their start and end apart: 2, of which 2 were waited for; matrix products, arithmetic and copies ran while one was open for 0% of the time, Pallas kernels for 3%

profile of v13, /device:TPU:1, one launch (start us, length us, event | category | flops | bytes accessed | tf_op | source)
XLA Modules:
  0.0 133.7 jit_solution(8362937703033126801)
XLA Ops:
  0.6 1.7 %shard_map.93 = (f32[16,72,128]{2,1,0:T(8,128)S(1)}, f32[128,8]{1,0:T(8,128)S(1)}, f32[8,128]{1,0:T(8,128)S(1)}) custom-call(bf16[128,1024]{1,0:T(8,128)(2,1)} %key_ref.5, bf16[128,1024]{1,0:T(8,128)(2,1)} %value_ref.5, f32[8,128]{1,0:T(8,128)} %bitcast.10), custom_call_target="tpu_custom_call" | custom-call | flops 67108864 | bytes 1126400 | tf_op jit(solution)/shard_map/pallas_call | solution.py:305
  2.4 25.8 %all_to_all.35.piece_ref = f32[16,72,128]{2,1,0:T(8,128)S(1)} all-to-all(f32[16,72,128]{2,1,0:T(8,128)S(1)} %get-tuple-element.20), channel_id=1, replica_groups={{0,32,64,96,8,40,72,104,16,48,80,112,24,56,88,120},{128,160,192,224,136..., dimensions={0} | all-to-all | bytes 1179648 | tf_op jit(solution)/shard_map/all_to_all | solution.py:354
  28.2 0.1 shard_map.94
  28.2 20.2 %all_to_all.36.total_ref = f32[4,72,128]{2,1,0:T(8,128)S(1)} all-to-all(f32[4,72,128]{2,1,0:T(8,128)S(1)} %shard_map.94), channel_id=1, replica_groups={{0,128,320,448},{32,160,352,480},{64,192,256,384},{96,224,288,416},{8,1..., dimensions={0} | all-to-all | bytes 294912 | tf_op jit(solution)/shard_map/all_to_all | solution.py:354
  48.4 0.9 shard_map.95
  49.3 5.5 %all-to-all-start.2 = ((f32[16,64,128]{2,1,0:T(8,128)}), f32[16,64,128]{2,1,0:T(8,128)S(1)}, u32[]{:S(2)}, u32[]{:S(2)}) async-start(f32[16,64,128]{2,1,0:T(8,128)} %get-tuple-element.21), calls=%async_computation.2 | async-start | bytes 1048576 | tf_op jit(solution)/shard_map/all_to_all | solution.py:354
  54.7 0.0 copy-done.1
  54.7 0.0 copy-done.2
  54.8 0.0 copy-start.3
  54.8 0.0 copy-start.4
  54.8 0.6 shard_map.96.inside_ref
  55.4 8.4 %all-to-all-done.2 = f32[16,64,128]{2,1,0:T(8,128)S(1)} async-done(((f32[16,64,128]{2,1,0:T(8,128)}), f32[16,64,128]{2,1,0:T(8,128)S(1)}, u32[]{:S(2)}, u32[]{:S(2)}) %all-to-all-start.2) | async-done | bytes 524320 | tf_op jit(solution)/shard_map/all_to_all | solution.py:354
  63.8 0.0 copy-done.3
  63.8 0.6 shard_map.97
  64.4 14.5 %all_to_all.37.sums_ref = f32[8,2,128]{2,1,0:T(2,128)S(1)} all-to-all(f32[8,2,128]{2,1,0:T(2,128)S(1)} %get-tuple-element.23), channel_id=1, replica_groups=mesh['ctx'=64,'tp'=8] {'tp'}, dimensions={0} | all-to-all | bytes 16384 | tf_op jit(solution)/shard_map/all_to_all | solution.py:390
  78.9 0.7 shard_map.99
  79.6 17.7 %all_to_all.38.piece_ref = f32[16,64,128]{2,1,0:T(8,128)S(1)} all-to-all(f32[16,64,128]{2,1,0:T(8,128)S(1)} %shard_map.99), channel_id=1, replica_groups={{0,32,64,96,8,40,72,104,16,48,80,112,24,56,88,120},{128,160,192,224,136..., dimensions={0} | all-to-all | bytes 1048576 | tf_op jit(solution)/shard_map/all_to_all | solution.py:354
  97.2 0.1 shard_map.100
  97.3 12.5 %all_to_all.39.total_ref = f32[4,64,128]{2,1,0:T(8,128)S(1)} all-to-all(f32[4,64,128]{2,1,0:T(8,128)S(1)} %shard_map.100), channel_id=1, replica_groups={{0,128,320,448},{32,160,352,480},{64,192,256,384},{96,224,288,416},{8,1..., dimensions={0} | all-to-all | bytes 262144 | tf_op jit(solution)/shard_map/all_to_all | solution.py:354
  109.8 0.9 shard_map.101
  110.7 11.4 %all-to-all-start.6 = ((f32[16,64,128]{2,1,0:T(8,128)}), f32[16,64,128]{2,1,0:T(8,128)S(1)}, u32[]{:S(2)}, u32[]{:S(2)}) async-start(f32[16,64,128]{2,1,0:T(8,128)} %shard_map.101), calls=%async_computation.6 | async-start | bytes 1048576 | tf_op jit(solution)/shard_map/all_to_all | solution.py:354
  122.0 3.4 %shard_map.98 = (bf16[128,1024]{1,0:T(8,128)(2,1)}, bf16[128,1024]{1,0:T(8,128)(2,1)}, f32[8,128,128]{2,1,0:T(8,128)S(1)}, f32[128,1024]{1,0:T(8,128)S(1)}) custom-call(bf16[128,1024]{1,0:T(8,128)(2,1)S(1)} %copy-done, bf16[128,1024]{1,0:T(8,128)(2,1)S(1)} %copy-done.1, ...), custom_call_target="tpu_custom_call", output_to_operand_aliasing={{2}: (5, {}), {3}: (6, {})} | custom-call | flops 436207616 | bytes 3690496 | tf_op jit(solution)/shard_map/pallas_call | solution.py:305
  125.4 7.0 %all-to-all-done.6 = f32[16,64,128]{2,1,0:T(8,128)S(1)} async-done(((f32[16,64,128]{2,1,0:T(8,128)}), f32[16,64,128]{2,1,0:T(8,128)S(1)}, u32[]{:S(2)}, u32[]{:S(2)}) %all-to-all-start.6) | async-done | bytes 524320 | tf_op jit(solution)/shard_map/all_to_all | solution.py:354
  132.4 1.2 shard_map.102
  (5 shorter events, 0.0 us)
Async XLA Ops:
  49.3 5.5 %copy-start = (bf16[128,1024]{1,0:T(8,128)(2,1)S(1)}, bf16[128,1024]{1,0:T(8,128)(2,1)}, u32[]{:S(2)}) copy-start(bf16[128,1024]{1,0:T(8,128)(2,1)} %query_ref.7) | copy-start | bytes 786436
  49.3 5.5 %copy-start.1 = (bf16[128,1024]{1,0:T(8,128)(2,1)S(1)}, bf16[128,1024]{1,0:T(8,128)(2,1)}, u32[]{:S(2)}) copy-start(bf16[128,1024]{1,0:T(8,128)(2,1)} %key_ref.5) | copy-start | bytes 786436
  49.3 5.5 %copy-start.2 = (bf16[128,1024]{1,0:T(8,128)(2,1)S(1)}, bf16[128,1024]{1,0:T(8,128)(2,1)}, u32[]{:S(2)}) copy-start(bf16[128,1024]{1,0:T(8,128)(2,1)} %value_ref.5) | copy-start | bytes 786436
  49.3 14.5 %all-to-all-start.2 = ((f32[16,64,128]{2,1,0:T(8,128)}), f32[16,64,128]{2,1,0:T(8,128)S(1)}, u32[]{:S(2)}, u32[]{:S(2)}) async-start(f32[16,64,128]{2,1,0:T(8,128)} %get-tuple-element.21), calls=%async_computation.2 | async-start | bytes 1048576 | tf_op jit(solution)/shard_map/all_to_all | solution.py:354
  54.8 9.0 %copy-start.3 = (bf16[128,1024]{1,0:T(8,128)(2,1)S(1)}, bf16[128,1024]{1,0:T(8,128)(2,1)}, u32[]{:S(2)}) copy-start(bf16[128,1024]{1,0:T(8,128)(2,1)} %grad_ref.5) | copy-start | bytes 786436
  54.8 9.0 %copy-start.4 = (f32[1024]{0:T(1024)S(1)}, f32[1024]{0:T(1024)}, u32[]{:S(2)}) copy-start(f32[1024]{0:T(1024)} %param.10) | copy-start | bytes 12292
  110.7 21.8 %all-to-all-start.6 = ((f32[16,64,128]{2,1,0:T(8,128)}), f32[16,64,128]{2,1,0:T(8,128)S(1)}, u32[]{:S(2)}, u32[]{:S(2)}) async-start(f32[16,64,128]{2,1,0:T(8,128)} %shard_map.101), calls=%async_computation.6 | async-start | bytes 1048576 | tf_op jit(solution)/shard_map/all_to_all | solution.py:354

commit v14 on v10

--- a/solution.py
+++ b/solution.py
@@ -68,14 +68,14 @@
 
 
 def turned(head, heads):
-    group, shift, _ = whereabouts(heads)
+    group, _, _ = whereabouts(heads)
     half = lax.axis_size("ctx") // (2 * heads) // 2
-    return head ^ jnp.where(group < half, 0, jnp.where(shift > 0, 4, 1))
+    return head ^ jnp.where(group < half, 0, 4)
 
 
 def rank(member, shift, cut):
     x, z = member % 4, (member // 4) ^ jnp.where(cut, 2, 0)
-    return jnp.where(shift > 0, z * 4 + x, x * 4 + z)
+    return z * 4 + x
 
 
 def cols(head, size):
@@ -326,7 +326,7 @@
         shift = index % 2 * (span // 2)
 
         def device(group, place):
-            x, z = (place % 4, place // 4) if shift else (place // 4, place % 4)
+            x, z = place % 4, place // 4
             return ((group * span + shift + z) % (count // 4) * 4 + x) * tp + index
 
         for group in range(groups):
@@ -334,7 +334,7 @@
         for piece in range(members):
             far.append(
                 [
-                    device(group, piece ^ ((8 if shift else 2) if group >= groups // 2 else 0))
+                    device(group, piece ^ (8 if group >= groups // 2 else 0))
                     for group in range(groups)
                 ]
             )

time: 137 us -> 137 us (level)
    all_to_all x1, blocking collectives: 12.5 us -> 15.1 us  [shards(): gathered = lax.all_to_all(sums, 'tp', 0, 0)]
    all_to_all x4, blocking collectives: 79.8 us -> 77.8 us  [exchange(): return lax.all_to_all(parts, ('ctx', 'tp'), 0, 0, axis_index_groups=lists)]
where the time goes in v14:
time: 137 us
  blocking collectives  93 us (68%)
  waiting for transfers between devices  18.1 us (13%)
  starting transfers between devices  14.8 us (11%)
  Pallas kernels  10.1 us (7%)
    all_to_all x4, blocking collectives, exchange(): return lax.all_to_all(parts, ('ctx', 'tp'), 0, 0, axis_index_groups=lists)  77.8 us
    all_to_all x2, waiting for transfers between devices, exchange(): return lax.all_to_all(parts, ('ctx', 'tp'), 0, 0, axis_index_groups=lists)  18.1 us
    all_to_all x1, blocking collectives, shards(): gathered = lax.all_to_all(sums, 'tp', 0, 0)  15.1 us
    all_to_all x2, starting transfers between devices, exchange(): return lax.all_to_all(parts, ('ctx', 'tp'), 0, 0, axis_index_groups=lists)  14.8 us
    pallas_call x10, Pallas kernels, call(): pl.pallas_call(kernel, out_shape=outs, in_specs=[hbm if copied else vmem]...  10.1 us
  transfers between devices with their start and end apart: 2, of which 2 were waited for; matrix products, arithmetic and copies ran while one was open for 0% of the time, Pallas kernels for 3%

profile of v14, /device:TPU:1, one launch (start us, length us, event | category | flops | bytes accessed | tf_op | source)
XLA Modules:
  0.0 136.7 jit_solution(17623880479733163033)
XLA Ops:
  0.6 1.7 %shard_map.93 = (f32[16,72,128]{2,1,0:T(8,128)S(1)}, f32[128,8]{1,0:T(8,128)S(1)}, f32[8,128]{1,0:T(8,128)S(1)}) custom-call(bf16[128,1024]{1,0:T(8,128)(2,1)} %key_ref.5, bf16[128,1024]{1,0:T(8,128)(2,1)} %value_ref.5, f32[8,128]{1,0:T(8,128)} %bitcast.10), custom_call_target="tpu_custom_call" | custom-call | flops 67108864 | bytes 1126400 | tf_op jit(solution)/shard_map/pallas_call | solution.py:307
  2.4 26.5 %all_to_all.35.piece_ref = f32[16,72,128]{2,1,0:T(8,128)S(1)} all-to-all(f32[16,72,128]{2,1,0:T(8,128)S(1)} %get-tuple-element.20), channel_id=1, replica_groups={{0,8,16,24,32,40,48,56,64,72,80,88,96,104,112,120},{128,136,144,152,160..., dimensions={0} | all-to-all | bytes 1179648 | tf_op jit(solution)/shard_map/all_to_all | solution.py:359
  28.9 0.1 shard_map.94
  29.0 19.1 %all_to_all.36.total_ref = f32[4,72,128]{2,1,0:T(8,128)S(1)} all-to-all(f32[4,72,128]{2,1,0:T(8,128)S(1)} %shard_map.94), channel_id=1, replica_groups={{0,128,320,448},{8,136,328,456},{16,144,336,464},{24,152,344,472},{32,1..., dimensions={0} | all-to-all | bytes 294912 | tf_op jit(solution)/shard_map/all_to_all | solution.py:359
  48.1 0.9 shard_map.95
  49.0 6.2 %all-to-all-start.2 = ((f32[16,64,128]{2,1,0:T(8,128)}), f32[16,64,128]{2,1,0:T(8,128)S(1)}, u32[]{:S(2)}, u32[]{:S(2)}) async-start(f32[16,64,128]{2,1,0:T(8,128)} %get-tuple-element.21), calls=%async_computation.2 | async-start | bytes 1048576 | tf_op jit(solution)/shard_map/all_to_all | solution.py:359
  55.2 0.0 copy-done
  55.2 0.0 copy-done.1
  55.2 0.0 copy-done.2
  55.2 0.0 copy-start.3
  55.2 0.0 copy-start.4
  55.2 0.6 shard_map.96.inside_ref
  55.8 9.1 %all-to-all-done.2 = f32[16,64,128]{2,1,0:T(8,128)S(1)} async-done(((f32[16,64,128]{2,1,0:T(8,128)}), f32[16,64,128]{2,1,0:T(8,128)S(1)}, u32[]{:S(2)}, u32[]{:S(2)}) %all-to-all-start.2) | async-done | bytes 524320 | tf_op jit(solution)/shard_map/all_to_all | solution.py:359
  65.0 0.6 shard_map.97
  65.6 15.1 %all_to_all.37.sums_ref = f32[8,2,128]{2,1,0:T(2,128)S(1)} all-to-all(f32[8,2,128]{2,1,0:T(2,128)S(1)} %get-tuple-element.23), channel_id=1, replica_groups=mesh['ctx'=64,'tp'=8] {'tp'}, dimensions={0} | all-to-all | bytes 16384 | tf_op jit(solution)/shard_map/all_to_all | solution.py:395
  80.7 0.7 shard_map.99
  81.4 16.5 %all_to_all.38.piece_ref = f32[16,64,128]{2,1,0:T(8,128)S(1)} all-to-all(f32[16,64,128]{2,1,0:T(8,128)S(1)} %shard_map.99), channel_id=1, replica_groups={{0,8,16,24,32,40,48,56,64,72,80,88,96,104,112,120},{128,136,144,152,160..., dimensions={0} | all-to-all | bytes 1048576 | tf_op jit(solution)/shard_map/all_to_all | solution.py:359
  97.9 0.1 shard_map.100
  98.0 15.7 %all_to_all.39.total_ref = f32[4,64,128]{2,1,0:T(8,128)S(1)} all-to-all(f32[4,64,128]{2,1,0:T(8,128)S(1)} %shard_map.100), channel_id=1, replica_groups={{0,128,320,448},{8,136,328,456},{16,144,336,464},{24,152,344,472},{32,1..., dimensions={0} | all-to-all | bytes 262144 | tf_op jit(solution)/shard_map/all_to_all | solution.py:359
  113.6 0.9 shard_map.101
  114.5 8.6 %all-to-all-start.6 = ((f32[16,64,128]{2,1,0:T(8,128)}), f32[16,64,128]{2,1,0:T(8,128)S(1)}, u32[]{:S(2)}, u32[]{:S(2)}) async-start(f32[16,64,128]{2,1,0:T(8,128)} %shard_map.101), calls=%async_computation.6 | async-start | bytes 1048576 | tf_op jit(solution)/shard_map/all_to_all | solution.py:359
  123.1 3.4 %shard_map.98 = (bf16[128,1024]{1,0:T(8,128)(2,1)}, bf16[128,1024]{1,0:T(8,128)(2,1)}, f32[8,128,128]{2,1,0:T(8,128)S(1)}, f32[128,1024]{1,0:T(8,128)S(1)}) custom-call(bf16[128,1024]{1,0:T(8,128)(2,1)S(1)} %copy-done, bf16[128,1024]{1,0:T(8,128)(2,1)S(1)} %copy-done.1, ...), custom_call_target="tpu_custom_call", output_to_operand_aliasing={{2}: (5, {}), {3}: (6, {})} | custom-call | flops 436207616 | bytes 3690496 | tf_op jit(solution)/shard_map/pallas_call | solution.py:307
  126.5 9.0 %all-to-all-done.6 = f32[16,64,128]{2,1,0:T(8,128)S(1)} async-done(((f32[16,64,128]{2,1,0:T(8,128)}), f32[16,64,128]{2,1,0:T(8,128)S(1)}, u32[]{:S(2)}, u32[]{:S(2)}) %all-to-all-start.6) | async-done | bytes 524320 | tf_op jit(solution)/shard_map/all_to_all | solution.py:359
  135.5 1.2 shard_map.102
  (5 shorter events, 0.0 us)
Async XLA Ops:
  48.9 6.2 %copy-start = (bf16[128,1024]{1,0:T(8,128)(2,1)S(1)}, bf16[128,1024]{1,0:T(8,128)(2,1)}, u32[]{:S(2)}) copy-start(bf16[128,1024]{1,0:T(8,128)(2,1)} %query_ref.7) | copy-start | bytes 786436
  49.0 6.3 %copy-start.1 = (bf16[128,1024]{1,0:T(8,128)(2,1)S(1)}, bf16[128,1024]{1,0:T(8,128)(2,1)}, u32[]{:S(2)}) copy-start(bf16[128,1024]{1,0:T(8,128)(2,1)} %key_ref.5) | copy-start | bytes 786436
  49.0 6.3 %copy-start.2 = (bf16[128,1024]{1,0:T(8,128)(2,1)S(1)}, bf16[128,1024]{1,0:T(8,128)(2,1)}, u32[]{:S(2)}) copy-start(bf16[128,1024]{1,0:T(8,128)(2,1)} %value_ref.5) | copy-start | bytes 786436
  49.0 16.0 %all-to-all-start.2 = ((f32[16,64,128]{2,1,0:T(8,128)}), f32[16,64,128]{2,1,0:T(8,128)S(1)}, u32[]{:S(2)}, u32[]{:S(2)}) async-start(f32[16,64,128]{2,1,0:T(8,128)} %get-tuple-element.21), calls=%async_computation.2 | async-start | bytes 1048576 | tf_op jit(solution)/shard_map/all_to_all | solution.py:359
  55.2 9.7 %copy-start.3 = (bf16[128,1024]{1,0:T(8,128)(2,1)S(1)}, bf16[128,1024]{1,0:T(8,128)(2,1)}, u32[]{:S(2)}) copy-start(bf16[128,1024]{1,0:T(8,128)(2,1)} %grad_ref.5) | copy-start | bytes 786436
  55.2 9.7 %copy-start.4 = (f32[1024]{0:T(1024)S(1)}, f32[1024]{0:T(1024)}, u32[]{:S(2)}) copy-start(f32[1024]{0:T(1024)} %param.10) | copy-start | bytes 12292
  114.5 21.0 %all-to-all-start.6 = ((f32[16,64,128]{2,1,0:T(8,128)}), f32[16,64,128]{2,1,0:T(8,128)S(1)}, u32[]{:S(2)}, u32[]{:S(2)}) async-start(f32[16,64,128]{2,1,0:T(8,128)} %shard_map.101), calls=%async_computation.6 | async-start | bytes 1048576 | tf_op jit(solution)/shard_map/all_to_all | solution.py:359
